TPU v7x, 32 devices: a whole 2x2x4 slice. The times are simulated.
32 devices in a mesh: seq: 4 (over y, x), dp: 8 (over z, core).
Axes of the slice: x: 2, y: 2, z: 4, core: 2. Of those that a mesh axis runs over, the one named last changes fastest.
Arguments:
- hidden_in: bfloat16 [32, 1024, 768], P('dp', 'seq'), may hold values from -6 to 6
- positions: int32 [32, 1024], P('dp', 'seq'), may hold values from 0 to 3069, as said below
- attn_gain: float32 [768], replicated, may hold values from 0.1 to 1.9
- attn_shift: float32 [768], replicated, may hold values from -1.75 to 1.75
- qkv_weight: bfloat16 [768, 2304], replicated, may hold values from -0.21875 to 0.21875
- qkv_bias: float32 [2304], replicated, may hold values from -1.75 to 1.75
- dense_weight: bfloat16 [768, 768], replicated, may hold values from -1.25 to 1.25
- dense_bias: float32 [768], replicated, may hold values from -1.75 to 1.75
- mlp_gain: float32 [768], replicated, may hold values from 0.1 to 1.9
- mlp_shift: float32 [768], replicated, may hold values from -1.75 to 1.75
- up_weight: bfloat16 [768, 3072], replicated, may hold values from -0.21875 to 0.21875
- up_bias: float32 [3072], replicated, may hold values from -1.75 to 1.75
- down_weight: bfloat16 [3072, 768], replicated, may hold values from -0.109375 to 0.109375
- down_bias: float32 [768], replicated, may hold values from -1.75 to 1.75
- out_grad: bfloat16 [32, 1024, 768], P('dp', 'seq'), may hold values from -6 to 6
Outputs:
- layer_out: bfloat16 [32, 1024, 768], P('dp', 'seq')
- input_grad: bfloat16 [32, 1024, 768], P('dp', 'seq')
- attn_gain_grad: float32 [768], replicated
- attn_shift_grad: float32 [768], replicated
- qkv_weight_grad: float32 [768, 2304], replicated
- qkv_bias_grad: float32 [2304], replicated
- dense_weight_grad: float32 [768, 768], replicated
- dense_bias_grad: float32 [768], replicated
- mlp_gain_grad: float32 [768], replicated
- mlp_shift_grad: float32 [768], replicated
- up_weight_grad: float32 [768, 3072], replicated
- up_bias_grad: float32 [3072], replicated
- down_weight_grad: float32 [3072, 768], replicated
- down_bias_grad: float32 [768], replicated
Inputs may be any that keep to these rules, and one draw needn't show every extreme that they name: Along each sentence, positions start at 0 and rise by 1 to 3 from one token to the next; in one sentence of each draw they rise by 3 throughout.
All inputs are finite; a program needn't handle non-finite values.
Results may differ from a plain program's by a relative error of at most 0.014.
Values may be sent and summed in bfloat16 or wider, within the bound.
A program may use at most 320 MiB of HBM per device.

v0:
```python
import jax
import jax.numpy as jnp
from jax import lax
from jax.sharding import PartitionSpec as P

HEADS = 12
HEAD = 64
ROT = 16


EPSILON = 1e-05
NEGATIVE = -1e30


def normalize(values, gain, shift):
    center = values - jnp.mean(values, axis=-1, keepdims=True)
    spread = jnp.mean(center * center, axis=-1, keepdims=True)
    return center * lax.rsqrt(spread + EPSILON) * gain + shift


def angles_of(positions, half_dims):
    freqs = jnp.power(10000.0, -2.0 * jnp.arange(half_dims, dtype=jnp.float32) / (2 * half_dims))
    return positions.astype(jnp.float32)[..., None] * freqs


def rotate(values, angles):
    half_dims = angles.shape[-1]
    cosine = jnp.cos(angles)[..., None, :]
    sine = jnp.sin(angles)[..., None, :]
    first = values[..., :half_dims]
    second = values[..., half_dims : 2 * half_dims]
    return jnp.concatenate(
        [
            first * cosine - second * sine,
            second * cosine + first * sine,
            values[..., 2 * half_dims :],
        ],
        axis=-1,
    )


def gelu_exact(values):
    return jax.nn.gelu(values, approximate=False)


def token_sum(left, right):
    return jnp.einsum("std,ste->de", left, right, preferred_element_type=jnp.float32)


def on_device(
    hidden_in,
    positions,
    attn_gain,
    attn_shift,
    qkv_weight,
    qkv_bias,
    dense_weight,
    dense_bias,
    mlp_gain,
    mlp_shift,
    up_weight,
    up_bias,
    down_weight,
    down_bias,
    out_grad,
):
    sentences, local_len, width = hidden_in.shape
    full_len = local_len * lax.axis_size("seq")
    scale = HEAD ** (-0.5)
    hidden = hidden_in.astype(jnp.float32)
    own_rank = lax.axis_index("seq")
    first_index = own_rank * local_len
    last_index = first_index + local_len - 1
    query_index = first_index + jnp.arange(local_len)
    angles = angles_of(positions, ROT // 2)
    normed, norm_back = jax.vjp(lambda v, g, b: normalize(v, g, b), hidden, attn_gain, attn_shift)
    normed_low = normed.astype(jnp.bfloat16)
    mixed = jnp.dot(normed_low, qkv_weight, preferred_element_type=jnp.float32) + qkv_bias
    query_rot = rotate(mixed[..., :width].reshape(sentences, local_len, HEADS, HEAD), angles)
    key_rot = rotate(
        mixed[..., width : 2 * width].reshape(sentences, local_len, HEADS, HEAD), angles
    )
    queries = query_rot.astype(jnp.bfloat16)
    key_low = key_rot.reshape(sentences, local_len, width).astype(jnp.bfloat16)
    value_low = mixed[..., 2 * width :].astype(jnp.bfloat16)

    def block_scores(keys):
        key_heads = keys.reshape(sentences, keys.shape[1], HEADS, HEAD)
        scores = (
            jnp.einsum("sqhd,skhd->shqk", queries, key_heads, preferred_element_type=jnp.float32)
            * scale
        )
        key_index = jnp.arange(keys.shape[1])
        allowed = query_index[:, None] >= key_index[None, :]
        return (scores, allowed)

    def attend_core(carry, piece):
        run_max, run_sum, run_acc = carry
        keys, values = piece
        scores, allowed = block_scores(keys)
        masked = jnp.where(allowed, scores, NEGATIVE)
        new_max = jnp.maximum(run_max, jnp.max(masked, axis=-1))
        weights = jnp.where(allowed, jnp.exp(masked - new_max[..., None]), 0.0)
        value_heads = values.reshape(sentences, values.shape[1], HEADS, HEAD)
        run_sum = jnp.sum(weights, axis=-1)
        run_acc = jnp.einsum(
            "shqk,skhd->shqd",
            weights.astype(jnp.bfloat16),
            value_heads,
            preferred_element_type=jnp.float32,
        )
        return (new_max, run_sum, run_acc)

    start_carry = (
        jnp.full((sentences, HEADS, local_len), NEGATIVE, jnp.float32),
        jnp.zeros((sentences, HEADS, local_len), jnp.float32),
        jnp.zeros((sentences, HEADS, local_len, HEAD), jnp.float32),
    )
    piece = (
        lax.all_gather(key_low, "seq", axis=1, tiled=True),
        lax.all_gather(value_low, "seq", axis=1, tiled=True),
    )
    run_max, run_sum, run_acc = lax.cond(
        jnp.int32(0) > last_index, lambda c: c, lambda c: attend_core(c, piece), start_carry
    )
    log_total = run_max + jnp.log(run_sum)
    attended = jnp.transpose(run_acc / run_sum[..., None], (0, 2, 1, 3)).reshape(
        sentences, local_len, width
    )
    attended_low = attended.astype(jnp.bfloat16)
    attn = jnp.dot(attended_low, dense_weight, preferred_element_type=jnp.float32) + dense_bias
    normed_mlp, mlp_norm_back = jax.vjp(
        lambda v, g, b: normalize(v, g, b), hidden, mlp_gain, mlp_shift
    )
    normed_mlp_low = normed_mlp.astype(jnp.bfloat16)
    upper = jnp.dot(normed_mlp_low, up_weight, preferred_element_type=jnp.float32) + up_bias
    active, gelu_back = jax.vjp(gelu_exact, upper)
    active_low = active.astype(jnp.bfloat16)
    layer_out = (
        hidden
        + attn
        + jnp.dot(active_low, down_weight, preferred_element_type=jnp.float32)
        + down_bias
    ).astype(jnp.bfloat16)
    grad_full = out_grad.astype(jnp.float32)
    down_weight_grad = token_sum(active_low, out_grad)
    down_bias_grad = jnp.sum(grad_full, axis=(0, 1))
    dense_weight_grad = token_sum(attended_low, out_grad)
    active_grad = jnp.einsum(
        "std,fd->stf", out_grad, down_weight, preferred_element_type=jnp.float32
    )
    upper_grad = gelu_back(active_grad)[0].astype(jnp.bfloat16)
    up_weight_grad = token_sum(normed_mlp_low, upper_grad)
    up_bias_grad = jnp.sum(upper_grad.astype(jnp.float32), axis=(0, 1))
    normed_mlp_grad = jnp.einsum(
        "stf,df->std", upper_grad, up_weight, preferred_element_type=jnp.float32
    )
    mlp_input_grad, mlp_gain_grad, mlp_shift_grad = mlp_norm_back(normed_mlp_grad)
    attended_grad = jnp.einsum(
        "std,ed->ste", out_grad, dense_weight, preferred_element_type=jnp.float32
    ).astype(jnp.bfloat16)
    attended_grad_heads = attended_grad.reshape(sentences, local_len, HEADS, HEAD)
    delta = jnp.transpose(
        jnp.sum(
            (attended_grad.astype(jnp.float32) * attended).reshape(
                sentences, local_len, HEADS, HEAD
            ),
            axis=-1,
        ),
        (0, 2, 1),
    )

    def score_grads(keys, values):
        piece_len = keys.shape[1]
        scores, allowed = block_scores(keys)
        probs = jnp.where(allowed, jnp.exp(scores - log_total[..., None]), 0.0)
        value_heads = values.reshape(sentences, piece_len, HEADS, HEAD)
        prob_grad = jnp.einsum(
            "sqhd,skhd->shqk", attended_grad_heads, value_heads, preferred_element_type=jnp.float32
        )
        score_grad = (probs * (prob_grad - delta[..., None])).astype(jnp.bfloat16)
        return (probs, score_grad)

    def full_core(piece):
        keys, values = piece
        piece_len = keys.shape[1]
        probs, score_grad = score_grads(keys, values)
        key_heads = keys.reshape(sentences, piece_len, HEADS, HEAD)
        value_grad = jnp.einsum(
            "shqk,sqhd->skhd",
            probs.astype(jnp.bfloat16),
            attended_grad_heads,
            preferred_element_type=jnp.float32,
        )
        query_grad = (
            jnp.einsum("shqk,skhd->sqhd", score_grad, key_heads, preferred_element_type=jnp.float32)
            * scale
        )
        key_grad = (
            jnp.einsum("shqk,sqhd->skhd", score_grad, queries, preferred_element_type=jnp.float32)
            * scale
        )
        update = jnp.stack(
            [
                key_grad.reshape(sentences, piece_len, width),
                value_grad.reshape(sentences, piece_len, width),
            ],
            axis=2,
        )
        return (query_grad, update)

    query_zero = jnp.zeros((sentences, local_len, HEADS, HEAD), jnp.float32)
    back_init = (query_zero, jnp.zeros((sentences, full_len, 2, width), jnp.float32))

    def back_piece(carry, piece, start):
        return lax.cond(start > last_index, lambda c: c, lambda c: full_core(piece), carry)

    back_result = back_piece(
        back_init,
        (
            lax.all_gather(key_low, "seq", axis=1, tiled=True),
            lax.all_gather(value_low, "seq", axis=1, tiled=True),
        ),
        jnp.int32(0),
    )
    query_grad, pair_grad = back_result
    own_pair = lax.psum_scatter(
        pair_grad.astype(jnp.bfloat16), "seq", scatter_dimension=1, tiled=True
    ).astype(jnp.float32)
    key_grad_own = own_pair[:, :, 0].reshape(sentences, local_len, HEADS, HEAD)
    value_grad_own = own_pair[:, :, 1]
    query_back = rotate(query_grad, -angles).reshape(sentences, local_len, width)
    key_back = rotate(key_grad_own, -angles).reshape(sentences, local_len, width)
    mixed_grad = jnp.concatenate([query_back, key_back, value_grad_own], axis=-1).astype(
        jnp.bfloat16
    )
    qkv_weight_grad = token_sum(normed_low, mixed_grad)
    qkv_bias_grad = jnp.sum(mixed_grad.astype(jnp.float32), axis=(0, 1))
    normed_grad = jnp.einsum(
        "ste,de->std", mixed_grad, qkv_weight, preferred_element_type=jnp.float32
    )
    attn_input_grad, attn_gain_grad, attn_shift_grad = norm_back(normed_grad)
    input_grad = (grad_full + attn_input_grad + mlp_input_grad).astype(jnp.bfloat16)
    summed = lax.psum(
        (
            attn_gain_grad,
            attn_shift_grad,
            qkv_weight_grad,
            qkv_bias_grad,
            dense_weight_grad,
            down_bias_grad,
            mlp_gain_grad,
            mlp_shift_grad,
            up_weight_grad,
            up_bias_grad,
            down_weight_grad,
            down_bias_grad,
        ),
        ("seq", "dp"),
    )
    return (
        layer_out,
        input_grad,
        summed[0],
        summed[1],
        summed[2],
        summed[3],
        summed[4],
        summed[5],
        summed[6],
        summed[7],
        summed[8],
        summed[9],
        summed[10],
        summed[11],
    )


def solution(mesh):
    return jax.shard_map(
        on_device,
        mesh=mesh,
        in_specs=(
            P("dp", "seq", None),
            P("dp", "seq"),
            P(),
            P(),
            P(),
            P(),
            P(),
            P(),
            P(),
            P(),
            P(),
            P(),
            P(),
            P(),
            P("dp", "seq", None),
        ),
        out_specs=(
            P("dp", "seq", None),
            P("dp", "seq", None),
            P(),
            P(),
            P(),
            P(),
            P(),
            P(),
            P(),
            P(),
            P(),
            P(),
            P(),
            P(),
        ),
        check_vma=False,
    )
```

profile of v0, /device:TPU:0, one launch (start us, length us, event | category | flops | bytes accessed | tf_op | source)
XLA Modules:
  0.0 1042.1 jit_solution(15824184756684552721)
XLA Ops:
  46.1 63.8 %all-gather.3.cloned.1.call-done = bf16[4,1024,768]{1,2,0:T(8,128)(2,1)} async-done(((bf16[4,256,768]{1,2,0:T(8,128)(2,1)}), bf16[4,1024,768]{1,2,0:T(8,128)(2,1)}) %all-gather.3.cloned.1.call-update) | async-done | bytes 6291472 | tf_op jit(solution)/shard_map/all_gather | solution.py:120
  109.9 72.6 %all-gather.5.cloned.1.call-done = bf16[4,1024,768]{2,1,0:T(8,128)(2,1)} async-done(((bf16[4,256,768]{2,1,0:T(8,128)(2,1)}), bf16[4,1024,768]{2,1,0:T(8,128)(2,1)}) %all-gather.5.cloned.1.call-update) | async-done | bytes 6291472 | tf_op jit(solution)/shard_map/all_gather | solution.py:121
  182.6 75.6 %conditional.2 = (f32[4,12,256]{2,1,0:T(8,128)}, f32[4,12,256]{2,1,0:T(8,128)}, f32[4,12,256,64]{2,3,1,0:T(8,128)S(1)}, f32[4,12,256]{2,1,0:T(8,128)}) conditional(s32[]{:T(128)} %convert_element_type.69, (s32[256]{0:T(256)S(1)}, bf16[4,1024,768]{1,2,0:T(8,128)(2,1)}, bf16[4,256,12,64]{1,3,2,0:T(8,128)(2,1)}, ...), branch_computations={%region_2.5_spmd, %region_5.6_spmd} | conditional | flops 3385053184 | bytes 183764096 | solution.py:123
  182.8 21.2 %fusion = (f32[4,12,256]{2,1,0:T(8,128)S(1)}, f32[4,12,256,1024]{3,2,1,0:T(8,128)}) fusion(pred[256,1024]{1,0:T(8,128)(4,1)S(1)} %iota_compare_fusion, bf16[4,256,12,64]{1,3,2,0:T(8,128)(2,1)} %get-tuple-element.47, bf16[4,1024,12,64]{1,3,2,0:T(8,128)(2,1)} %bitcast.82), kind=kOutput, calls=%fused_computation.2 | convolution fusion | flops 1648349184 | bytes 58507264 | tf_op jit(solution)/shard_map/cond/branch_0_fun/sqhd,skhd->shqk/dot_general | solution.py:90
  204.0 22.9 %fusion.2 = f32[4,12,256]{2,1,0:T(8,128)S(1)} fusion(f32[4,12,256,1024]{3,2,1,0:T(8,128)} %get-tuple-element.139, f32[4,12,256]{2,1,0:T(8,128)S(1)} %broadcast_maximum_fusion, pred[256,1024]{1,0:T(8,128)(4,1)S(1)} %iota_compare_fusion), kind=kLoop, calls=%fused_computation.4 | loop fusion | flops 62902272 | bytes 50692096 | tf_op jit(solution)/shard_map/cond/branch_0_fun/reduce_sum | solution.py:105
  236.8 21.3 %fusion.3 = f32[4,12,256,64]{2,3,1,0:T(8,128)S(1)} fusion(bf16[4,1024,12,64]{1,3,2,0:T(8,128)(2,1)} %bitcast.98, f32[4,12,256,1024]{3,2,1,0:T(8,128)} %get-tuple-element.139, f32[4,12,256]{2,1,0:T(8,128)} %copy-done.18, pred[256,1024]{1,0:T(8,128)(4,1)} %copy-done.7), kind=kOutput, calls=%fused_computation.5 | convolution fusion | flops 1673527296 | bytes 60080128 | tf_op jit(solution)/shard_map/cond/branch_0_fun/shqk,skhd->shqd/dot_general | solution.py:106
  277.4 137.0 %conditional.3 = (bf16[4,1024,2,768]{1,3,0,2:T(8,128)(2,1)}, f32[4,256,12,8]{1,3,2,0:T(8,128)}, f32[4,256,12,8]{1,3,2,0:T(8,128)}, bf16[4,256,12,48]{1,3,2,0:T(8,128)(2,1)}) conditional(s32[]{:T(128)} %convert_element_type.69, (s32[256]{0:T(256)S(1)}, bf16[4,1024,768]{1,2,0:T(8,128)(2,1)}, bf16[4,256,12,64]{1,3,2,0:T(8,128)(2,1)}, ...), branch_computations={%region_7.8_spmd, %region_8.9_spmd} | conditional | flops 8192536576 | bytes 313295904 | solution.py:216
  277.4 22.8 %fusion.76 = f32[4,12,256,1024]{3,2,1,0:T(8,128)} fusion(bf16[4,256,12,64]{1,3,2,0:T(8,128)(2,1)} %get-tuple-element.51, bf16[4,1024,12,64]{1,3,2,0:T(8,128)(2,1)} %bitcast.83), kind=kOutput, calls=%fused_computation.141 | convolution fusion | flops 1610612736 | bytes 58195968 | tf_op jit(solution)/shard_map/cond/branch_0_fun/sqhd,skhd->shqk/dot_general | solution.py:90
  313.8 31.2 %multiply_convert_fusion = bf16[4,12,256,1024]{3,2,1,0:T(8,128)(2,1)} fusion(f32[4,12,256,1024]{3,2,1,0:T(8,128)} %fusion.76, f32[4,12,256]{2,1,0:T(8,128)} %get-tuple-element.57, f32[4,12,256]{2,1,0:T(8,128)} %add.39, pred[256,1024]{1,0:T(8,128)(4,1)} %iota_compare_fusion.1, bf16[4,256,12,64]{1,3,2,0:T(8,128)(2,1)} %bitcast.104, ...), kind=kOutput, calls=%fused_computation.12 | convolution fusion | flops 1686110208 | bytes 83722240 | tf_op jit(solution)/shard_map/cond/branch_0_fun/sqhd,skhd->shqk/dot_general | solution.py:178
  345.0 15.8 %broadcast_multiply_fusion = bf16[4,12,1024,64]{2,3,1,0:T(8,128)(2,1)} fusion(bf16[4,256,12,64]{1,3,2,0:T(8,128)(2,1)} %get-tuple-element.51, bf16[4,12,256,1024]{3,2,1,0:T(8,128)(2,1)} %multiply_convert_fusion), kind=kOutput, calls=%fused_computation.18 | convolution fusion | flops 1616904192 | bytes 33030144 | tf_op jit(solution)/shard_map/cond/branch_0_fun/shqk,sqhd->skhd/dot_general | solution.py:200
  360.8 22.5 %fusion.10 = bf16[4,12,1024,64]{2,3,1,0:T(8,128)(2,1)} fusion(bf16[4,256,12,64]{1,3,2,0:T(8,128)(2,1)} %bitcast.105, f32[4,12,256,1024]{3,2,1,0:T(8,128)} %fusion.76, f32[4,12,256]{2,1,0:T(8,128)} %add.39, pred[256,1024]{1,0:T(8,128)(4,1)} %iota_compare_fusion.1), kind=kOutput, calls=%fused_computation.16 | convolution fusion | flops 1660944384 | bytes 58507264 | tf_op jit(solution)/shard_map/cond/branch_0_fun/shqk,sqhd->skhd/dot_general | solution.py:189
  383.3 10.4 %pad_maximum_fusion = bf16[4,1024,2,768]{1,3,0,2:T(8,128)(2,1)} fusion(bf16[4,1024,1,768]{1,3,0,2:T(8,128)(2,1)} %bitcast.103, bf16[4,1024,1,768]{1,3,0,2:T(8,128)(2,1)} %bitcast.85), kind=kLoop, calls=%fused_computation.15 | loop fusion | flops 6291456 | bytes 25165824 | tf_op jit(solution)/shard_map/cond/branch_0_fun/stack | solution.py:203
  393.8 15.7 %multiply_bitcast_fusion = f32[4,256,12,64]{1,3,2,0:T(8,128)} fusion(bf16[4,12,256,1024]{3,2,1,0:T(8,128)(2,1)} %multiply_convert_fusion, bf16[4,1024,12,64]{1,3,2,0:T(8,128)(2,1)} %bitcast.84), kind=kOutput, calls=%fused_computation.19 | convolution fusion | flops 1611399168 | bytes 34603008 | tf_op jit(solution)/shard_map/cond/branch_0_fun/shqk,skhd->sqhd/dot_general | solution.py:196
  414.4 16.7 %copy.58 = bf16[4,1024,2,768]{3,1,0,2:T(8,128)(2,1)} copy(bf16[4,1024,2,768]{1,3,0,2:T(8,128)(2,1)} %get-tuple-element.87) | data formatting | bytes 25165824 | tf_op jit(solution)/shard_map/cond | solution.py:216
  431.8 11.0 %fusion.56 = (u8[256,3072]{1,0:T(8,128)(4,1)S(1)}, u8[256,3072]{1,0:T(8,128)(4,1)S(1)}, f32[4,256,3072]{2,1,0:T(8,128)S(1)}) fusion(f32[3072]{0:T(1024)} %param.30, bf16[768,3072]{1,0:T(8,128)(2,1)} %param.29, bf16[4,256,768]{2,1,0:T(8,128)(2,1)} %param.19, f32[768]{0:T(1024)S(1)} %copy-done.35, f32[768]{0:T(1024)S(1)} %copy-done.28, ...), kind=kOutput, calls=%fused_computation.96 | convolution fusion | flops 4879024128 | bytes 20473856 | tf_op jit(solution)/shard_map/dot_general | solution.py:136
  442.9 30.5 %multiply_convert_fusion.1 = (bf16[4,256,3072]{2,1,0:T(8,128)(2,1)}, f32[4,256,3072]{2,1,0:T(8,128)}) fusion(f32[4,256,3072]{2,1,0:T(8,128)S(1)} %get-tuple-element.168, f32[3072]{0:T(1024)S(1)} %copy-done.32, u8[256,3072]{1,0:T(8,128)(4,1)S(1)} %get-tuple-element.114, u8[256,3072]{1,0:T(8,128)(4,1)S(1)} %get-tuple-element.113), kind=kLoop, calls=%fused_computation.33 | loop fusion | flops 223346688 | bytes 33042432 | tf_op jit(solution)/shard_map/convert_element_type | solution.py:138
  473.4 17.8 %convert_reduce_fusion = (f32[3072]{0:T(1024)}, bf16[4,256,3072]{2,1,0:T(8,128)(2,1)}) fusion(f32[4,256,3072]{2,1,0:T(8,128)} %get-tuple-element.137, bf16[4,256,768]{2,1,0:T(8,128)(2,1)S(1)} %copy-done.12, bf16[3072,768]{1,0:T(8,128)(2,1)} %param.31, f32[4,256,3072]{2,1,0:T(8,128)} %copy-done.3, f32[3072]{0:T(1024)S(1)} %copy-done.32), kind=kOutput, calls=%fused_computation.31 | convolution fusion | flops 4885312512 | bytes 37773312 | tf_op jit(solution)/shard_map/std,fd->stf/dot_general | solution.py:149
  491.2 11.2 %convolution_bitcast_fusion.1 = f32[768,3072]{1,0:T(8,128)} fusion(bf16[4,256,3072]{2,1,0:T(8,128)(2,1)} %get-tuple-element.173, bf16[4,256,768]{2,1,0:T(8,128)(2,1)S(1)} %copy-done.1, f32[768]{0:T(1024)S(1)} %copy-done.35, f32[768]{0:T(1024)S(1)} %copy-done.28, f32[4,256]{1,0:T(4,128)S(1)} %copy-done.24, f32[4,256]{1,0:T(4,128)S(1)} %copy-done.22), kind=kOutput, calls=%fused_computation.49 | convolution fusion | flops 4836556800 | bytes 17315840 | tf_op jit(solution)/shard_map/std,ste->de/dot_general | solution.py:47
  513.5 38.5 %reduce-scatter.2.cloned.1.call-done = bf16[4,256,2,768]{3,1,0,2:T(8,128)(2,1)} async-done(((bf16[4,1024,2,768]{3,1,0,2:T(8,128)(2,1)}), bf16[4,256,2,768]{3,1,0,2:T(8,128)(2,1)}) %reduce-scatter.2.cloned.1.call-update) | async-done | bytes 3145744 | tf_op jit(solution)/shard_map/reduce_scatter | solution.py:227
  570.3 9.9 convolution_bitcast_fusion.2
  589.0 8.9 fusion.28
  613.7 42.3 %all-reduce = (f32[768]{0:T(1024)}, f32[768]{0:T(1024)}, f32[2304]{0:T(1024)}, f32[768]{0:T(1024)S(1)}, f32[768]{0:T(1024)}, /*index=5*/f32[768]{0:T(1024)}, f32[3072]{0:T(1024)}) all-reduce(f32[768]{0:T(1024)} %get-tuple-element.124, f32[768]{0:T(1024)} %get-tuple-element.121, ...), channel_id=1, replica_groups=mesh['seq'=4,'dp'=8] {'seq','dp'}, use_global_device_ids=true, to_apply=%region_15.16 | all-reduce | flops 9216 | bytes 73728 | tf_op jit(solution)/shard_map/psum | solution.py:244
  656.0 357.7 %all-reduce.4.cloned.1.call-done = (f32[768,2304]{1,0:T(8,128)}, f32[768,768]{1,0:T(8,128)}, f32[768,3072]{1,0:T(8,128)}, f32[3072,768]{1,0:T(8,128)}) async-done(((f32[768,2304]{1,0:T(8,128)}, f32[768,768]{1,0:T(8,128)}, f32[768,3072]{1,0:T(8,128)}, f32[3072,768]{1,0:T(8,128)}), (f32[768,2304]{1,0:T(8,128)}, f32[768,768]{1,0:T(8,128)}, f32[768,3072]{1,0:T(8,128)}, ...) | async-done | bytes 28311568 | tf_op jit(solution)/shard_map/psum | solution.py:244
  1022.3 9.3 copy.93
  (147 shorter events, 153.3 us)
Async XLA Ops:
  7.2 102.7 %all-gather.3.cloned.1.call-start = ((), (), s32[]{:S(2)}) async-start(), calls=%async_computation.1 | async-start | bytes 7864320 | tf_op jit(solution)/shard_map/all_gather | solution.py:120
  17.9 5.6 copy-start.8
  37.1 145.5 %all-gather.5.cloned.1.call-start = ((), (), s32[]{:S(2)}) async-start(), calls=%async_computation.2 | async-start | bytes 7864320 | tf_op jit(solution)/shard_map/all_gather | solution.py:121
  40.3 511.6 %reduce-scatter.2.cloned.1.call-start = ((), (), s32[]{:S(2)}) async-start(), calls=%async_computation.3 | async-start | bytes 15728640 | tf_op jit(solution)/shard_map/reduce_scatter | solution.py:227
  182.8 21.2 %copy-start.7 = (pred[256,1024]{1,0:T(8,128)(4,1)}, pred[256,1024]{1,0:T(8,128)(4,1)S(1)}, u32[]{:S(2)}) copy-start(pred[256,1024]{1,0:T(8,128)(4,1)S(1)} %iota_compare_fusion) | copy-start | bytes 786436 | tf_op jit(solution)/shard_map/cond
  204.0 23.0 %copy-start.18 = (f32[4,12,256]{2,1,0:T(8,128)}, f32[4,12,256]{2,1,0:T(8,128)S(1)}, u32[]{:S(2)}) copy-start(f32[4,12,256]{2,1,0:T(8,128)S(1)} %broadcast_maximum_fusion) | copy-start | bytes 147460 | tf_op jit(solution)/shard_map/cond
  431.1 582.6 %all-reduce.4.cloned.1.call-start = ((), (), s32[]{:S(2)}) async-start(), calls=%async_computation.4 | async-start | bytes 56623104 | tf_op jit(solution)/shard_map/psum | solution.py:244
  431.8 11.0 %copy-start.32 = (f32[3072]{0:T(1024)S(1)}, f32[3072]{0:T(1024)}, u32[]{:S(2)}) copy-start(f32[3072]{0:T(1024)} %param.30) | copy-start | bytes 36868
  442.8 30.6 %copy-start.3 = (f32[4,256,3072]{2,1,0:T(8,128)}, f32[4,256,3072]{2,1,0:T(8,128)S(1)}, u32[]{:S(2)}) copy-start(f32[4,256,3072]{2,1,0:T(8,128)S(1)} %get-tuple-element.168) | copy-start | bytes 37748740
  442.8 30.6 %copy-start.12 = (bf16[4,256,768]{2,1,0:T(8,128)(2,1)S(1)}, bf16[4,256,768]{2,1,0:T(8,128)(2,1)}, u32[]{:S(2)}) copy-start(bf16[4,256,768]{2,1,0:T(8,128)(2,1)} %param.33) | copy-start | bytes 4718596
  473.4 17.8 %copy-start.1 = (bf16[4,256,768]{2,1,0:T(8,128)(2,1)S(1)}, bf16[4,256,768]{2,1,0:T(8,128)(2,1)}, u32[]{:S(2)}) copy-start(bf16[4,256,768]{2,1,0:T(8,128)(2,1)} %param.19) | copy-start | bytes 4718596
  491.2 11.2 %copy-start.9 = (bf16[4,256,3072]{2,1,0:T(8,128)(2,1)S(1)}, bf16[4,256,3072]{2,1,0:T(8,128)(2,1)}, u32[]{:S(2)}) copy-start(bf16[4,256,3072]{2,1,0:T(8,128)(2,1)} %get-tuple-element.136) | copy-start | bytes 18874372
  502.5 8.2 copy-start.4
  565.2 5.2 copy-start.30
  588.9 9.0 copy-start.2
  588.9 9.0 copy-start.5
  588.9 9.0 copy-start.16
  589.0 9.0 copy-start.36
  589.0 9.0 copy-start.37
  656.0 364.9 %copy-start.34 = (f32[768]{0:T(1024)}, f32[768]{0:T(1024)S(1)}, u32[]{:S(2)}) copy-start(f32[768]{0:T(1024)S(1)} %get-tuple-element.227) | copy-start | bytes 9220
  1014.3 6.6 copy-start.15
  1020.9 10.7 %slice-start = ((s8[9437184]{0:T(1024)(128)(4,1)}), s8[4194304]{0:T(1024)(128)(4,1)S(1)}, s32[]{:S(2)}) async-start(s8[9437184]{0:T(1024)(128)(4,1)} %bitcast.92), calls=%async_computation.5 | async-start | bytes 8388608
  1022.3 9.3 slice-start.1
  1022.3 9.3 slice-start.2
  (21 other events, 51.7 us)
Sparse Core Ops, SparseCore 0:
  37.2 72.7 all-gather.2
  112.4 70.1 all-gather.4
  431.2 120.7 reduce-scatter.1
  580.4 433.2 all-reduce.3
where the time goes:
time: 1050 us; the launch traced here: 1040 us
  waiting for transfers between devices  533 us (51%)
  matrix products  249 us (24%)
  local copies, waits for them, and re-layouts  106 us (10%)
  other arithmetic  98.1 us (9%)
  blocking collectives  42.3 us (4%)
  between operations  14.4 us (1%)
    psum x1, waiting for transfers between devices, on_device(): lax.psum((attn_gain_grad, attn_shift_grad, qkv_weight_grad, qkv_bias_grad...  358 us
    all_gather x1, waiting for transfers between devices, on_device(): lax.all_gather(value_low, 'seq', axis=1, tiled=True)  72.6 us
    all_gather x1, waiting for transfers between devices, on_device(): lax.all_gather(key_low, 'seq', axis=1, tiled=True)  63.8 us
    dot_general x2, matrix products, block_scores(): jnp.einsum('sqhd,skhd->shqk', queries, key_heads, preferred_element_type=...  44 us
    psum x1, blocking collectives, on_device(): lax.psum((attn_gain_grad, attn_shift_grad, qkv_weight_grad, qkv_bias_grad...  42.3 us
    reduce_scatter x1, waiting for transfers between devices, on_device(): lax.psum_scatter(pair_grad.astype(jnp.bfloat16), 'seq', scatter_dimension...  38.5 us
    dot_general x4, matrix products, token_sum(): jnp.einsum('std,ste->de', left, right, preferred_element_type=jnp.float32)  32.1 us
    dot_general x1, matrix products, score_grads(): jnp.einsum('sqhd,skhd->shqk', attended_grad_heads, value_heads, preferred...  31.2 us
  transfers between devices with their start and end apart: 4, of which 4 were waited for; matrix products, arithmetic and copies ran while one was open for 12% of the time, Pallas kernels for 0%

commit v1 on v0

v1 whole, which is shorter than its diff:
```python
import functools
import jax, jax.numpy as jnp
from jax import lax
from jax.experimental import pallas as pl
from jax.experimental.pallas import tpu as pltpu

HEADS, HEAD, ROT = 12, 64, 16
EPSILON = 1e-5
BF, F32 = jnp.bfloat16, jnp.float32
BLK = 256

def nn(a, b): return lax.dot_general(a, b, (((1,), (0,)), ((), ())), preferred_element_type=F32)
def nt(a, b): return lax.dot_general(a, b, (((1,), (1,)), ((), ())), preferred_element_type=F32)
def tn(a, b): return lax.dot_general(a, b, (((0,), (0,)), ((), ())), preferred_element_type=F32)

def norm_parts(x):
    mean = jnp.mean(x, axis=-1, keepdims=True)
    c = x - mean
    rstd = lax.rsqrt(jnp.mean(c * c, axis=-1, keepdims=True) + EPSILON)
    return c * rstd, rstd

def attn_kernel(x_ref, g_ref, cos_ref, sin_ref, gain_ref, shift_ref, wqkv_ref, bqkv_ref, wd_ref,
                attn_ref, ga_ref, dwqkv_ref, dwd_ref, small_ref, dbq_ref,
                wT, xaT, qkvT, kn, vn, dOT, obT, dmT):
    T, W = x_ref.shape
    nblk = T // BLK
    gain = gain_ref[...]; shift = shift_ref[...]
    for j in range(9):
        wT[j*256:(j+1)*256, :] = wqkv_ref[:, j*256:(j+1)*256].T

    @pl.loop(0, nblk)
    def _(b):
        rows = pl.ds(pl.multiple_of(b * BLK, BLK), BLK)
        x = x_ref[rows, :].astype(F32)
        xhat, _ = norm_parts(x)
        xa = (xhat * gain + shift).astype(BF)
        xaT[:, rows] = xa.T
        cos = cos_ref[:, rows]; sin = sin_ref[:, rows]
        for j in range(9):
            m = nt(wT[j*256:(j+1)*256, :], xa) + bqkv_ref[j*256:(j+1)*256, :]
            if j < 6:
                parts = []
                for h in range(4):
                    u = m[h*64:(h+1)*64]
                    u0, u1 = u[:8], u[8:16]
                    parts += [u0 * cos - u1 * sin, u1 * cos + u0 * sin, u[16:]]
                m = jnp.concatenate(parts, axis=0)
                if j < 3: m = m * (HEAD ** -0.5)
            mb = m.astype(BF)
            qkvT[j*256:(j+1)*256, rows] = mb
            if 3 <= j < 6: kn[rows, (j-3)*256:(j-2)*256] = mb.T
            if j >= 6: vn[rows, (j-6)*256:(j-5)*256] = mb.T
        g = g_ref[rows, :]
        for j in range(3):
            dOT[j*256:(j+1)*256, rows] = nt(wd_ref[j*256:(j+1)*256, :], g).astype(BF)

    sub = lax.broadcasted_iota(jnp.int32, (BLK, BLK), 0)
    lane = lax.broadcasted_iota(jnp.int32, (BLK, BLK), 1)
    keep = sub <= lane
    rowid = lax.broadcasted_iota(jnp.int32, (128, 1), 0)

    @pl.loop(0, HEADS // 2)
    def _(hp):
        r0 = pl.multiple_of(hp * 128, 128)
        cols = pl.ds(r0, 128)
        for hh in range(2):
            hr = pl.ds(pl.multiple_of(r0 + hh * 64, 64), 64)
            kr = pl.ds(pl.multiple_of(W + r0 + hh * 64, 64), 64)
            vr = pl.ds(pl.multiple_of(2 * W + r0 + hh * 64, 64), 64)
            msk = (rowid // 64 == hh)
            dk = [None] * nblk; dv = [None] * nblk
            for i in range(nblk):
                n = (i + 1) * BLK
                qs = slice(i * BLK, (i + 1) * BLK)
                qT2 = jnp.where(msk, qkvT[pl.ds(r0, 128), qs], 0).astype(BF)
                dO2 = jnp.where(msk, dOT[pl.ds(r0, 128), qs], 0).astype(BF)
                s = nn(kn[0:n, cols], qT2)
                d = jnp.where(keep, s[n-BLK:], -1e30)
                if n > BLK: s = jnp.concatenate([s[:n-BLK], d], axis=0)
                else: s = d
                m = jnp.max(s, axis=0, keepdims=True)
                e = jnp.exp(s - m)
                l = jnp.sum(e, axis=0, keepdims=True)
                inv = 1.0 / l
                p = e.astype(BF)
                oT = nn(qkvT[vr, 0:n], p) * inv
                dO = dOT[hr, qs].astype(F32)
                delta = jnp.sum(dO * oT, axis=0, keepdims=True)
                obT[hr, qs] = oT.astype(BF)
                dp = nn(vn[0:n, cols], dO2)
                ds = (e * ((dp - delta) * inv)).astype(BF)
                dqT = nn(qkvT[kr, 0:n], ds) * (HEAD ** -0.5)
                dkT = nt(qkvT[hr, qs], ds)
                dvT = nt((dO * inv).astype(BF), p)
                cos = cos_ref[:, qs]; sin = sin_ref[:, qs]
                d0, d1 = dqT[:8], dqT[8:16]
                dqT = jnp.concatenate([d0 * cos + d1 * sin, d1 * cos - d0 * sin, dqT[16:]], axis=0)
                dmT[hr, qs] = dqT.astype(BF)
                for b in range(i + 1):
                    sl = slice(b * BLK, (b + 1) * BLK)
                    dk[b] = dkT[:, sl] if dk[b] is None else dk[b] + dkT[:, sl]
                    dv[b] = dvT[:, sl] if dv[b] is None else dv[b] + dvT[:, sl]
            for b in range(nblk):
                sl = slice(b * BLK, (b + 1) * BLK)
                cos = cos_ref[:, sl]; sin = sin_ref[:, sl]
                d0, d1 = dk[b][:8], dk[b][8:16]
                dmT[kr, sl] = jnp.concatenate([d0 * cos + d1 * sin, d1 * cos - d0 * sin, dk[b][16:]], axis=0).astype(BF)
                dmT[vr, sl] = dv[b].astype(BF)

    small_ref[...] = jnp.zeros_like(small_ref)
    @pl.loop(0, nblk)
    def _(b):
        rows = pl.ds(pl.multiple_of(b * BLK, BLK), BLK)
        ob = obT[:, rows].T
        attn_ref[rows, :] = nn(ob, wd_ref[...]).astype(BF)
        dxa = nn(wqkv_ref[...], dmT[:, rows]).T
        xhat, rstd = norm_parts(x_ref[rows, :].astype(F32))
        small_ref[0:1, :] += jnp.sum(dxa * xhat, axis=0, keepdims=True)
        small_ref[1:2, :] += jnp.sum(dxa, axis=0, keepdims=True)
        small_ref[2:3, :] += jnp.sum(g_ref[rows, :].astype(F32), axis=0, keepdims=True)
        dn = dxa * gain
        ga = rstd * (dn - jnp.mean(dn, axis=-1, keepdims=True) - xhat * jnp.mean(dn * xhat, axis=-1, keepdims=True))
        ga_ref[rows, :] = ga.astype(BF)
    dwd_ref[...] = nn(obT[...], g_ref[...]).astype(BF)
    @pl.loop(0, 9)
    def _(j):
        c = pl.ds(pl.multiple_of(j * 256, 256), 256)
        dm = dmT[c, :]
        dwqkv_ref[:, c] = nt(xaT[...], dm).astype(BF)
        dbq_ref[:, c] = nt(jnp.ones((8, T), BF), dm)

def attn_call(x, g, cosT, sinT, gain, shift, wqkv, bqkv, wd):
    T, W = x.shape
    vm = pl.BlockSpec(memory_space=pltpu.VMEM)
    return pl.pallas_call(
        attn_kernel,
        out_shape=(jax.ShapeDtypeStruct((T, W), BF), jax.ShapeDtypeStruct((T, W), BF),
                   jax.ShapeDtypeStruct((W, 3*W), BF), jax.ShapeDtypeStruct((W, W), BF),
                   jax.ShapeDtypeStruct((8, W), F32), jax.ShapeDtypeStruct((8, 3*W), F32)),
        in_specs=[vm]*9, out_specs=(vm,)*6,
        scratch_shapes=[pltpu.VMEM((3*W, W), BF), pltpu.VMEM((W, T), BF), pltpu.VMEM((3*W, T), BF),
                        pltpu.VMEM((T, W), BF), pltpu.VMEM((T, W), BF), pltpu.VMEM((W, T), BF), pltpu.VMEM((W, T), BF),
                        pltpu.VMEM((3*W, T), BF)],
        compiler_params=pltpu.CompilerParams(vmem_limit_bytes=60 << 20),
    )(x, g, cosT, sinT, gain.reshape(1, W), shift.reshape(1, W), wqkv, bqkv.reshape(3*W, 1), wd)
from jax.sharding import PartitionSpec as P

def erf_parts(h):
    z = jnp.abs(h) * (0.5 ** 0.5)
    t = 1.0 / (1.0 + 0.3275911 * z)
    ez = jnp.exp(-0.5 * h * h)
    poly = t * (0.254829592 + t * (-0.284496736 + t * (1.421413741 + t * (-1.453152027 + t * 1.061405429))))
    tail = 0.5 * poly * ez
    return jnp.where(h >= 0, 1.0 - tail, tail), ez * 0.3989422804014327

def mlp_kernel(x_ref, g_ref, gain_ref, shift_ref, wu_ref, bu_ref, wd_ref, bias_ref,
               y_ref, gm_ref, dwu_ref, dwd_ref, small_ref, dbu_ref,
               xm, xmT, yacc, dxm):
    T, W = x_ref.shape
    FF = wu_ref.shape[1]
    C = 256
    nblk = T // BLK
    gain = gain_ref[...]; shift = shift_ref[...]
    @pl.loop(0, nblk)
    def _(b):
        rows = pl.ds(pl.multiple_of(b * BLK, BLK), BLK)
        x = x_ref[rows, :].astype(F32)
        xhat, _ = norm_parts(x)
        v = (xhat * gain + shift).astype(BF)
        xm[rows, :] = v
        xmT[:, rows] = v.T
        yacc[rows, :] = x + bias_ref[...]
    dxm[...] = jnp.zeros_like(dxm)

    @pl.loop(0, FF // C)
    def _(j):
        c = pl.ds(pl.multiple_of(j * C, C), C)
        wu = wu_ref[:, c]
        wd = wd_ref[c, :]
        bu = bu_ref[:, c]
        a_l, dh_l = [], []
        dbu = jnp.zeros((1, C), F32)
        for b in range(nblk):
            rows = slice(b * BLK, (b + 1) * BLK)
            h = nn(xm[rows, :], wu) + bu
            cdf, pdf = erf_parts(h)
            a = (h * cdf).astype(BF)
            da = nt(g_ref[rows, :], wd)
            dh = (da * (cdf + h * pdf)).astype(BF)
            dbu += jnp.sum(dh.astype(F32), axis=0, keepdims=True)
            a_l.append(a); dh_l.append(dh)
        a = jnp.concatenate(a_l, 0); dh = jnp.concatenate(dh_l, 0)
        dbu_ref[:, c] = dbu
        yacc[...] += nn(a, wd)
        dxm[...] += nt(dh, wu)
        dwu_ref[:, c] = nn(xmT[...], dh).astype(BF)
        dwd_ref[c, :] = tn(a, g_ref[...]).astype(BF)

    small_ref[...] = jnp.zeros_like(small_ref)
    @pl.loop(0, nblk)
    def _(b):
        rows = pl.ds(pl.multiple_of(b * BLK, BLK), BLK)
        y_ref[rows, :] = yacc[rows, :]
        xhat, rstd = norm_parts(x_ref[rows, :].astype(F32))
        dxa = dxm[rows, :]
        gf = g_ref[rows, :].astype(F32)
        small_ref[0:1, :] += jnp.sum(dxa * xhat, axis=0, keepdims=True)
        small_ref[1:2, :] += jnp.sum(dxa, axis=0, keepdims=True)
        small_ref[2:3, :] += jnp.sum(gf, axis=0, keepdims=True)
        dn = dxa * gain
        gm = rstd * (dn - jnp.mean(dn, axis=-1, keepdims=True) - xhat * jnp.mean(dn * xhat, axis=-1, keepdims=True))
        gm_ref[rows, :] = gm + gf

def mlp_call(x, g, gain, shift, wu, bu, wd, bias):
    T, W = x.shape
    FF = wu.shape[1]
    vm = pl.BlockSpec(memory_space=pltpu.VMEM)
    S = jax.ShapeDtypeStruct
    return pl.pallas_call(
        mlp_kernel,
        out_shape=(S((T, W), F32), S((T, W), F32), S((W, FF), BF), S((FF, W), BF), S((8, W), F32), S((1, FF), F32)),
        in_specs=[vm]*8, out_specs=(vm,)*6,
        scratch_shapes=[pltpu.VMEM((T, W), BF), pltpu.VMEM((W, T), BF), pltpu.VMEM((T, W), F32), pltpu.VMEM((T, W), F32)],
        compiler_params=pltpu.CompilerParams(vmem_limit_bytes=60 << 20),
    )(x, g, gain.reshape(1, W), shift.reshape(1, W), wu, bu.reshape(1, FF), wd, bias.reshape(1, W))


def on_device(hidden_in, positions, attn_gain, attn_shift, qkv_weight, qkv_bias, dense_weight, dense_bias,
              mlp_gain, mlp_shift, up_weight, up_bias, down_weight, down_bias, out_grad):
    sentences, local_len, width = hidden_in.shape
    seq = lax.axis_size("seq")
    assert sentences == seq
    tokens = sentences * local_len

    def to_sentence(v):
        return lax.all_to_all(v, "seq", 0, 1, tiled=True)[0]

    def to_rows(v):
        return lax.all_to_all(v[None], "seq", 1, 0, tiled=True)

    x_s = to_sentence(hidden_in)
    g_s = to_sentence(out_grad)
    pos = to_sentence(positions)
    freqs = jnp.power(10000.0, -2.0 * jnp.arange(ROT // 2, dtype=F32) / ROT)
    angles = freqs[:, None] * pos.astype(F32)[None, :]
    y, gm, dwu, dwd, small_m, dbu = mlp_call(
        hidden_in.reshape(tokens, width), out_grad.reshape(tokens, width), mlp_gain, mlp_shift,
        up_weight, up_bias, down_weight, dense_bias + down_bias)
    dwu, dwd = lax.psum((dwu, dwd), ("seq", "dp"))
    attn, ga, dwqkv, ddw, small_a, dbq = attn_call(
        x_s, g_s, jnp.cos(angles), jnp.sin(angles), attn_gain, attn_shift, qkv_weight, qkv_bias, dense_weight)
    attn = to_rows(attn)
    ga = to_rows(ga)
    layer_out = (y.reshape(hidden_in.shape) + attn.astype(F32)).astype(BF)
    input_grad = (gm.reshape(hidden_in.shape) + ga.astype(F32)).astype(BF)
    dwqkv, ddw = lax.psum((dwqkv, ddw), ("seq", "dp"))
    s = lax.psum((small_a[0], small_a[1], dbq[0], small_m[0], small_m[1], small_m[2], dbu[0]), ("seq", "dp"))
    return (layer_out, input_grad, s[0], s[1], dwqkv.astype(F32), s[2], ddw.astype(F32), s[5], s[3], s[4],
            dwu.astype(F32), s[6], dwd.astype(F32), s[5])


def solution(mesh):
    act, rep = P("dp", "seq", None), P()
    return jax.shard_map(
        on_device, mesh=mesh,
        in_specs=(act, P("dp", "seq")) + (rep,) * 12 + (act,),
        out_specs=(act, act) + (rep,) * 12,
        check_vma=False)
```

time: 1050 us -> 475 us (0.45)
  waiting for transfers between devices: 533 us -> 142 us
  matrix products: 249 us -> 0 us
  Pallas kernels: 0 us -> 127 us
  local copies, waits for them, and re-layouts: 106 us -> 35.2 us
  other arithmetic: 98.1 us -> 45.1 us
  blocking collectives: 42.3 us -> 91.4 us
  starting transfers between devices: 0.38 us -> 12.3 us
    dot_general x19 -> x0, matrix products: 249 us -> none  [the longest x2 44 us: block_scores(): jnp.einsum('sqhd,skhd->shqk', queries, key_heads, preferred_element_type=...]
    psum x1, waiting for transfers between devices: 358 us -> 137 us  [on_device(): dwqkv, ddw = lax.psum((dwqkv, ddw), ('seq', 'dp'))]
    all_gather x2 -> x0, waiting for transfers between devices: 136 us -> none  [the longest x1 72.6 us: on_device(): lax.all_gather(value_low, 'seq', axis=1, tiled=True)]
    pallas_call x0 -> x2, Pallas kernels: none -> 127 us  [the longest x1 74.1 us: attn_call(): pl.pallas_call(attn_kernel, out_shape=(jax.ShapeDtypeStruct((T, W), BF),...]
    reduce_scatter x1 -> x0, waiting for transfers between devices: 38.5 us -> none  [on_device(): lax.psum_scatter(pair_grad.astype(jnp.bfloat16), 'seq', scatter_dimension...]
    reduce_sum x7 -> x0, other arithmetic: 37.5 us -> none  [the longest x1 22.9 us: attend_core(): run_sum = jnp.sum(weights, axis=-1)]
    all_to_all x0 -> x2, blocking collectives: none -> 32.8 us  [to_sentence(): return lax.all_to_all(v, 'seq', 0, 1, tiled=True)[0]]
    slice x11 -> x2, local copies, waits for them, and re-layouts: 30 us -> 1.81 us  [the longest x1 0.92 us: on_device(): dbq[0]]
  transfers between devices with their start and end apart: 4 -> 4, of which waited for: 4 -> 2; matrix products, arithmetic and copies ran while one was open for 12% -> 12% of each run, Pallas kernels for 0% -> 11%
where the time goes in v1:
time: 475 us; the launch traced here: 468 us
  waiting for transfers between devices  142 us (30%)
  Pallas kernels  127 us (27%)
  blocking collectives  91.4 us (19%)
  other arithmetic  45.1 us (9%)
  local copies, waits for them, and re-layouts  35.2 us (7%)
  between operations  14.4 us (3%)
  starting transfers between devices  12.3 us (3%)
    psum x1, waiting for transfers between devices, on_device(): dwqkv, ddw = lax.psum((dwqkv, ddw), ('seq', 'dp'))  137 us
    pallas_call x1, Pallas kernels, attn_call(): pl.pallas_call(attn_kernel, out_shape=(jax.ShapeDtypeStruct((T, W), BF),...  74.1 us
    psum x1, blocking collectives, on_device(): lax.psum((small_a[0], small_a[1], dbq[0], small_m[0], small_m[1], small_m...  58.7 us
    pallas_call x1, Pallas kernels, mlp_call(): pl.pallas_call(mlp_kernel, out_shape=(S((T, W), F32), S((T, W), F32), S((...  53 us
    all_to_all x2, blocking collectives, to_sentence(): return lax.all_to_all(v, 'seq', 0, 1, tiled=True)[0]  32.8 us
    unnamed x4, other arithmetic  23.2 us
    unnamed x42, local copies, waits for them, and re-layouts  20.7 us
  transfers between devices with their start and end apart: 4, of which 2 were waited for; matrix products, arithmetic and copies ran while one was open for 12% of the time, Pallas kernels for 11%

profile of v1, /device:TPU:0, one launch (start us, length us, event | category | flops | bytes accessed | tf_op | source)
XLA Modules:
  0.0 467.7 jit_solution(8296251882768827604)
XLA Ops:
  7.9 9.6 %all_to_all.24 = s32[4,1,256]{2,1,0:T(1,128)S(1)} all-to-all(s32[4,1,256]{2,1,0:T(1,128)S(1)} %all_to_all.15), channel_id=1, replica_groups=mesh['seq'=4,'dp'=8] {'seq'}, dimensions={0} | all-to-all | bytes 8192 | tf_op jit(solution)/shard_map/all_to_all | solution.py:236
  17.5 23.1 %all_to_all.50 = bf16[4,256,768]{2,1,0:T(8,128)(2,1)} all-to-all(bf16[4,256,768]{2,1,0:T(8,128)(2,1)} %param.15), channel_id=1, replica_groups=mesh['seq'=4,'dp'=8] {'seq'}, dimensions={0} | all-to-all | bytes 3145728 | tf_op jit(solution)/shard_map/all_to_all | solution.py:236
  40.7 3.6 all-to-all-start.1
  48.7 53.0 %shard_map.254 = (f32[1024,768]{1,0:T(8,128)}, f32[1024,768]{1,0:T(8,128)}, bf16[768,3072]{1,0:T(8,128)(2,1)}, bf16[3072,768]{1,0:T(8,128)(2,1)}, f32[8,768]{1,0:T(8,128)}, /*index=5*/f32[1,3072]{1,0:T(1,128)}) custom-call(bf16[1024,768]{1,0:T(8,128)(2,1)} %bitcast.27, bf16[1024,768]{1,0:T(8,128)(2,1)} %bitcast.28, f32[1,768]{1,0:T(1,128)} %reshape.99.gain_ref, ...), custom_call_target="tpu_custom_call" | custom-call | tf_op jit(solution)/shard_map/pallas_call | solution.py:219
  103.7 74.1 %shard_map.255 = (bf16[1024,768]{1,0:T(8,128)(2,1)}, bf16[1024,768]{1,0:T(8,128)(2,1)}, bf16[768,2304]{1,0:T(8,128)(2,1)}, bf16[768,768]{1,0:T(8,128)(2,1)}, f32[8,768]{1,0:T(8,128)}, /*index=5*/f32[8,2304]{1,0:T(8,128)}) custom-call(bf16[1024,768]{1,0:T(8,128)(2,1)} %bitcast.29, bf16[1024,768]{1,0:T(8,128)(2,1)} %bitcast.30, ...), custom_call_target="tpu_custom_call" | custom-call | tf_op jit(solution)/shard_map/pallas_call | solution.py:135
  177.8 3.8 copy.37
  182.2 11.6 %reduce.12 = bf16[1024,768]{1,0:T(8,128)(2,1)} reduce(bf16[1024,1,768]{2,1,0:T(2,128)(2,1)S(1)} %bitcast.21, bf16[]{:T(256)} %broadcast.24), dimensions={1}, to_apply=%bitcast.19.reduce_sub_computation | reduce | bytes 3145730
  193.7 3.7 reshape.119
  197.5 4.3 all-to-all-start.4
  201.8 3.9 copy.38
  205.7 11.6 %reduce.13 = bf16[1024,768]{1,0:T(8,128)(2,1)} reduce(bf16[1024,1,768]{2,1,0:T(2,128)(2,1)S(1)} %bitcast.22, bf16[]{:T(256)} %broadcast.24), dimensions={1}, to_apply=%bitcast.20.reduce_sub_computation | reduce | bytes 3145730
  217.3 3.7 reshape.117
  221.0 5.3 %all-to-all-done.4 = bf16[4,2,98304]{2,1,0:T(2,128)(2,1)} async-done(((bf16[4,2,98304]{2,1,0:T(2,128)(2,1)}), bf16[4,2,98304]{2,1,0:T(2,128)(2,1)}, u32[]{:S(2)}, u32[]{:S(2)}) %all-to-all-start.4) | async-done | bytes 1572896 | tf_op jit(solution)/shard_map/all_to_all | solution.py:239
  226.3 4.4 all-to-all-start.3
  232.5 58.7 %all-reduce = (f32[768]{0:T(1024)}, f32[768]{0:T(1024)}, f32[2304]{0:T(1024)}, f32[768]{0:T(1024)S(1)}, f32[768]{0:T(1024)}, /*index=5*/f32[768]{0:T(1024)}, f32[3072]{0:T(1024)}) all-reduce(f32[768]{0:T(1024)S(1)} %get-tuple-element.56, f32[768]{0:T(1024)S(1)} %get-tuple-element.57, ...), channel_id=1, replica_groups=mesh['seq'=4,'dp'=8] {'seq','dp'}, use_global_device_ids=true, to_apply=%region_0.0 | all-reduce | flops 9216 | bytes 73728 | tf_op jit(solution)/shard_map/psum | solution.py:257
  291.2 3.1 reshape.120
  294.2 1.9 copy.34
  296.1 3.1 reshape.118
  299.4 1.7 copy-done
  302.1 4.4 add_convert_fusion
  306.5 136.7 %all-reduce.4.cloned.1.call-done = (bf16[768,2304]{1,0:T(8,128)(2,1)}, bf16[768,768]{1,0:T(8,128)(2,1)}, bf16[768,3072]{1,0:T(8,128)(2,1)}, bf16[3072,768]{1,0:T(8,128)(2,1)}) async-done(((bf16[768,2304]{1,0:T(8,128)(2,1)}, bf16[768,768]{1,0:T(8,128)(2,1)}, bf16[768,3072]{1,0:T(8,128)(2,1)}, bf16[3072,768]{1,0:T(8,128)(2,1)}), (bf16[768,2304]{1,0:T(8,128)(2,1)}, bf16[768,768]{1,0:T(8,128)(2,1)}, ...) | async-done | bytes 14155792 | tf_op jit(solution)/shard_map/psum | solution.py:256
  443.3 5.6 %convert_element_type.48 = f32[768,2304]{1,0:T(8,128)} convert(bf16[768,2304]{1,0:T(8,128)(2,1)} %get-tuple-element.50) | non-fusion elementwise | flops 1769472 | bytes 10616832 | tf_op jit(solution)/shard_map/convert_element_type | solution.py:258
  450.5 5.0 %convert_element_type.50 = f32[768,3072]{1,0:T(8,128)} convert(bf16[768,3072]{1,0:T(8,128)(2,1)S(1)} %bitcast.34) | non-fusion elementwise | flops 2359296 | bytes 14155776 | tf_op jit(solution)/shard_map/convert_element_type | solution.py:259
  455.6 4.5 convert_element_type.51
  (56 shorter events, 12.8 us)
Async XLA Ops:
  17.5 26.8 %copy-start.8 = (f32[768]{0:T(1024)S(1)}, f32[768]{0:T(1024)}, u32[]{:S(2)}) copy-start(f32[768]{0:T(1024)} %param.23) | copy-start | bytes 9220
  17.5 27.4 %copy-start.9 = (f32[768]{0:T(1024)S(1)}, f32[768]{0:T(1024)}, u32[]{:S(2)}) copy-start(f32[768]{0:T(1024)} %param.24) | copy-start | bytes 9220
  17.5 28.0 %copy-start.6 = (f32[768]{0:T(1024)S(1)}, f32[768]{0:T(1024)}, u32[]{:S(2)}) copy-start(f32[768]{0:T(1024)} %param.22) | copy-start | bytes 9220
  17.5 28.0 %copy-start.7 = (f32[768]{0:T(1024)S(1)}, f32[768]{0:T(1024)}, u32[]{:S(2)}) copy-start(f32[768]{0:T(1024)} %param.28) | copy-start | bytes 9220
  17.5 28.6 %copy-start.10 = (f32[768]{0:T(1024)S(1)}, f32[768]{0:T(1024)}, u32[]{:S(2)}) copy-start(f32[768]{0:T(1024)} %param.17) | copy-start | bytes 9220
  17.5 29.1 %copy-start.11 = (f32[768]{0:T(1024)S(1)}, f32[768]{0:T(1024)}, u32[]{:S(2)}) copy-start(f32[768]{0:T(1024)} %param.18) | copy-start | bytes 9220
  17.5 29.7 %copy-start.4 = (f32[2304]{0:T(1024)S(1)}, f32[2304]{0:T(1024)}, u32[]{:S(2)}) copy-start(f32[2304]{0:T(1024)} %param.20) | copy-start | bytes 27652
  40.7 61.8 %all-to-all-start.1 = ((bf16[4,256,768]{2,1,0:T(8,128)(2,1)}), bf16[4,256,768]{2,1,0:T(8,128)(2,1)S(1)}, u32[]{:S(2)}, u32[]{:S(2)}) async-start(bf16[4,256,768]{2,1,0:T(8,128)(2,1)} %param.29), calls=%async_computation.1 | async-start | bytes 3145728 | tf_op jit(solution)/shard_map/all_to_all | solution.py:236
  44.3 399.0 %all-reduce.4.cloned.1.call-start = ((), (), s32[]{:S(2)}) async-start(), calls=%async_computation.5 | async-start | bytes 28311552 | tf_op jit(solution)/shard_map/psum | solution.py:256
  102.5 1.1 copy-start.1
  197.5 28.8 %all-to-all-start.4 = ((bf16[4,2,98304]{2,1,0:T(2,128)(2,1)}), bf16[4,2,98304]{2,1,0:T(2,128)(2,1)}, u32[]{:S(2)}, u32[]{:S(2)}) async-start(bf16[4,2,98304]{2,1,0:T(2,128)(2,1)} %reshape.119), calls=%async_computation.4 | async-start | bytes 3145728 | tf_op jit(solution)/shard_map/all_to_all | solution.py:239
  217.3 15.2 %copy-start.5 = (f32[1,3072]{1,0:T(1,128)S(1)}, f32[1,3072]{1,0:T(1,128)}, u32[]{:S(2)}) copy-start(f32[1,3072]{1,0:T(1,128)} %get-tuple-element.36) | copy-start | bytes 36868
  226.3 69.8 %all-to-all-start.3 = ((bf16[4,2,98304]{2,1,0:T(2,128)(2,1)}), bf16[4,2,98304]{2,1,0:T(2,128)(2,1)}, u32[]{:S(2)}, u32[]{:S(2)}) async-start(bf16[4,2,98304]{2,1,0:T(2,128)(2,1)} %reshape.117), calls=%async_computation.3 | async-start | bytes 3145728 | tf_op jit(solution)/shard_map/all_to_all | solution.py:239
  291.2 168.9 %copy-start.12 = (f32[768]{0:T(1024)}, f32[768]{0:T(1024)S(1)}, u32[]{:S(2)}) copy-start(f32[768]{0:T(1024)S(1)} %get-tuple-element.87) | copy-start | bytes 9220
  299.2 1.9 copy-start
  299.2 2.9 copy-start.2
  443.3 7.2 %slice-start.2 = ((s8[4718592]{0:T(1024)(128)(4,1)}), s8[4194304]{0:T(1024)(128)(4,1)S(1)}, s32[]{:S(2)}) async-start(s8[4718592]{0:T(1024)(128)(4,1)} %bitcast.33), calls=%async_computation.8 | async-start | bytes 8388608
  443.3 5.6 %copy-start.3 = (bf16[768,768]{1,0:T(8,128)(2,1)S(1)}, bf16[768,768]{1,0:T(8,128)(2,1)}, u32[]{:S(2)}) copy-start(bf16[768,768]{1,0:T(8,128)(2,1)} %get-tuple-element.51) | copy-start | bytes 3538948
  443.3 7.2 %slice-start.3 = ((s8[4718592]{0:T(1024)(128)(4,1)}), s8[524288]{0:T(1024)(128)(4,1)S(1)}, s32[]{:S(2)}) async-start(s8[4718592]{0:T(1024)(128)(4,1)} %bitcast.33), calls=%async_computation.9 | async-start | bytes 1048576
  448.9 6.6 %slice-start = ((s8[4718592]{0:T(1024)(128)(4,1)}), s8[4194304]{0:T(1024)(128)(4,1)S(1)}, s32[]{:S(2)}) async-start(s8[4718592]{0:T(1024)(128)(4,1)} %bitcast.31), calls=%async_computation.6 | async-start | bytes 8388608
  450.5 5.1 %slice-start.1 = ((s8[4718592]{0:T(1024)(128)(4,1)}), s8[524288]{0:T(1024)(128)(4,1)S(1)}, s32[]{:S(2)}) async-start(s8[4718592]{0:T(1024)(128)(4,1)} %bitcast.31), calls=%async_computation.7 | async-start | bytes 1048576
Sparse Core Ops, SparseCore 0:
  177.9 265.2 all-reduce.3

commit v2 on v1

v2 whole, which is shorter than its diff:
```python
import functools
import jax, jax.numpy as jnp
from jax import lax
from jax.experimental import pallas as pl
from jax.experimental.pallas import tpu as pltpu
from jax.sharding import PartitionSpec as P

HEADS, HEAD, ROT = 12, 64, 16
EPSILON = 1e-5
BF, F32 = jnp.bfloat16, jnp.float32
BLK = 256

def nn(a, b): return lax.dot_general(a, b, (((1,), (0,)), ((), ())), preferred_element_type=F32)
def nt(a, b): return lax.dot_general(a, b, (((1,), (1,)), ((), ())), preferred_element_type=F32)
def tn(a, b): return lax.dot_general(a, b, (((0,), (0,)), ((), ())), preferred_element_type=F32)

def norm_parts(x):
    mean = jnp.mean(x, axis=-1, keepdims=True)
    c = x - mean
    rstd = lax.rsqrt(jnp.mean(c * c, axis=-1, keepdims=True) + EPSILON)
    return c * rstd, rstd

def attn_kernel(x_ref, g_ref, cs_ref, gain_ref, shift_ref, wqkv_ref, bqkv_ref, wd_ref,
                attn_ref, ga_ref, da_ref, small_ref, dbq_ref,
                wT, xaT, qkvT, kn, vn, dOT, obT, dmT):
    T, W = x_ref.shape
    nblk = T // BLK
    gain = gain_ref[...]; shift = shift_ref[...]
    for j in range(9):
        wT[j*256:(j+1)*256, :] = wqkv_ref[:, j*256:(j+1)*256].T

    @pl.loop(0, nblk)
    def _(b):
        rows = pl.ds(pl.multiple_of(b * BLK, BLK), BLK)
        x = x_ref[rows, :].astype(F32)
        xhat, _ = norm_parts(x)
        xa = (xhat * gain + shift).astype(BF)
        xaT[:, rows] = xa.T
        cos = cs_ref[b, :8, :]; sin = cs_ref[b, 8:, :]
        for j in range(9):
            m = nt(wT[j*256:(j+1)*256, :], xa) + bqkv_ref[j*256:(j+1)*256, :]
            if j < 6:
                parts = []
                for h in range(4):
                    u = m[h*64:(h+1)*64]
                    u0, u1 = u[:8], u[8:16]
                    parts += [u0 * cos - u1 * sin, u1 * cos + u0 * sin, u[16:]]
                m = jnp.concatenate(parts, axis=0)
                if j < 3: m = m * (HEAD ** -0.5)
            mb = m.astype(BF)
            qkvT[j*256:(j+1)*256, rows] = mb
            if 3 <= j < 6: kn[rows, (j-3)*256:(j-2)*256] = mb.T
            if j >= 6: vn[rows, (j-6)*256:(j-5)*256] = mb.T
        g = g_ref[rows, :]
        for j in range(3):
            dOT[j*256:(j+1)*256, rows] = nt(wd_ref[j*256:(j+1)*256, :], g).astype(BF)

    sub = lax.broadcasted_iota(jnp.int32, (BLK, BLK), 0)
    lane = lax.broadcasted_iota(jnp.int32, (BLK, BLK), 1)
    keep = sub <= lane
    rowid = lax.broadcasted_iota(jnp.int32, (128, 1), 0)

    @pl.loop(0, HEADS // 2)
    def _(hp):
        r0 = pl.multiple_of(hp * 128, 128)
        cols = pl.ds(r0, 128)
        for hh in range(2):
            hr = pl.ds(pl.multiple_of(r0 + hh * 64, 64), 64)
            kr = pl.ds(pl.multiple_of(W + r0 + hh * 64, 64), 64)
            vr = pl.ds(pl.multiple_of(2 * W + r0 + hh * 64, 64), 64)
            msk = (rowid // 64 == hh)
            dk = [None] * nblk; dv = [None] * nblk
            for i in range(nblk):
                n = (i + 1) * BLK
                qs = slice(i * BLK, (i + 1) * BLK)
                qT2 = jnp.where(msk, qkvT[pl.ds(r0, 128), qs], 0).astype(BF)
                dO2 = jnp.where(msk, dOT[pl.ds(r0, 128), qs], 0).astype(BF)
                s = nn(kn[0:n, cols], qT2)
                d = jnp.where(keep, s[n-BLK:], -1e30)
                if n > BLK: s = jnp.concatenate([s[:n-BLK], d], axis=0)
                else: s = d
                m = jnp.max(s, axis=0, keepdims=True)
                e = jnp.exp(s - m)
                l = jnp.sum(e, axis=0, keepdims=True)
                inv = 1.0 / l
                p = e.astype(BF)
                oT = nn(qkvT[vr, 0:n], p) * inv
                dO = dOT[hr, qs].astype(F32)
                delta = jnp.sum(dO * oT, axis=0, keepdims=True)
                obT[hr, qs] = oT.astype(BF)
                dp = nn(vn[0:n, cols], dO2)
                ds = (e * ((dp - delta) * inv)).astype(BF)
                dqT = nn(qkvT[kr, 0:n], ds) * (HEAD ** -0.5)
                dkT = nt(qkvT[hr, qs], ds)
                dvT = nt((dO * inv).astype(BF), p)
                cos = cs_ref[i, :8, :]; sin = cs_ref[i, 8:, :]
                d0, d1 = dqT[:8], dqT[8:16]
                dqT = jnp.concatenate([d0 * cos + d1 * sin, d1 * cos - d0 * sin, dqT[16:]], axis=0)
                dmT[hr, qs] = dqT.astype(BF)
                for b in range(i + 1):
                    sl = slice(b * BLK, (b + 1) * BLK)
                    dk[b] = dkT[:, sl] if dk[b] is None else dk[b] + dkT[:, sl]
                    dv[b] = dvT[:, sl] if dv[b] is None else dv[b] + dvT[:, sl]
            for b in range(nblk):
                sl = slice(b * BLK, (b + 1) * BLK)
                cos = cs_ref[b, :8, :]; sin = cs_ref[b, 8:, :]
                d0, d1 = dk[b][:8], dk[b][8:16]
                dmT[kr, sl] = jnp.concatenate([d0 * cos + d1 * sin, d1 * cos - d0 * sin, dk[b][16:]], axis=0).astype(BF)
                dmT[vr, sl] = dv[b].astype(BF)

        dm = jnp.concatenate([dmT[pl.ds(r0, 128), :], dmT[pl.ds(W + r0, 128), :], dmT[pl.ds(2 * W + r0, 128), :]], axis=0)
        da_ref[hp, :384, :] = nt(dm, xaT[...]).astype(BF)
        da_ref[hp, 384:, :] = nn(obT[pl.ds(r0, 128), :], g_ref[...]).astype(BF)

    small_ref[...] = jnp.zeros_like(small_ref)
    @pl.loop(0, nblk)
    def _(b):
        rows = pl.ds(pl.multiple_of(b * BLK, BLK), BLK)
        ob = obT[:, rows].T
        attn_ref[rows, :] = nn(ob, wd_ref[...]).astype(BF)
        dxa = nn(wqkv_ref[...], dmT[:, rows]).T
        xhat, rstd = norm_parts(x_ref[rows, :].astype(F32))
        small_ref[0:1, :] += jnp.sum(dxa * xhat, axis=0, keepdims=True)
        small_ref[1:2, :] += jnp.sum(dxa, axis=0, keepdims=True)
        small_ref[2:3, :] += jnp.sum(g_ref[rows, :].astype(F32), axis=0, keepdims=True)
        dn = dxa * gain
        ga = rstd * (dn - jnp.mean(dn, axis=-1, keepdims=True) - xhat * jnp.mean(dn * xhat, axis=-1, keepdims=True))
        ga_ref[rows, :] = ga.astype(BF)
    @pl.loop(0, 9)
    def _(j):
        c = pl.ds(pl.multiple_of(j * 256, 256), 256)
        dbq_ref[:, c] = nt(jnp.ones((8, T), BF), dmT[c, :])


def attn_call(x, g, cs, gain, shift, wqkv, bqkv, wd):
    T, W = x.shape
    assert T // cs.shape[0] == BLK
    vm = pl.BlockSpec(memory_space=pltpu.VMEM)
    S = jax.ShapeDtypeStruct
    return pl.pallas_call(
        attn_kernel,
        out_shape=(S((T, W), BF), S((T, W), BF), S((HEADS // 2, 512, W), BF), S((8, W), F32), S((8, 3 * W), F32)),
        in_specs=[vm] * 8, out_specs=(vm,) * 5,
        scratch_shapes=[pltpu.VMEM((3 * W, W), BF), pltpu.VMEM((W, T), BF), pltpu.VMEM((3 * W, T), BF),
                        pltpu.VMEM((T, W), BF), pltpu.VMEM((T, W), BF), pltpu.VMEM((W, T), BF),
                        pltpu.VMEM((W, T), BF), pltpu.VMEM((3 * W, T), BF)],
        compiler_params=pltpu.CompilerParams(vmem_limit_bytes=60 << 20),
    )(x, g, cs, gain.reshape(1, W), shift.reshape(1, W), wqkv, bqkv.reshape(3 * W, 1), wd)


MESH = pl.DeviceIdType.MESH


class Place:
    def __init__(self, sizes):
        self.seq_n, self.dp_n = sizes
        self.seq = lax.axis_index("seq")
        self.dp = lax.axis_index("dp")
        self.core = [("dp", 1)]
        self.seq_bits = [("seq", 1 << b) for b in range(self.seq_n.bit_length() - 1)]
        self.dp_bits = [("dp", 1 << b) for b in range(1, self.dp_n.bit_length() - 1)]

    def mine(self, bit):
        at = self.seq if bit[0] == "seq" else self.dp
        return lax.rem(at // bit[1], 2)

    def partner(self, bit):
        step = bit[1] * (1 - 2 * self.mine(bit))
        if bit[0] == "seq":
            return (self.seq + step, self.dp)
        return (self.seq, self.dp + step)

    def peer(self, k):
        at = self.seq
        for b in range(self.seq_n.bit_length() - 1):
            if k >> b & 1:
                at = at + (1 << b) * (1 - 2 * self.mine(("seq", 1 << b)))
        return at

    def enter(self):
        targets = [(self.peer(k), self.dp) for k in range(1, self.seq_n)]
        targets += [self.partner(bit) for bit in self.core + self.dp_bits]
        bar = pltpu.get_barrier_semaphore()
        for t in targets:
            pl.semaphore_signal(bar, inc=1, device_id=t, device_id_type=MESH)
        pl.semaphore_wait(bar, len(targets))


class Halving:
    def __init__(self, place, rows, bits, unit=16):
        self.place, self.rows, self.bits = place, rows, bits
        self.plan = []
        lo, n, off = 0, rows, 0
        for bit in bits:
            halve = n % (2 * unit) == 0
            part = n // 2 if halve else n
            keep = lo + place.mine(bit) * part if halve else lo
            give = lo + (1 - place.mine(bit)) * part if halve else lo
            self.plan.append((bit, halve, part, keep, give, off))
            lo, n, off = keep, part, off + part
        self.lo, self.n, self.land_rows = lo, n, off

    @staticmethod
    def land(rows, count, unit=16):
        n, off = rows, 0
        for _ in range(count):
            n = n // 2 if n % (2 * unit) == 0 else n
            off += n
        return off

    def copy(self, i, buf, land, send, recv):
        bit, _, part, _, give, off = self.plan[i]
        return pltpu.make_async_remote_copy(
            buf.at[pl.ds(pl.multiple_of(give, 16), part)], land.at[pl.ds(off, part)], send, recv,
            device_id=self.place.partner(bit), device_id_type=MESH)

    def add(self, i, buf, land):
        _, _, part, keep, _, off = self.plan[i]
        rows = pl.ds(pl.multiple_of(keep, 16), part)
        buf[rows] = (buf[rows].astype(F32) + land[pl.ds(off, part)].astype(F32)).astype(buf.dtype)

    def spread(self, i, buf, send, recv):
        bit, halve, part, keep, _, _ = self.plan[i]
        if not halve:
            return None
        at = (slice(None),) * (len(buf.shape) - 2) + (pl.ds(pl.multiple_of(keep, 16), part),)
        return pltpu.make_async_remote_copy(
            buf.at[at], buf.at[at], send, recv, device_id=self.place.partner(bit), device_id_type=MESH)


def cdf_pdf(h):
    t = 1.0 / (1.0 + (0.3275911 * 0.5 ** 0.5) * jnp.abs(h))
    ez = jnp.exp(-0.5 * h * h)
    poly = t * (0.5 * 0.254829592 + t * (0.5 * -0.284496736 + t * (
        0.5 * 1.421413741 + t * (0.5 * -1.453152027 + t * (0.5 * 1.061405429)))))
    tail = poly * ez
    return jnp.where(h >= 0, 1.0 - tail, tail), ez * 0.3989422804014327


def mlp_kernel(sizes, x_ref, g_ref, cs_ref, gain_ref, shift_ref, wu_ref, bu_ref, wd_ref, bias_ref,
               y_ref, gm_ref, xs_ref, gs_ref, css_ref, du_ref, dd_ref, small_ref, dbu_ref,
               xm, xmT, dxm, land_u, land_d, a_s, dh_s, su, ru, sd, rd, sa, ra, sl):
    place = Place(sizes)
    ns = place.seq_n
    L, W = x_ref.shape[1:]
    T = ns * L
    n_chunk, _, C = du_ref.shape
    hu = Halving(place, W, place.core + place.dp_bits + place.seq_bits)
    hd = Halving(place, C, place.core + place.seq_bits + place.dp_bits)
    steps = len(hu.bits)
    place.enter()

    moves = []
    me = pl.ds(pl.multiple_of(place.seq * L, L), L)
    for a, (src, dst) in enumerate(((x_ref, xs_ref), (g_ref, gs_ref), (cs_ref, css_ref))):
        for k in range(ns - 1, 0, -1):
            to = place.peer(k)
            moves.append(pltpu.make_async_remote_copy(
                src.at[to], dst.at[place.seq] if a == 2 else dst.at[me], sa.at[a, k], ra.at[a, k],
                device_id=(to, place.dp), device_id_type=MESH))
        moves.append(pltpu.make_async_copy(
            src.at[place.seq], dst.at[place.seq] if a == 2 else dst.at[me], sl.at[a]))
    for m in moves:
        m.start()

    gain = gain_ref[...]
    shift = shift_ref[...]
    for b in range(ns):
        rows = slice(b * L, (b + 1) * L)
        x = x_ref[b].astype(F32)
        xhat, _ = norm_parts(x)
        v = (xhat * gain + shift).astype(BF)
        xm[rows, :] = v
        xmT[:, rows] = v.T
        y_ref[rows, :] = x + bias_ref[...]
    dxm[...] = jnp.zeros_like(dxm)
    small_ref[...] = jnp.zeros_like(small_ref)

    def finish(p, s):
        for h, buf, land, send, recv in ((hu, du_ref, land_u, su, ru), (hd, dd_ref, land_d, sd, rd)):
            h.copy(s, buf.at[p], land.at[p], send.at[p, s], recv.at[p, s]).wait()
            h.add(s, buf.at[p], land.at[p])

    def begin(p, s):
        for h, buf, land, send, recv in ((hu, du_ref, land_u, su, ru), (hd, dd_ref, land_d, sd, rd)):
            h.copy(s, buf.at[p], land.at[p], send.at[p, s], recv.at[p, s]).start()

    @pl.loop(0, n_chunk + steps)
    def _(j):
        c = pl.ds(pl.multiple_of(jnp.minimum(j, n_chunk - 1) * C, C), C)

        @pl.when(j < n_chunk)
        def _():
            wu = wu_ref[:, c]
            wd = wd_ref[c, :]
            bu = bu_ref[:, c]
            dbu = jnp.zeros((1, C), F32)
            for b in range(ns):
                rows = slice(b * L, (b + 1) * L)
                h = nn(xm[rows, :], wu) + bu
                cdf, pdf = cdf_pdf(h)
                a_s[rows, :] = (h * cdf).astype(BF)
                dh = (nt(g_ref[b], wd) * (cdf + h * pdf)).astype(BF)
                dh_s[rows, :] = dh
                dbu += jnp.sum(dh.astype(F32), axis=0, keepdims=True)
            dbu_ref[:, c] = dbu

        for s in range(1, steps + 1):
            p = j - s

            @pl.when((p >= 0) & (p < n_chunk))
            def _():
                finish(p, s - 1)
                if s < steps:
                    begin(p, s)

        @pl.when(j < n_chunk)
        def _():
            wu = wu_ref[:, c]
            wd = wd_ref[c, :]
            dh = dh_s[...]
            a = a_s[...]
            du_ref[j] = nn(xmT[...], dh).astype(BF)
            dd_ref[j] = tn(a, g_ref[...].reshape(T, W)).astype(BF)
            begin(j, 0)
            y_ref[...] += nn(a, wd)
            dxm[...] += nt(dh, wu)

        @pl.when((j >= n_chunk) & (j < n_chunk + ns))
        def _():
            b = j - n_chunk
            rows = pl.ds(pl.multiple_of(b * L, L), L)
            xhat, rstd = norm_parts(x_ref[b].astype(F32))
            dxa = dxm[rows, :]
            gf = g_ref[b].astype(F32)
            small_ref[0:1, :] += jnp.sum(dxa * xhat, axis=0, keepdims=True)
            small_ref[1:2, :] += jnp.sum(dxa, axis=0, keepdims=True)
            small_ref[2:3, :] += jnp.sum(gf, axis=0, keepdims=True)
            dn = dxa * gain
            gm_ref[rows, :] = gf + rstd * (dn - jnp.mean(dn, axis=-1, keepdims=True)
                                           - xhat * jnp.mean(dn * xhat, axis=-1, keepdims=True))

    for m in moves:
        m.wait()


def mlp_call(sizes, x, g, cs, gain, shift, wu, bu, wd, bias):
    ns, L, W = x.shape
    T = ns * L
    FF = wu.shape[1]
    C = 256
    n = FF // C
    steps = sum(s.bit_length() - 1 for s in sizes)
    vm = pl.BlockSpec(memory_space=pltpu.VMEM)
    hbm = pl.BlockSpec(memory_space=pl.ANY)
    S = jax.ShapeDtypeStruct
    dma = pltpu.SemaphoreType.DMA
    return pl.pallas_call(
        functools.partial(mlp_kernel, sizes),
        out_shape=(S((T, W), F32), S((T, W), F32), S((T, W), BF), S((T, W), BF), S(cs.shape, F32),
                   S((n, W, C), BF), S((n, C, W), BF), S((8, W), F32), S((1, FF), F32)),
        in_specs=[vm] * 9, out_specs=(vm, vm, hbm, hbm, hbm, vm, vm, vm, vm),
        scratch_shapes=[pltpu.VMEM((T, W), BF), pltpu.VMEM((W, T), BF), pltpu.VMEM((T, W), F32),
                        pltpu.VMEM((n, Halving.land(W, steps), C), BF),
                        pltpu.VMEM((n, Halving.land(C, steps), W), BF),
                        pltpu.VMEM((T, C), BF), pltpu.VMEM((T, C), BF),
                        dma((n, steps)), dma((n, steps)), dma((n, steps)), dma((n, steps)),
                        dma((3, ns)), dma((3, ns)), dma((3,))],
        compiler_params=pltpu.CompilerParams(vmem_limit_bytes=60 << 20, collective_id=0, has_side_effects=True),
    )(x, g, cs, gain.reshape(1, W), shift.reshape(1, W), wu, bu.reshape(1, FF), wd, bias.reshape(1, W))


def tail_kernel(sizes, groups, du_in, dd_in, da_in, small_in, attn_ref, ga_ref,
                du_ref, dd_ref, da_ref, small_ref, attn_out, ga_out,
                buf, land_x, land_y, land_s, *sems):
    s_ag, r_ag, s_x, r_x, s_y, r_y, s_s, r_s, sa, ra, sl = sems
    place = Place(sizes)
    ns = place.seq_n
    L = attn_ref.shape[0] // ns
    n_u, W, C = du_in.shape
    hu = Halving(place, W, place.core + place.dp_bits + place.seq_bits)
    hd = Halving(place, C, place.core + place.seq_bits + place.dp_bits)
    n_a, R, _ = da_in.shape
    hx = Halving(place, R // 2, place.core + place.seq_bits + place.dp_bits)
    hy = Halving(place, R // 2, place.core + place.seq_bits[::-1] + place.dp_bits)
    steps = len(hu.bits)
    place.enter()
    moves = []
    me = pl.ds(pl.multiple_of(place.seq * L, L), L)
    for a, (src, dst) in enumerate(((attn_ref, attn_out), (ga_ref, ga_out))):
        for k in range(ns - 1, 0, -1):
            to = place.peer(k)
            moves.append(pltpu.make_async_remote_copy(
                src.at[pl.ds(pl.multiple_of(to * L, L), L)], dst.at[place.seq], sa.at[a, k], ra.at[a, k],
                device_id=(to, place.dp), device_id_type=MESH))
        moves.append(pltpu.make_async_copy(src.at[me], dst.at[place.seq], sl.at[a]))
    loads = [pltpu.make_async_copy(da_in, buf, sl.at[2])]
    for n, (h, src, dst) in enumerate(((hu, du_in, du_ref), (hd, dd_in, dd_ref))):
        at = (slice(None), pl.ds(pl.multiple_of(h.lo, 16), h.n))
        loads.append(pltpu.make_async_copy(src.at[at], dst.at[at], sl.at[3 + n]))
    small_ref[...] = small_in[...]
    for m in loads:
        m.start()
    for m in loads:
        m.wait()
    half = R // 2
    size = n_u // groups
    pieces = []

    def gather(h, buf_of, at):
        ops = []
        for i in reversed(range(steps)):
            c = h.spread(i, buf_of, s_ag.at[at, i], r_ag.at[at, i])
            if c is not None:
                ops.append((c, None))
        return ops

    seqs = []
    for p in range(n_a):
        for h, lo, land, send, recv in ((hx, 0, land_x, s_x, r_x), (hy, half, land_y, s_y, r_y)):
            ops = []
            b = buf.at[p, pl.ds(lo, half)]
            for i in range(steps):
                c = h.copy(i, b, land.at[p], send.at[p, i], recv.at[p, i])
                ops.append((c, functools.partial(h.add, i, b, land.at[p])))
            seqs.append(ops)
    small_ops = []
    for i, bit in enumerate(hx.bits):
        c = pltpu.make_async_remote_copy(small_ref, land_s.at[i], s_s.at[i], r_s.at[i],
                                         device_id=place.partner(bit), device_id_type=MESH)

        def add(i=i):
            small_ref[...] += land_s[i]
        small_ops.append((c, add))
    seqs.append(small_ops)
    for gidx in range(groups):
        g = pl.ds(gidx * size, size)
        seqs.append(gather(hu, du_ref.at[g], 2 * gidx))
        seqs.append(gather(hd, dd_ref.at[g], 2 * gidx + 1))
    for ops in seqs:
        ops[0][0].start()
    for i in range(max(len(o) for o in seqs)):
        for ops in seqs:
            if i < len(ops):
                ops[i][0].wait()
                if ops[i][1] is not None:
                    ops[i][1]()
                if i + 1 < len(ops):
                    ops[i + 1][0].start()
    for m in moves:
        m.start()
    outs = []
    for n, (h, lo) in enumerate(((hx, 0), (hy, half))):
        at = (slice(None), pl.ds(pl.multiple_of(lo + h.lo, 16), h.n))
        outs.append(pltpu.make_async_copy(buf.at[at], da_ref.at[at], sl.at[3 + n]))
    for m in outs:
        m.start()
    for m in outs:
        m.wait()
    seqs = [gather(hx, da_ref.at[:, pl.ds(0, half)], 2 * groups), gather(hy, da_ref.at[:, pl.ds(half, half)], 2 * groups + 1)]
    for ops in seqs:
        ops[0][0].start()
    for i in range(max(len(o) for o in seqs)):
        for ops in seqs:
            if i < len(ops):
                ops[i][0].wait()
                if i + 1 < len(ops):
                    ops[i + 1][0].start()
    for m in moves:
        m.wait()


def tail_call(sizes, du, dd, da, small, attn, ga):
    ns = sizes[0]
    T, W = attn.shape
    L = T // ns
    n_a, R, _ = da.shape
    groups = 3
    steps = sum(s.bit_length() - 1 for s in sizes)
    vm = pl.BlockSpec(memory_space=pltpu.VMEM)
    hbm = pl.BlockSpec(memory_space=pl.ANY)
    S = jax.ShapeDtypeStruct
    dma = pltpu.SemaphoreType.DMA
    nl = Halving.land(R // 2, steps)
    return pl.pallas_call(
        functools.partial(tail_kernel, sizes, groups),
        out_shape=(S(du.shape, BF), S(dd.shape, BF), S(da.shape, BF), S(small.shape, F32),
                   S((ns, L, W), BF), S((ns, L, W), BF)),
        in_specs=[hbm, hbm, hbm, vm, vm, vm], out_specs=(hbm, hbm, hbm, vm, hbm, hbm),
        scratch_shapes=[pltpu.VMEM(da.shape, BF), pltpu.VMEM((n_a, nl, W), BF), pltpu.VMEM((n_a, nl, W), BF),
                        pltpu.VMEM((steps,) + small.shape, F32),
                        dma((2 * groups + 2, steps)), dma((2 * groups + 2, steps)),
                        dma((n_a, steps)), dma((n_a, steps)), dma((n_a, steps)), dma((n_a, steps)),
                        dma((steps,)), dma((steps,)), dma((2, ns)), dma((2, ns)), dma((5,))],
        compiler_params=pltpu.CompilerParams(vmem_limit_bytes=60 << 20, collective_id=1, has_side_effects=True),
    )(du, dd, da, small, attn, ga)


def on_device(hidden_in, positions, attn_gain, attn_shift, qkv_weight, qkv_bias, dense_weight, dense_bias,
              mlp_gain, mlp_shift, up_weight, up_bias, down_weight, down_bias, out_grad):
    sentences, local_len, width = hidden_in.shape
    sizes = (lax.axis_size("seq"), lax.axis_size("dp"))
    assert sentences == sizes[0]
    freqs = jnp.power(10000.0, -2.0 * jnp.arange(ROT // 2, dtype=F32) / ROT)
    angles = freqs[:, None] * positions.astype(F32)[:, None, :]
    cs = jnp.concatenate([jnp.cos(angles), jnp.sin(angles)], axis=1)
    y, gm, x_s, g_s, cs_s, du, dd, small_m, dbu = mlp_call(
        sizes, hidden_in, out_grad, cs, mlp_gain, mlp_shift, up_weight, up_bias, down_weight, dense_bias + down_bias)
    attn, ga, da, small_a, dbq = attn_call(
        x_s, g_s, cs_s, attn_gain, attn_shift, qkv_weight, qkv_bias, dense_weight)
    small = jnp.concatenate([small_a[0], small_a[1], small_m[0], small_m[1], small_m[2], dbq[0], dbu[0]]).reshape(-1, 128)
    du, dd, da, small, attn, ga = tail_call(sizes, du, dd, da, small, attn, ga)
    layer_out = (y.reshape(hidden_in.shape) + attn.astype(F32)).astype(BF)
    input_grad = (gm.reshape(hidden_in.shape) + ga.astype(F32)).astype(BF)
    s = small.reshape(-1)
    W = width
    n_u, _, C = du.shape
    dwu = jnp.transpose(du, (1, 0, 2)).reshape(W, n_u * C).astype(F32)
    dwd = dd.reshape(-1, W).astype(F32)
    da = da.reshape(-1, 4, 128, W)
    dwqkv = jnp.transpose(da[:, :3], (3, 1, 0, 2)).reshape(W, 3 * W).astype(F32)
    ddw = da[:, 3].reshape(W, W).astype(F32)
    db = s[4 * W:5 * W]
    return (layer_out, input_grad, s[:W], s[W:2 * W], dwqkv, s[5 * W:8 * W], ddw, db, s[2 * W:3 * W], s[3 * W:4 * W],
            dwu, s[8 * W:], dwd, db)


def solution(mesh):
    act, rep = P("dp", "seq", None), P()
    return jax.shard_map(
        on_device, mesh=mesh,
        in_specs=(act, P("dp", "seq")) + (rep,) * 12 + (act,),
        out_specs=(act, act) + (rep,) * 12,
        check_vma=False)
```

time: 475 us -> 419 us (0.88); the launches traced: 468 us -> 418 us
  Pallas kernels: 127 us -> 349 us
  waiting for transfers between devices: 142 us -> 0 us
  blocking collectives: 91.4 us -> 0 us
  other arithmetic: 45.1 us -> 26.9 us
  between operations: 14.4 us -> 0.8 us
  starting transfers between devices: 12.3 us -> 0 us
  local copies, waits for them, and re-layouts: 35.2 us -> 40.7 us
    pallas_call x2 -> x3, Pallas kernels: 127 us -> 349 us  [the longest x1 158 us: tail_call(): pl.pallas_call(functools.partial(tail_kernel, sizes, groups), out_shape=(...]
    psum x1 -> x0, waiting for transfers between devices: 137 us -> none  [on_device(): dwqkv, ddw = lax.psum((dwqkv, ddw), ('seq', 'dp'))]
    psum x1 -> x0, blocking collectives: 58.7 us -> none  [on_device(): lax.psum((small_a[0], small_a[1], dbq[0], small_m[0], small_m[1], small_m...]
    all_to_all x2 -> x0, blocking collectives: 32.8 us -> none  [to_sentence(): return lax.all_to_all(v, 'seq', 0, 1, tiled=True)[0]]
    unnamed x4 -> x1, other arithmetic: 23.2 us -> 0.01 us
    all_to_all x3 -> x0, starting transfers between devices: 12.3 us -> none  [the longest x2 8.71 us: to_rows(): return lax.all_to_all(v[None], 'seq', 1, 0, tiled=True)]
    convert_element_type x0 -> x1, local copies, waits for them, and re-layouts: none -> 9.63 us  [on_device(): dwu = jnp.transpose(du, (1, 0, 2)).reshape(W, n_u * C).astype(F32)]
    broadcast_in_dim x2 -> x0, local copies, waits for them, and re-layouts: 7.73 us -> none  [to_rows(): return lax.all_to_all(v[None], 'seq', 1, 0, tiled=True)]
  transfers between devices with their start and end apart: 4 -> 0, of which waited for: 2 -> 0; matrix products, arithmetic and copies ran while one was open for 12% -> 0% of each run, Pallas kernels for 11% -> 0%
where the time goes in v2:
time: 419 us; the launch traced here: 418 us
  Pallas kernels  349 us (83%)
  local copies, waits for them, and re-layouts  40.7 us (10%)
  other arithmetic  26.9 us (6%)
    pallas_call x1, Pallas kernels, tail_call(): pl.pallas_call(functools.partial(tail_kernel, sizes, groups), out_shape=(...  158 us
    pallas_call x1, Pallas kernels, mlp_call(): pl.pallas_call(functools.partial(mlp_kernel, sizes), out_shape=(S((T, W),...  116 us
    pallas_call x1, Pallas kernels, attn_call(): pl.pallas_call(attn_kernel, out_shape=(S((T, W), BF), S((T, W), BF), S((H...  74.6 us
    unnamed x21, local copies, waits for them, and re-layouts  18.8 us
    convert_element_type x1, local copies, waits for them, and re-layouts, on_device(): dwu = jnp.transpose(du, (1, 0, 2)).reshape(W, n_u * C).astype(F32)  9.63 us

profile of v2, /device:TPU:0, one launch (start us, length us, event | category | flops | bytes accessed | tf_op | source)
XLA Modules:
  0.0 417.7 jit_solution(4795444233763782818)
XLA Ops:
  0.7 1.3 reshape.91.gain_ref
  1.9 1.3 reshape.92.shift_ref
  3.2 1.3 reshape.86.gain_ref
  4.5 1.3 reshape.87.shift_ref
  5.7 0.7 convert_element_type.45
  6.4 0.7 add.9
  7.9 0.6 pad_maximum_fusion.cs_ref
  8.5 2.1 reshape.101.bqkv_ref
  10.6 116.3 %shard_map.254 = (f32[1024,768]{1,0:T(8,128)}, f32[1024,768]{1,0:T(8,128)}, bf16[1024,768]{1,0:T(8,128)(2,1)}, bf16[1024,768]{1,0:T(8,128)(2,1)}, f32[4,16,256]{...) custom-call(bf16[4,256,768]{2,1,0:T(8,128)(2,1)} %x_ref.1, ...), custom_call_target="tpu_custom_call" | custom-call | tf_op jit(solution)/shard_map/pallas_call | solution.py:358
  126.9 0.9 slice_reduce_fusion.1
  127.8 74.6 %shard_map.255 = (bf16[1024,768]{1,0:T(8,128)(2,1)}, bf16[1024,768]{1,0:T(8,128)(2,1)}, bf16[6,512,768]{2,1,0:T(8,128)(2,1)}, f32[8,768]{1,0:T(8,128)}, f32[8,2304]{1,0:T(8,128)}) custom-call(bf16[1024,768]{1,0:T(8,128)(2,1)} %get-tuple-element.37.x_ref, bf16[1024,768]{1,0:T(8,128)(2,1)} %get-tuple-element.38.g_ref, f32[4,16,256]{2,1,0:T(8,128)} %get-tuple-element.39.cs_ref, ...), custom_call_target="tpu_custom_call" | custom-call | tf_op jit(solution)/shard_map/pallas_call | solution.py:140
  202.4 0.8 slice_reduce_fusion.4
  203.3 0.9 slice_reduce_fusion
  204.3 0.6 copy-done.3
  204.9 158.5 %shard_map.256 = (bf16[12,768,256]{2,1,0:T(8,128)(2,1)}, bf16[12,256,768]{2,1,0:T(8,128)(2,1)}, bf16[6,512,768]{2,1,0:T(8,128)(2,1)}, f32[72,128]{1,0:T(8,128)},...) custom-call(bf16[12,768,256]{2,1,0:T(8,128)(2,1)} %get-tuple-element.35.du_in, ...), custom_call_target="tpu_custom_call" | custom-call | tf_op jit(solution)/shard_map/pallas_call | solution.py:485
  363.4 5.4 %add_convert_fusion = (bf16[4,256,768]{2,1,0:T(8,128)(2,1)}, bf16[4,256,768]{2,1,0:T(8,128)(2,1)}) fusion(f32[4,256,768]{2,1,0:T(8,128)} %bitcast.37, bf16[4,256,768]{2,1,0:T(8,128)(2,1)} %get-tuple-element.49, f32[4,256,768]{2,1,0:T(8,128)S(1)} %bitcast.36, bf16[4,256,768]{2,1,0:T(8,128)(2,1)} %get-tuple-element.47), kind=kLoop, calls=%fused_computation.3 | loop fusion | flops 4718592 | bytes 12582912 | tf_op jit(solution)/shard_map/convert_element_type | solution.py:514
  370.0 0.6 slice_bitcast_fusion.2
  370.7 1.7 bitcast_convert_fusion.1
  372.3 3.8 copy_convert_fusion
  376.1 8.0 %copy.33 = f32[768,2304]{1,0:T(8,128)} copy(f32[768,2304]{0,1:T(8,128)} %bitcast.33) | data formatting | bytes 14155776
  384.1 7.0 %convert_bitcast_fusion = f32[768,12,256]{2,0,1:T(8,128)} fusion(bf16[12,768,256]{2,1,0:T(8,128)(2,1)} %get-tuple-element.52), kind=kLoop, calls=%fused_computation | loop fusion | flops 2359296 | bytes 14155776 | tf_op jit(solution)/shard_map/convert_element_type | solution.py:518
  391.1 9.6 %copy.32 = f32[768,12,256]{0,2,1:T(8,128)} copy(f32[768,12,256]{2,0,1:T(8,128)} %convert_bitcast_fusion) | data formatting | bytes 18874368 | tf_op jit(solution)/shard_map/convert_element_type | solution.py:518
  400.7 9.6 %copy.34 = f32[768,3072]{1,0:T(8,128)} copy(f32[768,3072]{0,1:T(8,128)} %bitcast.32) | data formatting | bytes 18874368
  410.3 6.8 %bitcast_convert_fusion = f32[3072,768]{1,0:T(8,128)} fusion(bf16[12,256,768]{2,1,0:T(8,128)(2,1)} %get-tuple-element.53), kind=kLoop, calls=%fused_computation.1 | loop fusion | flops 2359296 | bytes 14155776 | tf_op jit(solution)/shard_map/convert_element_type | solution.py:519
  (26 shorter events, 2.7 us)
Async XLA Ops:
  127.8 76.4 %copy-start.5 = (f32[1,3072]{1,0:T(1,128)S(1)}, f32[1,3072]{1,0:T(1,128)}, u32[]{:S(2)}) copy-start(f32[1,3072]{1,0:T(1,128)} %get-tuple-element.44) | copy-start | bytes 36868
  204.3 0.6 copy-start.3
  204.9 158.5 %copy-start.1 = (f32[1024,768]{1,0:T(8,128)S(1)}, f32[1024,768]{1,0:T(8,128)}, u32[]{:S(2)}) copy-start(f32[1024,768]{1,0:T(8,128)} %get-tuple-element.34) | copy-start | bytes 9437188
  363.4 5.4 %copy-start.2 = (f32[72,128]{1,0:T(8,128)S(1)}, f32[72,128]{1,0:T(8,128)}, u32[]{:S(2)}) copy-start(f32[72,128]{1,0:T(8,128)} %get-tuple-element.50) | copy-start | bytes 110596
  363.4 7.2 %copy-start = (bf16[6,512,768]{2,1,0:T(8,128)(2,1)S(1)}, bf16[6,512,768]{2,1,0:T(8,128)(2,1)}, u32[]{:S(2)}) copy-start(bf16[6,512,768]{2,1,0:T(8,128)(2,1)} %get-tuple-element.51) | copy-start | bytes 14155780
  370.6 46.5 %copy-start.4 = (f32[768]{0:T(1024)}, f32[768]{0:T(1024)S(1)}, u32[]{:S(2)}) copy-start(f32[768]{0:T(1024)S(1)} %get-tuple-element.109) | copy-start | bytes 9220

commit v3 on v2

--- a/solution.py
+++ b/solution.py
@@ -20,11 +20,71 @@
     rstd = lax.rsqrt(jnp.mean(c * c, axis=-1, keepdims=True) + EPSILON)
     return c * rstd, rstd
 
-def attn_kernel(x_ref, g_ref, cs_ref, gain_ref, shift_ref, wqkv_ref, bqkv_ref, wd_ref,
-                attn_ref, ga_ref, da_ref, small_ref, dbq_ref,
-                wT, xaT, qkvT, kn, vn, dOT, obT, dmT):
+GROUPS = 3
+
+
+def attn_kernel(sizes, x_ref, g_ref, cs_ref, gain_ref, shift_ref, wqkv_ref, bqkv_ref, wd_ref, du_in, dd_in,
+                attn_ref, ga_ref, da_out, du_ref, dd_ref, small_ref, dbq_ref,
+                wT, xaT, qkvT, kn, vn, dOT, obT, dmT, da_ref, land_x, land_y,
+                s_x, r_x, s_y, r_y, s_u, r_u, s_d, r_d, sl):
     T, W = x_ref.shape
     nblk = T // BLK
+    place = Place(sizes)
+    n_u, _, C = du_ref.shape
+    hu = Halving(place, W, place.core + place.dp_bits + place.seq_bits)
+    hd = Halving(place, C, place.core + place.seq_bits + place.dp_bits)
+    pairs, R, _ = da_ref.shape
+    hx = Halving(place, R // 2, place.core + place.seq_bits + place.dp_bits)
+    hy = Halving(place, R // 2, place.core + place.seq_bits[::-1] + place.dp_bits)
+    steps = len(hx.bits)
+    place.enter()
+    loads = []
+    for n, (h, src, dst) in enumerate(((hu, du_in, du_ref), (hd, dd_in, dd_ref))):
+        loads.append(pltpu.make_async_copy(src, dst.at[:, pl.ds(pl.multiple_of(h.lo, 16), h.n)], sl.at[n]))
+    for m in loads:
+        m.start()
+
+    size = n_u // GROUPS
+    plan = {}
+    for gi in range(GROUPS):
+        grp = pl.ds(gi * size, size)
+        for h, buf, send, recv in ((hu, du_ref, s_u, r_u), (hd, dd_ref, s_d, r_d)):
+            ops = h.chain(buf.at[grp], send.at[gi], recv.at[gi])
+            at = gi * 4
+            for k in range(len(ops) + 1):
+                plan.setdefault(at, []).append(functools.partial(advance, ops, k))
+                if k < len(ops):
+                    at += 2 if k in (1, 2) else 1
+    last = max(plan)
+    assert last < nblk + 2 * pairs
+
+    def tick(slot, lo, hi):
+        for at in range(lo, hi + 1):
+            if at in plan:
+                @pl.when(slot == at)
+                def _():
+                    for act in plan[at]:
+                        act()
+
+    def each(p):
+        return ((hx, da_ref.at[p, pl.ds(0, R // 2)], land_x.at[p], s_x.at[p], r_x.at[p]),
+                (hy, da_ref.at[p, pl.ds(R // 2, R // 2)], land_y.at[p], s_y.at[p], r_y.at[p]))
+
+    def halve(p, s):
+        @pl.when((p >= 0) & (p < pairs))
+        def _():
+            for h, buf, land, send, recv in each(p):
+                if s > 0:
+                    h.copy(s - 1, buf, land, send.at[s - 1], recv.at[s - 1]).wait()
+                    h.add(s - 1, buf, land)
+                if s < steps:
+                    h.copy(s, buf, land, send.at[s], recv.at[s]).start()
+
+    def halves(i, second):
+        for s in range(1, steps + 1):
+            if (s % 2 == 0) == second:
+                halve(i - (s + 1) // 2, s)
+
     gain = gain_ref[...]; shift = shift_ref[...]
     for j in range(9):
         wT[j*256:(j+1)*256, :] = wqkv_ref[:, j*256:(j+1)*256].T
@@ -54,6 +114,12 @@
         g = g_ref[rows, :]
         for j in range(3):
             dOT[j*256:(j+1)*256, rows] = nt(wd_ref[j*256:(j+1)*256, :], g).astype(BF)
+
+        @pl.when(b == 0)
+        def _():
+            for m in loads:
+                m.wait()
+        tick(b, 0, nblk - 1)
 
     sub = lax.broadcasted_iota(jnp.int32, (BLK, BLK), 0)
     lane = lax.broadcasted_iota(jnp.int32, (BLK, BLK), 1)
@@ -107,10 +173,16 @@
                 d0, d1 = dk[b][:8], dk[b][8:16]
                 dmT[kr, sl] = jnp.concatenate([d0 * cos + d1 * sin, d1 * cos - d0 * sin, dk[b][16:]], axis=0).astype(BF)
                 dmT[vr, sl] = dv[b].astype(BF)
+            if hh == 0:
+                tick(nblk + 2 * hp, nblk, last)
+                halves(hp, False)
 
         dm = jnp.concatenate([dmT[pl.ds(r0, 128), :], dmT[pl.ds(W + r0, 128), :], dmT[pl.ds(2 * W + r0, 128), :]], axis=0)
         da_ref[hp, :384, :] = nt(dm, xaT[...]).astype(BF)
         da_ref[hp, 384:, :] = nn(obT[pl.ds(r0, 128), :], g_ref[...]).astype(BF)
+        tick(nblk + 2 * hp + 1, nblk, last)
+        halves(hp, True)
+        halve(hp, 0)
 
     small_ref[...] = jnp.zeros_like(small_ref)
     @pl.loop(0, nblk)
@@ -126,26 +198,54 @@
         dn = dxa * gain
         ga = rstd * (dn - jnp.mean(dn, axis=-1, keepdims=True) - xhat * jnp.mean(dn * xhat, axis=-1, keepdims=True))
         ga_ref[rows, :] = ga.astype(BF)
+
+        @pl.when(lax.rem(b, 2) == 0)
+        def _():
+            halves(pairs + b // 2, False)
+
+        @pl.when(lax.rem(b, 2) == 1)
+        def _():
+            halves(pairs + b // 2, True)
     @pl.loop(0, 9)
     def _(j):
         c = pl.ds(pl.multiple_of(j * 256, 256), 256)
         dbq_ref[:, c] = nt(jnp.ones((8, T), BF), dmT[c, :])
-
-
-def attn_call(x, g, cs, gain, shift, wqkv, bqkv, wd):
+    for i in range(nblk, 2 * ((steps + 1) // 2) + 1):
+        halves(pairs + i // 2, i % 2 == 1)
+    outs = []
+    for n, (h, lo) in enumerate(((hx, 0), (hy, R // 2))):
+        outs.append(pltpu.make_async_copy(da_ref.at[:, pl.ds(pl.multiple_of(lo + h.lo, 16), h.n)], da_out.at[:, n], sl.at[n]))
+    for m in outs:
+        m.start()
+    for m in outs:
+        m.wait()
+
+
+def attn_call(sizes, x, g, cs, gain, shift, wqkv, bqkv, wd, du, dd):
     T, W = x.shape
     assert T // cs.shape[0] == BLK
+    n, C = du.shape[0], du.shape[2]
+    assert dd.shape[0] == n
+    pairs, R = HEADS // 2, 512
+    steps = sum(s.bit_length() - 1 for s in sizes)
     vm = pl.BlockSpec(memory_space=pltpu.VMEM)
+    hbm = pl.BlockSpec(memory_space=pl.ANY)
     S = jax.ShapeDtypeStruct
+    dma = pltpu.SemaphoreType.DMA
+    land = Halving.land(R // 2, steps)
     return pl.pallas_call(
-        attn_kernel,
-        out_shape=(S((T, W), BF), S((T, W), BF), S((HEADS // 2, 512, W), BF), S((8, W), F32), S((8, 3 * W), F32)),
-        in_specs=[vm] * 8, out_specs=(vm,) * 5,
+        functools.partial(attn_kernel, sizes),
+        out_shape=(S((T, W), BF), S((T, W), BF), S((pairs, 2, Halving.left(R // 2, steps), W), BF),
+                   S((n, W, C), BF), S((n, C, W), BF), S((8, W), F32), S((8, 3 * W), F32)),
+        in_specs=[vm] * 8 + [hbm] * 2, out_specs=(vm, vm, hbm, hbm, hbm, vm, vm),
         scratch_shapes=[pltpu.VMEM((3 * W, W), BF), pltpu.VMEM((W, T), BF), pltpu.VMEM((3 * W, T), BF),
                         pltpu.VMEM((T, W), BF), pltpu.VMEM((T, W), BF), pltpu.VMEM((W, T), BF),
-                        pltpu.VMEM((W, T), BF), pltpu.VMEM((3 * W, T), BF)],
-        compiler_params=pltpu.CompilerParams(vmem_limit_bytes=60 << 20),
-    )(x, g, cs, gain.reshape(1, W), shift.reshape(1, W), wqkv, bqkv.reshape(3 * W, 1), wd)
+                        pltpu.VMEM((W, T), BF), pltpu.VMEM((3 * W, T), BF),
+                        pltpu.VMEM((pairs, R, W), BF), pltpu.VMEM((pairs, land, W), BF), pltpu.VMEM((pairs, land, W), BF),
+                        dma((pairs, steps)), dma((pairs, steps)), dma((pairs, steps)), dma((pairs, steps)),
+                        dma((GROUPS, steps)), dma((GROUPS, steps)), dma((GROUPS, steps)), dma((GROUPS, steps)), dma((2,))],
+        compiler_params=pltpu.CompilerParams(vmem_limit_bytes=60 << 20, collective_id=1, has_side_effects=True),
+    )(x, g, cs, gain.reshape(1, W), shift.reshape(1, W), wqkv, bqkv.reshape(3 * W, 1), wd, du, dd)
 
 
 MESH = pl.DeviceIdType.MESH
@@ -184,6 +284,13 @@
         for t in targets:
             pl.semaphore_signal(bar, inc=1, device_id=t, device_id_type=MESH)
         pl.semaphore_wait(bar, len(targets))
+
+
+def advance(ops, k):
+    if k > 0:
+        ops[k - 1].wait()
+    if k < len(ops):
+        ops[k].start()
 
 
 class Halving:
@@ -208,6 +315,12 @@
             off += n
         return off
 
+    @staticmethod
+    def left(rows, count, unit=16):
+        for _ in range(count):
+            rows = rows // 2 if rows % (2 * unit) == 0 else rows
+        return rows
+
     def copy(self, i, buf, land, send, recv):
         bit, _, part, _, give, off = self.plan[i]
         return pltpu.make_async_remote_copy(
@@ -227,6 +340,10 @@
         return pltpu.make_async_remote_copy(
             buf.at[at], buf.at[at], send, recv, device_id=self.place.partner(bit), device_id_type=MESH)
 
+    def chain(self, buf, send, recv):
+        ops = [self.spread(i, buf, send.at[i], recv.at[i]) for i in reversed(range(len(self.bits)))]
+        return [c for c in ops if c is not None]
+
 
 def cdf_pdf(h):
     t = 1.0 / (1.0 + (0.3275911 * 0.5 ** 0.5) * jnp.abs(h))
@@ -237,9 +354,12 @@
     return jnp.where(h >= 0, 1.0 - tail, tail), ez * 0.3989422804014327
 
 
+MOVES = 8
+
+
 def mlp_kernel(sizes, x_ref, g_ref, cs_ref, gain_ref, shift_ref, wu_ref, bu_ref, wd_ref, bias_ref,
-               y_ref, gm_ref, xs_ref, gs_ref, css_ref, du_ref, dd_ref, small_ref, dbu_ref,
-               xm, xmT, dxm, land_u, land_d, a_s, dh_s, su, ru, sd, rd, sa, ra, sl):
+               y_ref, gm_ref, xs_ref, gs_ref, css_ref, du_out, dd_out, small_ref, dbu_ref,
+               xm, xmT, dxm, du_ref, dd_ref, land_u, land_d, a_s, dh_s, su, ru, sd, rd, sa, ra, sc, rc, sl):
     place = Place(sizes)
     ns = place.seq_n
     L, W = x_ref.shape[1:]
@@ -250,17 +370,28 @@
     steps = len(hu.bits)
     place.enter()
 
-    moves = []
+    part = L // MOVES
+
+    def moves(i):
+        out = []
+        for a, (src, dst) in enumerate(((x_ref, xs_ref), (g_ref, gs_ref))):
+            for k in range(ns - 1, 0, -1):
+                to = place.peer(k)
+                out.append(pltpu.make_async_remote_copy(
+                    src.at[to, pl.ds(pl.multiple_of(i * part, part), part)],
+                    dst.at[pl.ds(pl.multiple_of(place.seq * L + i * part, part), part)],
+                    sa.at[a, k, i], ra.at[a, k, i], device_id=(to, place.dp), device_id_type=MESH))
+        return out
+
+    once = []
     me = pl.ds(pl.multiple_of(place.seq * L, L), L)
-    for a, (src, dst) in enumerate(((x_ref, xs_ref), (g_ref, gs_ref), (cs_ref, css_ref))):
-        for k in range(ns - 1, 0, -1):
-            to = place.peer(k)
-            moves.append(pltpu.make_async_remote_copy(
-                src.at[to], dst.at[place.seq] if a == 2 else dst.at[me], sa.at[a, k], ra.at[a, k],
-                device_id=(to, place.dp), device_id_type=MESH))
-        moves.append(pltpu.make_async_copy(
-            src.at[place.seq], dst.at[place.seq] if a == 2 else dst.at[me], sl.at[a]))
-    for m in moves:
+    for k in range(ns - 1, 0, -1):
+        to = place.peer(k)
+        once.append(pltpu.make_async_remote_copy(
+            cs_ref.at[to], css_ref.at[place.seq], sc.at[k], rc.at[k], device_id=(to, place.dp), device_id_type=MESH))
+    for a, (src, dst) in enumerate(((x_ref, xs_ref.at[me]), (g_ref, gs_ref.at[me]), (cs_ref, css_ref.at[place.seq]))):
+        once.append(pltpu.make_async_copy(src.at[place.seq], dst, sl.at[a]))
+    for m in once + moves(0):
         m.start()
 
     gain = gain_ref[...]
@@ -288,6 +419,11 @@
     @pl.loop(0, n_chunk + steps)
     def _(j):
         c = pl.ds(pl.multiple_of(jnp.minimum(j, n_chunk - 1) * C, C), C)
+
+        @pl.when((j > 0) & (j < MOVES))
+        def _():
+            for m in moves(j):
+                m.start()
 
         @pl.when(j < n_chunk)
         def _():
@@ -340,7 +476,17 @@
             gm_ref[rows, :] = gf + rstd * (dn - jnp.mean(dn, axis=-1, keepdims=True)
                                            - xhat * jnp.mean(dn * xhat, axis=-1, keepdims=True))
 
-    for m in moves:
+    outs = []
+    for n, (h, src, dst) in enumerate(((hu, du_ref, du_out), (hd, dd_ref, dd_out))):
+        outs.append(pltpu.make_async_copy(src.at[:, pl.ds(pl.multiple_of(h.lo, 16), h.n)], dst, sl.at[3 + n]))
+    for m in outs:
+        m.start()
+
+    @pl.loop(0, MOVES)
+    def _(i):
+        for m in moves(i):
+            m.wait()
+    for m in once + outs:
         m.wait()
 
 
@@ -358,33 +504,37 @@
     return pl.pallas_call(
         functools.partial(mlp_kernel, sizes),
         out_shape=(S((T, W), F32), S((T, W), F32), S((T, W), BF), S((T, W), BF), S(cs.shape, F32),
-                   S((n, W, C), BF), S((n, C, W), BF), S((8, W), F32), S((1, FF), F32)),
-        in_specs=[vm] * 9, out_specs=(vm, vm, hbm, hbm, hbm, vm, vm, vm, vm),
+                   S((n, Halving.left(W, steps), C), BF), S((n, Halving.left(C, steps), W), BF), S((8, W), F32), S((1, FF), F32)),
+        in_specs=[vm] * 9, out_specs=(vm, vm, hbm, hbm, hbm, hbm, hbm, vm, vm),
         scratch_shapes=[pltpu.VMEM((T, W), BF), pltpu.VMEM((W, T), BF), pltpu.VMEM((T, W), F32),
+                        pltpu.VMEM((n, W, C), BF), pltpu.VMEM((n, C, W), BF),
                         pltpu.VMEM((n, Halving.land(W, steps), C), BF),
                         pltpu.VMEM((n, Halving.land(C, steps), W), BF),
                         pltpu.VMEM((T, C), BF), pltpu.VMEM((T, C), BF),
                         dma((n, steps)), dma((n, steps)), dma((n, steps)), dma((n, steps)),
-                        dma((3, ns)), dma((3, ns)), dma((3,))],
+                        dma((2, ns, MOVES)), dma((2, ns, MOVES)), dma((ns,)), dma((ns,)), dma((5,))],
         compiler_params=pltpu.CompilerParams(vmem_limit_bytes=60 << 20, collective_id=0, has_side_effects=True),
     )(x, g, cs, gain.reshape(1, W), shift.reshape(1, W), wu, bu.reshape(1, FF), wd, bias.reshape(1, W))
 
 
-def tail_kernel(sizes, groups, du_in, dd_in, da_in, small_in, attn_ref, ga_ref,
-                du_ref, dd_ref, da_ref, small_ref, attn_out, ga_out,
-                buf, land_x, land_y, land_s, *sems):
-    s_ag, r_ag, s_x, r_x, s_y, r_y, s_s, r_s, sa, ra, sl = sems
+def tail_kernel(sizes, da_in, small_in, attn_ref, ga_ref,
+                da_ref, small_ref, attn_out, ga_out,
+                land_s, s_ag, r_ag, s_s, r_s, sa, ra, sl):
     place = Place(sizes)
     ns = place.seq_n
     L = attn_ref.shape[0] // ns
-    n_u, W, C = du_in.shape
-    hu = Halving(place, W, place.core + place.dp_bits + place.seq_bits)
-    hd = Halving(place, C, place.core + place.seq_bits + place.dp_bits)
-    n_a, R, _ = da_in.shape
-    hx = Halving(place, R // 2, place.core + place.seq_bits + place.dp_bits)
-    hy = Halving(place, R // 2, place.core + place.seq_bits[::-1] + place.dp_bits)
-    steps = len(hu.bits)
+    n_a, R, _ = da_ref.shape
+    half = R // 2
+    hx = Halving(place, half, place.core + place.seq_bits + place.dp_bits)
+    hy = Halving(place, half, place.core + place.seq_bits[::-1] + place.dp_bits)
     place.enter()
+    loads = []
+    for n, (h, lo) in enumerate(((hx, 0), (hy, half))):
+        at = (slice(None), pl.ds(pl.multiple_of(lo + h.lo, 16), h.n))
+        loads.append(pltpu.make_async_copy(da_in.at[:, n], da_ref.at[at], sl.at[2 + n]))
+    small_ref[...] = small_in[...]
+    for m in loads:
+        m.start()
     moves = []
     me = pl.ds(pl.multiple_of(place.seq * L, L), L)
     for a, (src, dst) in enumerate(((attn_ref, attn_out), (ga_ref, ga_out))):
@@ -394,106 +544,116 @@
                 src.at[pl.ds(pl.multiple_of(to * L, L), L)], dst.at[place.seq], sa.at[a, k], ra.at[a, k],
                 device_id=(to, place.dp), device_id_type=MESH))
         moves.append(pltpu.make_async_copy(src.at[me], dst.at[place.seq], sl.at[a]))
-    loads = [pltpu.make_async_copy(da_in, buf, sl.at[2])]
-    for n, (h, src, dst) in enumerate(((hu, du_in, du_ref), (hd, dd_in, dd_ref))):
-        at = (slice(None), pl.ds(pl.multiple_of(h.lo, 16), h.n))
-        loads.append(pltpu.make_async_copy(src.at[at], dst.at[at], sl.at[3 + n]))
-    small_ref[...] = small_in[...]
-    for m in loads:
-        m.start()
     for m in loads:
         m.wait()
-    half = R // 2
-    size = n_u // groups
-    pieces = []
-
-    def gather(h, buf_of, at):
-        ops = []
-        for i in reversed(range(steps)):
-            c = h.spread(i, buf_of, s_ag.at[at, i], r_ag.at[at, i])
-            if c is not None:
-                ops.append((c, None))
-        return ops
-
-    seqs = []
-    for p in range(n_a):
-        for h, lo, land, send, recv in ((hx, 0, land_x, s_x, r_x), (hy, half, land_y, s_y, r_y)):
-            ops = []
-            b = buf.at[p, pl.ds(lo, half)]
-            for i in range(steps):
-                c = h.copy(i, b, land.at[p], send.at[p, i], recv.at[p, i])
-                ops.append((c, functools.partial(h.add, i, b, land.at[p])))
-            seqs.append(ops)
-    small_ops = []
-    for i, bit in enumerate(hx.bits):
-        c = pltpu.make_async_remote_copy(small_ref, land_s.at[i], s_s.at[i], r_s.at[i],
-                                         device_id=place.partner(bit), device_id_type=MESH)
-
-        def add(i=i):
-            small_ref[...] += land_s[i]
-        small_ops.append((c, add))
-    seqs.append(small_ops)
-    for gidx in range(groups):
-        g = pl.ds(gidx * size, size)
-        seqs.append(gather(hu, du_ref.at[g], 2 * gidx))
-        seqs.append(gather(hd, dd_ref.at[g], 2 * gidx + 1))
-    for ops in seqs:
-        ops[0][0].start()
-    for i in range(max(len(o) for o in seqs)):
-        for ops in seqs:
-            if i < len(ops):
-                ops[i][0].wait()
-                if ops[i][1] is not None:
-                    ops[i][1]()
-                if i + 1 < len(ops):
-                    ops[i + 1][0].start()
-    for m in moves:
-        m.start()
-    outs = []
-    for n, (h, lo) in enumerate(((hx, 0), (hy, half))):
-        at = (slice(None), pl.ds(pl.multiple_of(lo + h.lo, 16), h.n))
-        outs.append(pltpu.make_async_copy(buf.at[at], da_ref.at[at], sl.at[3 + n]))
-    for m in outs:
-        m.start()
-    for m in outs:
-        m.wait()
-    seqs = [gather(hx, da_ref.at[:, pl.ds(0, half)], 2 * groups), gather(hy, da_ref.at[:, pl.ds(half, half)], 2 * groups + 1)]
-    for ops in seqs:
-        ops[0][0].start()
-    for i in range(max(len(o) for o in seqs)):
-        for ops in seqs:
-            if i < len(ops):
-                ops[i][0].wait()
-                if i + 1 < len(ops):
-                    ops[i + 1][0].start()
+    chains = [hx.chain(da_ref.at[:, pl.ds(0, half)], s_ag.at[0], r_ag.at[0]),
+              hy.chain(da_ref.at[:, pl.ds(half, half)], s_ag.at[1], r_ag.at[1])]
+    small = [pltpu.make_async_remote_copy(small_ref, land_s.at[i], s_s.at[i], r_s.at[i],
+                                          device_id=place.partner(bit), device_id_type=MESH)
+             for i, bit in enumerate(hx.bits)]
+    for i in range(len(small) + 1):
+        for ops in chains:
+            if i <= len(ops):
+                advance(ops, i)
+        if i > 0:
+            small[i - 1].wait()
+            small_ref[...] += land_s[i - 1]
+        if i < len(small):
+            small[i].start()
+        if i == 0:
+            for m in moves:
+                m.start()
     for m in moves:
         m.wait()
 
 
-def tail_call(sizes, du, dd, da, small, attn, ga):
+def tail_call(sizes, da, small, attn, ga):
     ns = sizes[0]
     T, W = attn.shape
     L = T // ns
-    n_a, R, _ = da.shape
-    groups = 3
+    pairs, R = da.shape[0], 512
     steps = sum(s.bit_length() - 1 for s in sizes)
     vm = pl.BlockSpec(memory_space=pltpu.VMEM)
     hbm = pl.BlockSpec(memory_space=pl.ANY)
     S = jax.ShapeDtypeStruct
     dma = pltpu.SemaphoreType.DMA
-    nl = Halving.land(R // 2, steps)
     return pl.pallas_call(
-        functools.partial(tail_kernel, sizes, groups),
-        out_shape=(S(du.shape, BF), S(dd.shape, BF), S(da.shape, BF), S(small.shape, F32),
-                   S((ns, L, W), BF), S((ns, L, W), BF)),
-        in_specs=[hbm, hbm, hbm, vm, vm, vm], out_specs=(hbm, hbm, hbm, vm, hbm, hbm),
-        scratch_shapes=[pltpu.VMEM(da.shape, BF), pltpu.VMEM((n_a, nl, W), BF), pltpu.VMEM((n_a, nl, W), BF),
-                        pltpu.VMEM((steps,) + small.shape, F32),
-                        dma((2 * groups + 2, steps)), dma((2 * groups + 2, steps)),
-                        dma((n_a, steps)), dma((n_a, steps)), dma((n_a, steps)), dma((n_a, steps)),
-                        dma((steps,)), dma((steps,)), dma((2, ns)), dma((2, ns)), dma((5,))],
-        compiler_params=pltpu.CompilerParams(vmem_limit_bytes=60 << 20, collective_id=1, has_side_effects=True),
-    )(du, dd, da, small, attn, ga)
+        functools.partial(tail_kernel, sizes),
+        out_shape=(S((pairs, R, W), BF), S(small.shape, F32), S((ns, L, W), BF), S((ns, L, W), BF)),
+        in_specs=[hbm, vm, hbm, hbm], out_specs=(hbm, vm, hbm, hbm),
+        scratch_shapes=[pltpu.VMEM((steps,) + small.shape, F32), dma((2, steps)), dma((2, steps)),
+                        dma((steps,)), dma((steps,)), dma((2, ns)), dma((2, ns)), dma((4,))],
+        compiler_params=pltpu.CompilerParams(collective_id=2, has_side_effects=True),
+    )(da, small, attn, ga)
+
+
+def finish_kernel(du, dd, da, y, gm, attn, ga, dwu, dwd, dwqkv, ddw, out, grad,
+                  vu, vd, va, ou, od, oq, ow, vy, vm, vo, vg, s_in, s_out):
+    n, W, C = du.shape
+    pairs = da.shape[0]
+    tokens = y.shape[0]
+    ins, outs = [], []
+
+    def fetch(src, dst):
+        c = pltpu.make_async_copy(src, dst, s_in.at[len(ins)])
+        ins.append(c)
+        c.start()
+        return c
+
+    def store(src, dst):
+        c = pltpu.make_async_copy(src, dst, s_out.at[len(outs)])
+        outs.append(c)
+        c.start()
+
+    fu = [fetch(du.at[i], vu.at[i]) for i in range(n)]
+    fd = [fetch(dd.at[i], vd.at[i]) for i in range(n)]
+    fa = [fetch(da.at[i], va.at[i]) for i in range(pairs)]
+    fy = [fetch(a, b) for a, b in ((y, vy), (attn, vo), (gm, vm), (ga, vg))]
+    for i in range(n):
+        c = slice(i * C, (i + 1) * C)
+        fu[i].wait()
+        ou[:, c] = vu[i].astype(F32)
+        store(ou.at[:, c], dwu.at[:, c])
+        fd[i].wait()
+        od[c, :] = vd[i].astype(F32)
+        store(od.at[c, :], dwd.at[c, :])
+    for i in range(pairs):
+        fa[i].wait()
+        for k in range(3):
+            c = slice(k * W + i * 128, k * W + (i + 1) * 128)
+            oq[:, c] = va[i, k * 128:(k + 1) * 128, :].astype(F32).T
+            store(oq.at[:, c], dwqkv.at[:, c])
+        c = slice(i * 128, (i + 1) * 128)
+        ow[c, :] = va[i, 384:, :].astype(F32)
+        store(ow.at[c, :], ddw.at[c, :])
+    for f in fy:
+        f.wait()
+    vo[...] = (vy[...] + vo[...].astype(F32)).astype(BF)
+    store(vo, out)
+    vg[...] = (vm[...] + vg[...].astype(F32)).astype(BF)
+    store(vg, grad)
+    for c in outs:
+        c.wait()
+
+
+def finish_call(du, dd, da, y, gm, attn, ga):
+    n, W, C = du.shape
+    pairs, R, _ = da.shape
+    FF = n * C
+    tokens = y.shape[0]
+    hbm = pl.BlockSpec(memory_space=pl.ANY)
+    S = jax.ShapeDtypeStruct
+    V = pltpu.VMEM
+    dma = pltpu.SemaphoreType.DMA
+    return pl.pallas_call(
+        finish_kernel,
+        out_shape=(S((W, FF), F32), S((FF, W), F32), S((W, 3 * W), F32), S((W, W), F32), S((tokens, W), BF), S((tokens, W), BF)),
+        in_specs=[hbm] * 7, out_specs=(hbm,) * 6,
+        scratch_shapes=[V(du.shape, BF), V(dd.shape, BF), V(da.shape, BF), V((W, FF), F32), V((FF, W), F32),
+                        V((W, 3 * W), F32), V((W, W), F32), V((tokens, W), F32), V((tokens, W), F32),
+                        V((tokens, W), BF), V((tokens, W), BF), dma((2 * n + pairs + 4,)), dma((2 * n + 4 * pairs + 2,))],
+        compiler_params=pltpu.CompilerParams(vmem_limit_bytes=62 << 20),
+    )(du, dd, da, y, gm, attn, ga)
 
 
 def on_device(hidden_in, positions, attn_gain, attn_shift, qkv_weight, qkv_bias, dense_weight, dense_bias,
@@ -506,23 +666,16 @@
     cs = jnp.concatenate([jnp.cos(angles), jnp.sin(angles)], axis=1)
     y, gm, x_s, g_s, cs_s, du, dd, small_m, dbu = mlp_call(
         sizes, hidden_in, out_grad, cs, mlp_gain, mlp_shift, up_weight, up_bias, down_weight, dense_bias + down_bias)
-    attn, ga, da, small_a, dbq = attn_call(
-        x_s, g_s, cs_s, attn_gain, attn_shift, qkv_weight, qkv_bias, dense_weight)
+    attn, ga, da, du, dd, small_a, dbq = attn_call(
+        sizes, x_s, g_s, cs_s, attn_gain, attn_shift, qkv_weight, qkv_bias, dense_weight, du, dd)
     small = jnp.concatenate([small_a[0], small_a[1], small_m[0], small_m[1], small_m[2], dbq[0], dbu[0]]).reshape(-1, 128)
-    du, dd, da, small, attn, ga = tail_call(sizes, du, dd, da, small, attn, ga)
-    layer_out = (y.reshape(hidden_in.shape) + attn.astype(F32)).astype(BF)
-    input_grad = (gm.reshape(hidden_in.shape) + ga.astype(F32)).astype(BF)
+    da, small, attn, ga = tail_call(sizes, da, small, attn, ga)
+    W = width
+    dwu, dwd, dwqkv, ddw, layer_out, input_grad = finish_call(du, dd, da, y, gm, attn.reshape(-1, W), ga.reshape(-1, W))
     s = small.reshape(-1)
-    W = width
-    n_u, _, C = du.shape
-    dwu = jnp.transpose(du, (1, 0, 2)).reshape(W, n_u * C).astype(F32)
-    dwd = dd.reshape(-1, W).astype(F32)
-    da = da.reshape(-1, 4, 128, W)
-    dwqkv = jnp.transpose(da[:, :3], (3, 1, 0, 2)).reshape(W, 3 * W).astype(F32)
-    ddw = da[:, 3].reshape(W, W).astype(F32)
     db = s[4 * W:5 * W]
-    return (layer_out, input_grad, s[:W], s[W:2 * W], dwqkv, s[5 * W:8 * W], ddw, db, s[2 * W:3 * W], s[3 * W:4 * W],
-            dwu, s[8 * W:], dwd, db)
+    return (layer_out.reshape(hidden_in.shape), input_grad.reshape(hidden_in.shape), s[:W], s[W:2 * W], dwqkv,
+            s[5 * W:8 * W], ddw, db, s[2 * W:3 * W], s[3 * W:4 * W], dwu, s[8 * W:], dwd, db)
 
 
 def solution(mesh):

time: 419 us -> 353 us (0.84)
  local copies, waits for them, and re-layouts: 40.7 us -> 11.4 us
  other arithmetic: 26.9 us -> 2.25 us
  Pallas kernels: 349 us -> 338 us
    convert_element_type x5 -> x0, other arithmetic: 24.6 us -> none  [the longest x1 7.01 us: on_device(): dwu = jnp.transpose(du, (1, 0, 2)).reshape(W, n_u * C).astype(F32)]
    unnamed x21, local copies, waits for them, and re-layouts: 18.8 us -> 1.26 us
    pallas_call x1, Pallas kernels: 116 us -> 104 us  [mlp_call(): pl.pallas_call(functools.partial(mlp_kernel, sizes), out_shape=(S((T, W),...]
    convert_element_type x1 -> x0, local copies, waits for them, and re-layouts: 9.63 us -> none  [on_device(): dwu = jnp.transpose(du, (1, 0, 2)).reshape(W, n_u * C).astype(F32)]
    pallas_call x2 -> x3, Pallas kernels: 233 us -> 234 us  [the longest x1 138 us: attn_call(): pl.pallas_call(functools.partial(attn_kernel, sizes), out_shape=(S((T, W)...]
where the time goes in v3:
time: 353 us
  Pallas kernels  338 us (96%)
  local copies, waits for them, and re-layouts  11.4 us (3%)
    pallas_call x1, Pallas kernels, attn_call(): pl.pallas_call(functools.partial(attn_kernel, sizes), out_shape=(S((T, W)...  138 us
    pallas_call x1, Pallas kernels, mlp_call(): pl.pallas_call(functools.partial(mlp_kernel, sizes), out_shape=(S((T, W),...  104 us
    pallas_call x1, Pallas kernels, tail_call(): pl.pallas_call(functools.partial(tail_kernel, sizes), out_shape=(S((pairs...  76.2 us
    pallas_call x1, Pallas kernels, finish_call(): pl.pallas_call(finish_kernel, out_shape=(S((W, FF), F32), S((FF, W), F32)...  20 us

profile of v3, /device:TPU:0, one launch (start us, length us, event | category | flops | bytes accessed | tf_op | source)
XLA Modules:
  0.0 352.8 jit_solution(13971359519401838075)
XLA Ops:
  0.6 0.7 convert_element_type.3
  1.3 0.2 multiply_cosine_fusion
  1.6 0.6 pad_maximum_fusion.cs_ref
  2.2 0.7 add.3
  2.9 0.6 reshape.81.bias_ref
  3.5 1.3 reshape.78.gain_ref
  4.7 1.3 reshape.79.shift_ref
  6.0 103.9 %shard_map.254 = (f32[1024,768]{1,0:T(8,128)}, f32[1024,768]{1,0:T(8,128)}, bf16[1024,768]{1,0:T(8,128)(2,1)}, bf16[1024,768]{1,0:T(8,128)(2,1)}, f32[4,16,256]{...) custom-call(bf16[4,256,768]{2,1,0:T(8,128)(2,1)} %x_ref.1, ...), custom_call_target="tpu_custom_call" | custom-call | tf_op jit(solution)/shard_map/pallas_call | solution.py:504
  110.0 0.0 copy-done.3
  110.0 1.4 reshape.90.bqkv_ref
  111.4 0.6 reshape.82.gain_ref
  111.9 0.6 reshape.83.shift_ref
  112.5 138.3 %shard_map.255 = (bf16[1024,768]{1,0:T(8,128)(2,1)}, bf16[1024,768]{1,0:T(8,128)(2,1)}, bf16[6,2,16,768]{3,2,1,0:T(8,128)(2,1)}, bf16[12,768,256]{2,1,0:T(8,128)...) custom-call(bf16[1024,768]{1,0:T(8,128)(2,1)} %get-tuple-element.40.x_ref, ...), custom_call_target="tpu_custom_call" | custom-call | tf_op jit(solution)/shard_map/pallas_call | solution.py:236
  250.8 0.8 slice_reduce_fusion.4
  251.7 0.9 slice_reduce_fusion.1
  252.7 0.9 slice_reduce_fusion
  253.6 0.0 copy-start.1
  253.6 0.6 copy-done.1
  254.2 76.2 %shard_map.256 = (bf16[6,512,768]{2,1,0:T(8,128)(2,1)}, f32[72,128]{1,0:T(8,128)}, bf16[4,256,768]{2,1,0:T(8,128)(2,1)}, bf16[4,256,768]{2,1,0:T(8,128)(2,1)}) custom-call(bf16[6,2,16,768]{3,2,1,0:T(8,128)(2,1)} %get-tuple-element.47.da_in, f32[72,128]{1,0:T(8,128)} %bitcast.23, bf16[1024,768]{1,0:T(8,128)(2,1)} %get-tuple-element.52.attn_ref, ...), custom_call_target="tpu_custom_call" | custom-call | tf_op jit(solution)/shard_map/pallas_call | solution.py:580
  330.4 20.0 %shard_map.257 = (f32[768,3072]{1,0:T(8,128)}, f32[3072,768]{1,0:T(8,128)}, f32[768,2304]{1,0:T(8,128)}, f32[768,768]{1,0:T(8,128)}, bf16[1024,768]{1,0:T(8,128)(2,1)}, /*index=5*/bf16[1024,768]{1,0:T(8,128)(2,1)}) custom-call(bf16[12,768,256]{2,1,0:T(8,128)(2,1)} %get-tuple-element.45.du, bf16[12,256,768]{2,1,0:T(8,128)(2,1)} %get-tuple-element.46.dd, ...), custom_call_target="tpu_custom_call" | custom-call | tf_op jit(solution)/shard_map/pallas_call | solution.py:648
  350.4 0.6 slice_bitcast_fusion.2
  351.0 0.6 slice_bitcast_fusion
  351.6 0.6 slice_bitcast_fusion.1
  352.2 0.6 copy.38
  (20 shorter events, 0.1 us)
Async XLA Ops:
  6.0 104.0 %copy-start.3 = (f32[2304]{0:T(1024)S(1)}, f32[2304]{0:T(1024)}, u32[]{:S(2)}) copy-start(f32[2304]{0:T(1024)} %param.20) | copy-start | bytes 27652
  6.0 105.3 %copy-start.5 = (f32[768]{0:T(1024)S(1)}, f32[768]{0:T(1024)}, u32[]{:S(2)}) copy-start(f32[768]{0:T(1024)} %param.17) | copy-start | bytes 9220
  6.0 105.9 %copy-start.6 = (f32[768]{0:T(1024)S(1)}, f32[768]{0:T(1024)}, u32[]{:S(2)}) copy-start(f32[768]{0:T(1024)} %param.18) | copy-start | bytes 9220
  112.5 141.1 %copy-start.4 = (f32[1,3072]{1,0:T(1,128)S(1)}, f32[1,3072]{1,0:T(1,128)}, u32[]{:S(2)}) copy-start(f32[1,3072]{1,0:T(1,128)} %get-tuple-element.51) | copy-start | bytes 36868
  253.6 0.6 copy-start.1
  330.4 20.0 %copy-start = (f32[72,128]{1,0:T(8,128)S(1)}, f32[72,128]{1,0:T(8,128)}, u32[]{:S(2)}) copy-start(f32[72,128]{1,0:T(8,128)} %get-tuple-element.61) | copy-start | bytes 110596
  351.0 1.8 copy-start.2

commit v4 on v1

v4 whole, which is shorter than its diff:
```python
import functools
import jax
import jax.numpy as jnp
from jax import lax
from jax.experimental import pallas as pl
from jax.experimental.pallas import tpu as pltpu
from jax.sharding import PartitionSpec as P

HEADS = 12
HEAD = 64
ROT = 16
EPSILON = 1e-05
NEGATIVE = -1e30
BF, F32 = jnp.bfloat16, jnp.float32
MESH = pl.DeviceIdType.MESH
CHUNK = 256
MOVES = 8


def nn(a, b):
    return lax.dot_general(a, b, (((1,), (0,)), ((), ())), preferred_element_type=F32)


def nt(a, b):
    return lax.dot_general(a, b, (((1,), (1,)), ((), ())), preferred_element_type=F32)


def tn(a, b):
    return lax.dot_general(a, b, (((0,), (0,)), ((), ())), preferred_element_type=F32)


def norm_parts(x):
    center = x - jnp.mean(x, axis=-1, keepdims=True)
    rstd = lax.rsqrt(jnp.mean(center * center, axis=-1, keepdims=True) + EPSILON)
    return center * rstd, rstd


def norm_back(grad, xhat, rstd):
    return rstd * (grad - jnp.mean(grad, axis=-1, keepdims=True) - xhat * jnp.mean(grad * xhat, axis=-1, keepdims=True))


def cdf_pdf(h):
    t = 1.0 / (1.0 + (0.3275911 * 0.5 ** 0.5) * jnp.abs(h))
    ez = jnp.exp(-0.5 * h * h)
    poly = t * (0.5 * 0.254829592 + t * (0.5 * -0.284496736 + t * (
        0.5 * 1.421413741 + t * (0.5 * -1.453152027 + t * (0.5 * 1.061405429)))))
    tail = poly * ez
    return jnp.where(h >= 0, 1.0 - tail, tail), ez * 0.3989422804014327


def mul8(v):
    return pl.multiple_of(v, 16)


class Place:
    def __init__(self, sizes):
        self.seq_n, self.dp_n = sizes
        self.seq = lax.axis_index("seq")
        self.dp = lax.axis_index("dp")
        self.seq_bits, self.dp_bits = [], []
        for b in range(self.seq_n.bit_length() - 1):
            mine = lax.rem(self.seq // (1 << b), 2)
            self.seq_bits.append((mine, (self.seq + (1 << b) * (1 - 2 * mine), self.dp)))
        for b in range(self.dp_n.bit_length() - 1):
            mine = lax.rem(self.dp // (1 << b), 2)
            self.dp_bits.append((mine, (self.seq, self.dp + (1 << b) * (1 - 2 * mine))))
        self.core, self.dp_bits = self.dp_bits[:1], self.dp_bits[1:]

    def seq_first(self, turn):
        mixed = []
        for a, b in zip(self.seq_bits, self.seq_bits[::-1]):
            mine = a[0] + turn * (b[0] - a[0])
            mixed.append((mine, (a[1][0] + turn * (b[1][0] - a[1][0]), self.dp)))
        return self.core + mixed + self.dp_bits

    def seq_last(self):
        return self.core + self.dp_bits + self.seq_bits

    def peer(self, k):
        at = self.seq
        for b, (mine, _) in enumerate(self.seq_bits):
            at = at + (1 << b) * lax.rem(k // (1 << b), 2) * (1 - 2 * mine)
        return at

    def enter(self):
        targets = [(self.peer(jnp.int32(k)), self.dp) for k in range(1, self.seq_n)]
        targets += [bit[1] for bit in self.core + self.dp_bits]
        bar = pltpu.get_barrier_semaphore()
        for t in targets:
            pl.semaphore_signal(bar, inc=1, device_id=t, device_id_type=MESH)
        pl.semaphore_wait(bar, len(targets))


class Halving:
    def __init__(self, rows, bits):
        self.plan = []
        lo, n, off = 0, rows, 0
        for mine, partner in bits:
            halve = n % 32 == 0
            part = n // 2 if halve else n
            keep = lo + mine * part if halve else lo
            give = lo + (1 - mine) * part if halve else lo
            self.plan.append((partner, halve, part, keep, give, off))
            lo, n, off = keep, part, off + part
        self.lo, self.n = lo, n

    @staticmethod
    def land(rows, count):
        n, off = rows, 0
        for _ in range(count):
            n = n // 2 if n % 32 == 0 else n
            off += n
        return off

    def copy(self, i, buf, land, send, recv):
        partner, _, part, _, give, off = self.plan[i]
        return pltpu.make_async_remote_copy(
            buf.at[pl.ds(mul8(give), part)], land.at[pl.ds(off, part)], send.at[i], recv.at[i],
            device_id=partner, device_id_type=MESH)

    def finish(self, i, buf, land, send, recv):
        self.copy(i, buf, land, send, recv).wait()
        _, _, part, keep, _, off = self.plan[i]
        rows = pl.ds(mul8(keep), part)
        buf[rows] = (buf[rows].astype(F32) + land[pl.ds(off, part)].astype(F32)).astype(buf.dtype)

    def own(self, lo=0):
        return (slice(None), pl.ds(mul8(lo + self.lo), self.n))

    def chain(self, buf, send, recv):
        ops = []
        for i in reversed(range(len(self.plan))):
            partner, halve, part, keep, _, _ = self.plan[i]
            if halve:
                at = (slice(None), pl.ds(mul8(keep), part))
                ops.append(pltpu.make_async_remote_copy(
                    buf.at[at], buf.at[at], send.at[i], recv.at[i], device_id=partner, device_id_type=MESH))
        return ops


def advance(ops, k):
    if k > 0:
        ops[k - 1].wait()
    if k < len(ops):
        ops[k].start()


ENDS_M = (1, 3, 5, 6, 7, 8, 9)
ENDS_A = (1, 2, 3, 4, 5, 6, 7)
GAIN_A, SHIFT_A, GAIN_M, SHIFT_M, BIAS, BIAS_QKV, BIAS_UP = 0, 1, 2, 3, 4, 5, 8
SMALL = 16


def layer_kernel(sizes, x_in, g_in, cs_ref, vec_ref, bqkv_ref, wu_in, wd_in, wqkv_in, wo_in,
                 y_out, gm_out, du_out, dd_out, da_out, attn_out, ga_out, small_out,
                 du, dd, land_u, land_d, da, land_x, land_y, xs, gs, css, small, land_s,
                 su, ru, sd, rd, sx, rx, sy, ry, s_u, r_u, s_d, r_d, s_x, r_x, s_y, r_y,
                 s_in, r_in, s_c, r_c, s_out, r_out, s_s, r_s, s_l):
    place = Place(sizes)
    ns = place.seq_n
    _, L, W = x_in.shape
    T = ns * L
    n_chunk, _, C = du.shape
    pairs, R, _ = da.shape
    H2 = R // 2
    hu = Halving(W, place.seq_last())
    steps = len(hu.plan)
    hx = Halving(H2, place.seq_first(0))
    hy = Halving(H2, place.seq_first(1))
    last_m = ENDS_M[steps - 1]
    last_a = ENDS_A[steps - 1]
    t_l = n_chunk
    t_p = t_l + 1
    t_h = t_p + ns
    t_e = t_h + HEADS
    t_g = t_e + 1
    t_s = t_g + ns
    local = iter(range(100))

    place.enter()

    def mlp_pieces(p):
        at = lax.rem(p, 2) * (n_chunk // 2) + p // 2
        hd = Halving(C, place.seq_first(lax.rem(p, 2)))
        return ((hu, (du.at[at], land_u.at[at], su.at[at], ru.at[at])),
                (hd, (dd.at[at], land_d.at[at], sd.at[at], rd.at[at])))

    def attn_pieces(p):
        return ((hx, (da.at[p, pl.ds(0, H2)], land_x.at[p], sx.at[p], rx.at[p])),
                (hy, (da.at[p, pl.ds(H2, H2)], land_y.at[p], sy.at[p], ry.at[p])))

    def begin(pieces):
        for h, refs in pieces:
            h.copy(0, *refs).start()

    def halve(pieces, s):
        for h, refs in pieces:
            h.finish(s, *refs)
            if s + 1 < steps:
                h.copy(s + 1, *refs).start()

    plan = {}

    def spread(at, gaps, srcs):
        for h, src, dst, lo, send, recv in srcs:
            sem = s_l.at[next(local)]
            own = pltpu.make_async_copy(src.at[h.own(lo)], dst.at[h.own(lo)], sem)
            view = dst.at[:, pl.ds(lo, H2)] if src.shape[1] == R and h in (hx, hy) else dst
            ops = h.chain(view, send, recv)
            t = at
            plan.setdefault(t, []).append(own.start)
            t += 1
            plan.setdefault(t, []).append(own.wait)
            for k in range(len(ops) + 1):
                plan.setdefault(t, []).append(functools.partial(advance, ops, k))
                t += gaps[min(k, len(gaps) - 1)]

    half = n_chunk // 2
    third = half // 2
    for gi in range(4):
        turn, lo = gi // 2, (gi // 2) * half + (gi % 2) * third
        made = 2 * ((gi % 2) * third + third - 1) + turn
        grp = pl.ds(lo, third)
        hd = Halving(C, place.seq_first(turn))
        spread(made + last_m, (2, 2, 2, 1, 1), ((hu, du.at[grp], du_out.at[grp], 0, s_u.at[gi], r_u.at[gi]),
                                                (hd, dd.at[grp], dd_out.at[grp], 0, s_d.at[gi], r_d.at[gi])))
    for gi in range(2):
        grp = pl.ds(gi * (pairs // 2), pairs // 2)
        made = t_h + 2 * ((gi + 1) * (pairs // 2) - 1) + 1
        spread(made + last_a, (1,), ((hx, da.at[grp], da_out.at[grp], 0, s_x.at[gi], r_x.at[gi]),
                                     (hy, da.at[grp], da_out.at[grp], H2, s_y.at[gi], r_y.at[gi])))
    for i in range(steps + 1):
        def exchange(i=i):
            def cp(i):
                return pltpu.make_async_remote_copy(small, land_s.at[i], s_s.at[i], r_s.at[i],
                                                    device_id=place.seq_last()[i][1], device_id_type=MESH)
            if i > 0:
                cp(i - 1).wait()
                small[...] += land_s[i - 1]
            if i < steps:
                cp(i).start()
        plan.setdefault(t_s + i, []).append(exchange)
    end = max(plan) + 1

    def tick(t, lo, hi):
        for s in range(steps):
            p = t - ENDS_M[s]

            @pl.when((p >= 0) & (p < n_chunk))
            def _():
                halve(mlp_pieces(p), s)
        if hi > t_h:
            for s in range(steps):
                q = t - t_h - 1 - ENDS_A[s]

                @pl.when((q >= 0) & (q < 2 * pairs) & (lax.rem(q + 2 * pairs, 2) == 0))
                def _():
                    halve(attn_pieces(q // 2), s)
        for at in range(lo, hi):
            if at in plan:
                @pl.when(t == at)
                def _():
                    for act in plan[at]:
                        act()

    part = L // MOVES

    def moves(i):
        out = []
        for a, (src, dst) in enumerate(((x_in, xs), (g_in, gs))):
            for k in range(ns - 1, 0, -1):
                to = place.peer(jnp.int32(k))
                out.append(pltpu.make_async_remote_copy(
                    src.at[to, pl.ds(mul8(i * part), part)], dst.at[pl.ds(mul8(place.seq * L + i * part), part)],
                    s_in.at[a, k, i], r_in.at[a, k, i], device_id=(to, place.dp), device_id_type=MESH))
        return out

    once = []
    me = pl.ds(mul8(place.seq * L), L)
    for k in range(ns - 1, 0, -1):
        to = place.peer(jnp.int32(k))
        once.append(pltpu.make_async_remote_copy(
            cs_ref.at[to], css.at[place.seq], s_c.at[k], r_c.at[k], device_id=(to, place.dp), device_id_type=MESH))
    for src, dst in ((x_in, xs.at[me]), (g_in, gs.at[me]), (cs_ref, css.at[place.seq])):
        once.append(pltpu.make_async_copy(src.at[place.seq], dst, s_l.at[next(local)]))

    def row(i):
        return vec_ref[i:i + 1, :]

    def feed_forward(wu_ref, wd_ref, x_ref, g_ref, xm, xmT, dxm, y, a_s, dh_s):
        loads = [pltpu.make_async_copy(src, dst, s_l.at[next(local)])
                 for src, dst in ((x_in, x_ref), (g_in, g_ref), (wu_in, wu_ref), (wd_in, wd_ref))]
        for m in loads + once + moves(0):
            m.start()
        loads[0].wait()
        small[...] = jnp.zeros_like(small)
        for b in range(ns):
            rows = slice(b * L, (b + 1) * L)
            x = x_ref[b].astype(F32)
            xhat, _ = norm_parts(x)
            v = (xhat * row(2) + row(3)).astype(BF)
            xm[rows, :] = v
            xmT[:, rows] = v.T
            y[rows, :] = x + row(4)
        dxm[...] = jnp.zeros_like(dxm)
        for m in loads[1:]:
            m.wait()

        @pl.loop(0, t_l + 1)
        def _(t):
            c = pl.ds(pl.multiple_of(jnp.minimum(t, n_chunk - 1) * C, C), C)

            @pl.when((t > 0) & (t < 4) | (t > 4) & (t < 2 * MOVES - 4) & (lax.rem(t, 2) == 1))
            def _():
                for m in moves(jnp.where(t < 4, t, (t + 3) // 2)):
                    m.start()

            @pl.when(t < n_chunk)
            def _():
                wu = wu_ref[:, c]
                wd = wd_ref[c, :]
                bu = vec_ref[pl.ds(8 + t // 3, 1), pl.ds(pl.multiple_of(lax.rem(t, 3) * C, C), C)]
                dbu = jnp.zeros((1, C), F32)
                for b in range(ns):
                    rows = slice(b * L, (b + 1) * L)
                    h = nn(xm[rows, :], wu) + bu
                    cdf, pdf = cdf_pdf(h)
                    a_s[rows, :] = (h * cdf).astype(BF)
                    dh = (nt(g_ref[b], wd) * (cdf + h * pdf)).astype(BF)
                    dh_s[rows, :] = dh
                    dbu += jnp.sum(dh.astype(F32), axis=0, keepdims=True)
                small[pl.ds(BIAS_UP + t // 3, 1), pl.ds(pl.multiple_of(lax.rem(t, 3) * C, C), C)] = dbu

            tick(t, 0, t_l + 1)

            @pl.when(t < n_chunk)
            def _():
                wu = wu_ref[:, c]
                wd = wd_ref[c, :]
                dh = dh_s[...]
                a = a_s[...]
                at = lax.rem(t, 2) * (n_chunk // 2) + t // 2
                du[at] = nn(xmT[...], dh).astype(BF)
                dd[at] = tn(a, g_ref[...].reshape(T, W)).astype(BF)
                begin(mlp_pieces(t))
                y[...] += nn(a, wd)
                dxm[...] += nt(dh, wu)

            @pl.when(t == t_l)
            def _():
                store = pltpu.make_async_copy(y, y_out, s_l.at[next(local)])
                store.start()
                for b in range(ns):
                    rows = slice(b * L, (b + 1) * L)
                    xhat, rstd = norm_parts(x_ref[b].astype(F32))
                    dxa = dxm[rows, :]
                    gf = g_ref[b].astype(F32)
                    small[GAIN_M:GAIN_M + 1, :] += jnp.sum(dxa * xhat, axis=0, keepdims=True)
                    small[SHIFT_M:SHIFT_M + 1, :] += jnp.sum(dxa, axis=0, keepdims=True)
                    small[BIAS:BIAS + 1, :] += jnp.sum(gf, axis=0, keepdims=True)
                    dxm[rows, :] = gf + norm_back(dxa * row(2), xhat, rstd)
                back = pltpu.make_async_copy(dxm, gm_out, s_l.at[next(local)])
                back.start()
                store.wait()
                back.wait()

        @pl.loop(0, MOVES)
        def _(i):
            for m in moves(i):
                m.wait()
        for m in once:
            m.wait()

    def attention(wqkv, wo, wT, xaT, qkvT, kn, vn, dOT, obT, attn, ga):
        loads = [pltpu.make_async_copy(src, dst, s_l.at[next(local)]) for src, dst in ((wqkv_in, wqkv), (wo_in, wo))]
        for m in loads:
            m.start()
        for m in loads:
            m.wait()
        for j in range(9):
            wT[j * 256:(j + 1) * 256, :] = wqkv[:, j * 256:(j + 1) * 256].T
        sub = lax.broadcasted_iota(jnp.int32, (L, L), 0)
        lane = lax.broadcasted_iota(jnp.int32, (L, L), 1)
        keep = sub <= lane
        rowid = lax.broadcasted_iota(jnp.int32, (128, 1), 0)

        def back_copy(a, k, src, dst):
            to = place.peer(k)
            return pltpu.make_async_remote_copy(
                src.at[pl.ds(mul8(to * L), L)], dst.at[place.seq], s_out.at[a, k], r_out.at[a, k],
                device_id=(to, place.dp), device_id_type=MESH)

        def own_copy(a, src, dst):
            return pltpu.make_async_copy(src.at[me], dst.at[place.seq], s_out.at[a, 0])

        def unrotate(d, b):
            cos = css[b, :8, :]
            sin = css[b, 8:, :]
            return jnp.concatenate([d[:8] * cos + d[8:16] * sin, d[8:16] * cos - d[:8] * sin, d[16:]], axis=0)

        @pl.loop(t_p, end)
        def _(t):
            tick(t, t_p, end)

            @pl.when(t < t_h)
            def _():
                b = t - t_p
                rows = pl.ds(pl.multiple_of(b * L, L), L)
                xhat, _ = norm_parts(xs[rows, :].astype(F32))
                xa = (xhat * row(0) + row(1)).astype(BF)
                xaT[:, rows] = xa.T
                cos = css[b, :8, :]
                sin = css[b, 8:, :]
                for j in range(9):
                    at = slice(j * 256, (j + 1) * 256)
                    m = nt(wT[at, :], xa) + bqkv_ref[at, :]
                    if j < 6:
                        parts = []
                        for h in range(4):
                            u = m[h * 64:(h + 1) * 64]
                            parts += [u[:8] * cos - u[8:16] * sin, u[8:16] * cos + u[:8] * sin, u[16:]]
                        m = jnp.concatenate(parts, axis=0)
                        if j < 3:
                            m = m * (HEAD ** -0.5)
                    mb = m.astype(BF)
                    qkvT[at, rows] = mb
                    if 3 <= j < 6:
                        kn[rows, (j - 3) * 256:(j - 2) * 256] = mb.T
                    if j >= 6:
                        vn[rows, (j - 6) * 256:(j - 5) * 256] = mb.T
                g = gs[rows, :]
                for j in range(3):
                    at = slice(j * 256, (j + 1) * 256)
                    dOT[at, rows] = nt(wo[at, :], g).astype(BF)

            @pl.when((t >= t_h) & (t < t_e))
            def _():
                head = t - t_h
                pair = head // 2
                r0 = pl.multiple_of(pair * 128, 128)
                cols = pl.ds(r0, 128)
                hr = pl.ds(pl.multiple_of(head * 64, 64), 64)
                kr = pl.ds(pl.multiple_of(W + head * 64, 64), 64)
                vr = pl.ds(pl.multiple_of(2 * W + head * 64, 64), 64)
                msk = rowid // 64 == lax.rem(head, 2)
                dk = [None] * ns
                dv = [None] * ns
                dq = [None] * ns
                for i in range(ns):
                    n = (i + 1) * L
                    qs = slice(i * L, (i + 1) * L)
                    qT2 = jnp.where(msk, qkvT[cols, qs], 0).astype(BF)
                    dO2 = jnp.where(msk, dOT[cols, qs], 0).astype(BF)
                    s = nn(kn[0:n, cols], qT2)
                    d = jnp.where(keep, s[n - L:], NEGATIVE)
                    s = jnp.concatenate([s[:n - L], d], axis=0) if i > 0 else d
                    e = jnp.exp(s - jnp.max(s, axis=0, keepdims=True))
                    inv = 1.0 / jnp.sum(e, axis=0, keepdims=True)
                    p = e.astype(BF)
                    oT = nn(qkvT[vr, 0:n], p) * inv
                    dO = dOT[hr, qs].astype(F32)
                    delta = jnp.sum(dO * oT, axis=0, keepdims=True)
                    obT[hr, qs] = oT.astype(BF)
                    dp = nn(vn[0:n, cols], dO2)
                    ds = (e * ((dp - delta) * inv)).astype(BF)
                    dq[i] = nn(qkvT[kr, 0:n], ds) * (HEAD ** -0.5)
                    dkT = nt(qkvT[hr, qs], ds)
                    dvT = nt((dO * inv).astype(BF), p)
                    for b in range(i + 1):
                        sl = slice(b * L, (b + 1) * L)
                        dk[b] = dkT[:, sl] if dk[b] is None else dk[b] + dkT[:, sl]
                        dv[b] = dvT[:, sl] if dv[b] is None else dv[b] + dvT[:, sl]
                for b in range(ns):
                    sl = slice(b * L, (b + 1) * L)
                    qkvT[hr, sl] = unrotate(dq[b], b).astype(BF)
                    qkvT[kr, sl] = unrotate(dk[b], b).astype(BF)
                    qkvT[vr, sl] = dv[b].astype(BF)

                @pl.when(lax.rem(head, 2) == 1)
                def _():
                    dm = jnp.concatenate([qkvT[cols, :], qkvT[pl.ds(W + r0, 128), :], qkvT[pl.ds(2 * W + r0, 128), :]], axis=0)
                    da[pair, :384, :] = nt(dm, xaT[...]).astype(BF)
                    da[pair, 384:, :] = nn(obT[cols, :], gs[...]).astype(BF)
                    begin(attn_pieces(pair))
                    db = nt(jnp.ones((8, T), BF), dm)
                    for i in range(3):
                        small[BIAS_QKV + i:BIAS_QKV + i + 1, cols] = db[0:1, i * 128:(i + 1) * 128]

            @pl.when(t == t_e)
            def _():
                for k in range(ns - 1, -1, -1):
                    b = place.peer(jnp.int32(k))
                    rows = pl.ds(pl.multiple_of(b * L, L), L)
                    attn[rows, :] = nn(obT[:, rows].T, wo[...]).astype(BF)
                    if k > 0:
                        back_copy(0, k, attn, attn_out).start()
                    else:
                        own_copy(0, attn, attn_out).start()

            @pl.when((t >= t_g) & (t < t_s))
            def _():
                k = t_s - 1 - t
                b = place.peer(k)
                rows = pl.ds(pl.multiple_of(b * L, L), L)
                dxa = nn(wqkv[...], qkvT[:, rows]).T
                xhat, rstd = norm_parts(xs[rows, :].astype(F32))
                small[GAIN_A:GAIN_A + 1, :] += jnp.sum(dxa * xhat, axis=0, keepdims=True)
                small[SHIFT_A:SHIFT_A + 1, :] += jnp.sum(dxa, axis=0, keepdims=True)
                ga[rows, :] = norm_back(dxa * row(0), xhat, rstd).astype(BF)

                @pl.when(k > 0)
                def _():
                    back_copy(1, k, ga, ga_out).start()

                @pl.when(k == 0)
                def _():
                    own_copy(1, ga, ga_out).start()

        for a, (src, dst) in enumerate(((attn, attn_out), (ga, ga_out))):
            for k in range(ns - 1, 0, -1):
                back_copy(a, jnp.int32(k), src, dst).wait()
            own_copy(a, src, dst).wait()
        small_out[...] = small[...]

    V = pltpu.VMEM
    FF = n_chunk * C
    pl.run_scoped(feed_forward, V((W, FF), BF), V((FF, W), BF), V((ns, L, W), BF), V((ns, L, W), BF), V((T, W), BF),
                  V((W, T), BF), V((T, W), F32), V((T, W), F32), V((T, C), BF), V((T, C), BF))
    pl.run_scoped(attention, V((W, 3 * W), BF), V((W, W), BF), V((3 * W, W), BF), V((W, T), BF), V((3 * W, T), BF), V((T, W), BF), V((T, W), BF),
                  V((W, T), BF), V((W, T), BF), V((T, W), BF), V((T, W), BF))


def layer_call(sizes, x, g, cs, vec, bqkv, wu, wd, wqkv, wo):
    ns, L, W = x.shape
    T = ns * L
    FF = wu.shape[1]
    C = CHUNK
    n = FF // C
    pairs, R = HEADS // 2, 4 * 2 * HEAD
    steps = sum(s.bit_length() - 1 for s in sizes)
    vm = pl.BlockSpec(memory_space=pltpu.VMEM)
    hbm = pl.BlockSpec(memory_space=pl.ANY)
    S = jax.ShapeDtypeStruct
    V = pltpu.VMEM
    dma = pltpu.SemaphoreType.DMA
    la = Halving.land(R // 2, steps)
    return pl.pallas_call(
        functools.partial(layer_kernel, sizes),
        out_shape=(S((T, W), F32), S((T, W), F32), S((n, W, C), BF), S((n, C, W), BF), S((pairs, R, W), BF),
                   S((ns, L, W), BF), S((ns, L, W), BF), S((SMALL, W), F32)),
        in_specs=[hbm, hbm, vm, vm, vm, hbm, hbm, hbm, hbm], out_specs=(hbm,) * 7 + (vm,),
        scratch_shapes=[V((n, W, C), BF), V((n, C, W), BF), V((n, Halving.land(W, steps), C), BF),
                        V((n, Halving.land(C, steps), W), BF), V((pairs, R, W), BF), V((pairs, la, W), BF),
                        V((pairs, la, W), BF), V((T, W), BF), V((T, W), BF), V(cs.shape, F32), V((SMALL, W), F32), V((steps, SMALL, W), F32)]
        + [dma((n, steps))] * 4 + [dma((pairs, steps))] * 4 + [dma((4, steps))] * 4 + [dma((2, steps))] * 4
        + [dma((2, ns, MOVES))] * 2 + [dma((ns,))] * 2 + [dma((2, ns))] * 2 + [dma((steps,))] * 2 + [dma((32,))],
        compiler_params=pltpu.CompilerParams(vmem_limit_bytes=62 << 20, collective_id=0, has_side_effects=True),
    )(x, g, cs, vec, bqkv, wu, wd, wqkv, wo)


def finish_kernel(du, dd, da, y, gm, attn, ga, dwu, dwd, dwqkv, ddw, out, grad,
                  vu, vd, va, ou, od, oq, ow, vy, vm, vo, vg, s_in, s_out):
    n, W, C = du.shape
    pairs = da.shape[0]
    ins, outs = [], []

    def fetch(src, dst):
        c = pltpu.make_async_copy(src, dst, s_in.at[len(ins)])
        ins.append(c)
        c.start()
        return c

    def store(src, dst):
        c = pltpu.make_async_copy(src, dst, s_out.at[len(outs)])
        outs.append(c)
        c.start()

    fu = [fetch(du.at[i], vu.at[i]) for i in range(n)]
    fd = [fetch(dd.at[i], vd.at[i]) for i in range(n)]
    fa = [fetch(da.at[i], va.at[i]) for i in range(pairs)]
    fy = [fetch(a, b) for a, b in ((y, vy), (attn, vo), (gm, vm), (ga, vg))]
    for i in range(n):
        j = 2 * i if i < n // 2 else 2 * (i - n // 2) + 1
        c = slice(j * C, (j + 1) * C)
        fu[i].wait()
        ou[:, c] = vu[i].astype(F32)
        store(ou.at[:, c], dwu.at[:, c])
        fd[i].wait()
        od[c, :] = vd[i].astype(F32)
        store(od.at[c, :], dwd.at[c, :])
    for i in range(pairs):
        fa[i].wait()
        for k in range(3):
            c = slice(k * W + i * 128, k * W + (i + 1) * 128)
            oq[:, c] = va[i, k * 128:(k + 1) * 128, :].astype(F32).T
            store(oq.at[:, c], dwqkv.at[:, c])
        c = slice(i * 128, (i + 1) * 128)
        ow[c, :] = va[i, 384:, :].astype(F32)
        store(ow.at[c, :], ddw.at[c, :])
    for f in fy:
        f.wait()
    vo[...] = (vy[...] + vo[...].astype(F32)).astype(BF)
    store(vo, out)
    vg[...] = (vm[...] + vg[...].astype(F32)).astype(BF)
    store(vg, grad)
    for c in outs:
        c.wait()


def finish_call(du, dd, da, y, gm, attn, ga):
    n, W, C = du.shape
    pairs = da.shape[0]
    FF = n * C
    tokens = y.shape[0]
    hbm = pl.BlockSpec(memory_space=pl.ANY)
    S = jax.ShapeDtypeStruct
    V = pltpu.VMEM
    dma = pltpu.SemaphoreType.DMA
    return pl.pallas_call(
        finish_kernel,
        out_shape=(S((W, FF), F32), S((FF, W), F32), S((W, 3 * W), F32), S((W, W), F32), S((tokens, W), BF), S((tokens, W), BF)),
        in_specs=[hbm] * 7, out_specs=(hbm,) * 6,
        scratch_shapes=[V(du.shape, BF), V(dd.shape, BF), V(da.shape, BF), V((W, FF), F32), V((FF, W), F32),
                        V((W, 3 * W), F32), V((W, W), F32), V((tokens, W), F32), V((tokens, W), F32),
                        V((tokens, W), BF), V((tokens, W), BF), dma((2 * n + pairs + 4,)), dma((2 * n + 4 * pairs + 2,))],
        compiler_params=pltpu.CompilerParams(vmem_limit_bytes=62 << 20),
    )(du, dd, da, y, gm, attn, ga)


def on_device(hidden_in, positions, attn_gain, attn_shift, qkv_weight, qkv_bias, dense_weight, dense_bias,
              mlp_gain, mlp_shift, up_weight, up_bias, down_weight, down_bias, out_grad):
    sentences, local_len, W = hidden_in.shape
    sizes = (lax.axis_size("seq"), lax.axis_size("dp"))
    assert sentences == sizes[0]
    freqs = jnp.power(10000.0, -2.0 * jnp.arange(ROT // 2, dtype=F32) / ROT)
    angles = freqs[:, None] * positions.astype(F32)[:, None, :]
    cs = jnp.concatenate([jnp.cos(angles), jnp.sin(angles)], axis=1)
    zero = jnp.zeros((W,), F32)
    vec = jnp.concatenate([attn_gain, attn_shift, mlp_gain, mlp_shift, dense_bias + down_bias, zero, zero, zero,
                           up_bias, zero, zero, zero, zero]).reshape(16, W)
    y, gm, du, dd, da, attn, ga, small = layer_call(
        sizes, hidden_in, out_grad, cs, vec, qkv_bias.reshape(-1, 1), up_weight, down_weight, qkv_weight, dense_weight)
    dwu, dwd, dwqkv, ddw, layer_out, input_grad = finish_call(du, dd, da, y, gm, attn.reshape(-1, W), ga.reshape(-1, W))
    db = small[BIAS]
    return (layer_out.reshape(hidden_in.shape), input_grad.reshape(hidden_in.shape), small[GAIN_A], small[SHIFT_A], dwqkv,
            small[BIAS_QKV:BIAS_UP].reshape(-1), ddw, db, small[GAIN_M], small[SHIFT_M], dwu,
            small[BIAS_UP:BIAS_UP + 4].reshape(-1), dwd, db)


def solution(mesh):
    act, rep = P("dp", "seq", None), P()
    return jax.shard_map(
        on_device, mesh=mesh,
        in_specs=(act, P("dp", "seq")) + (rep,) * 12 + (act,),
        out_specs=(act, act) + (rep,) * 12,
        check_vma=False)
```

time: 475 us -> 290 us (0.61); the launches traced: 468 us -> 290 us
  Pallas kernels: 127 us -> 276 us
  waiting for transfers between devices: 142 us -> 0 us
  blocking collectives: 91.4 us -> 0 us
  other arithmetic: 45.1 us -> 2.25 us
  local copies, waits for them, and re-layouts: 35.2 us -> 11.1 us
  between operations: 14.4 us -> 0.68 us
  starting transfers between devices: 12.3 us -> 0 us
    pallas_call x2, Pallas kernels: 127 us -> 276 us  [the longest x1 256 us: layer_call(): pl.pallas_call(functools.partial(layer_kernel, sizes), out_shape=(S((T, W...]
    psum x1 -> x0, waiting for transfers between devices: 137 us -> none  [on_device(): dwqkv, ddw = lax.psum((dwqkv, ddw), ('seq', 'dp'))]
    psum x1 -> x0, blocking collectives: 58.7 us -> none  [on_device(): lax.psum((small_a[0], small_a[1], dbq[0], small_m[0], small_m[1], small_m...]
    all_to_all x2 -> x0, blocking collectives: 32.8 us -> none  [to_sentence(): return lax.all_to_all(v, 'seq', 0, 1, tiled=True)[0]]
    unnamed x4 -> x2, other arithmetic: 23.2 us -> 0.71 us
    convert_element_type x6 -> x1, other arithmetic: 21.1 us -> 0.69 us  [on_device(): angles = freqs[:, None] * positions.astype(F32)[:, None, :]]
    unnamed x42 -> x9, local copies, waits for them, and re-layouts: 20.7 us -> 4.08 us
    all_to_all x3 -> x0, starting transfers between devices: 12.3 us -> none  [the longest x2 8.71 us: to_rows(): return lax.all_to_all(v[None], 'seq', 1, 0, tiled=True)]
  transfers between devices with their start and end apart: 4 -> 0, of which waited for: 2 -> 0; matrix products, arithmetic and copies ran while one was open for 12% -> 0% of each run, Pallas kernels for 11% -> 0%
where the time goes in v4:
time: 290 us
  Pallas kernels  276 us (95%)
  local copies, waits for them, and re-layouts  11.1 us (4%)
    pallas_call x1, Pallas kernels, layer_call(): pl.pallas_call(functools.partial(layer_kernel, sizes), out_shape=(S((T, W...  256 us
    pallas_call x1, Pallas kernels, finish_call(): pl.pallas_call(finish_kernel, out_shape=(S((W, FF), F32), S((FF, W), F32)...  20 us

profile of v4, /device:TPU:0, one launch (start us, length us, event | category | flops | bytes accessed | tf_op | source)
XLA Modules:
  0.0 289.6 jit_solution(11849958525515558571)
XLA Ops:
  0.7 0.7 convert_element_type.3
  1.4 0.7 constant_dynamic-update-slice_fusion.5
  2.0 0.7 constant_dynamic-update-slice_fusion.4
  2.7 0.7 constant_dynamic-update-slice_fusion.3
  3.4 0.7 constant_dynamic-update-slice_fusion.2
  4.1 0.7 constant_dynamic-update-slice_fusion.1
  4.8 0.7 constant_dynamic-update-slice_fusion
  5.5 0.6 reshape.58.vec_ref
  6.2 0.2 multiply_cosine_fusion
  6.4 0.6 pad_maximum_fusion.cs_ref
  7.0 2.1 reshape.66.bqkv_ref
  9.1 255.6 %shard_map.254 = (f32[1024,768]{1,0:T(8,128)}, f32[1024,768]{1,0:T(8,128)}, bf16[12,768,256]{2,1,0:T(8,128)(2,1)}, bf16[12,256,768]{2,1,0:T(8,128)(2,1)}, bf16[6...) custom-call(bf16[4,256,768]{2,1,0:T(8,128)(2,1)} %x_in.1, ...), custom_call_target="tpu_custom_call" | custom-call | tf_op jit(solution)/shard_map/pallas_call | solution.py:547
  264.7 0.7 slice.23
  265.5 0.6 reshape.64
  266.1 0.7 slice.27
  266.8 1.6 slice_reduce_fusion
  268.4 0.0 copy-start
  268.4 0.6 reshape.65
  269.0 20.0 %shard_map.255 = (f32[768,3072]{1,0:T(8,128)}, f32[3072,768]{1,0:T(8,128)}, f32[768,2304]{1,0:T(8,128)}, f32[768,768]{1,0:T(8,128)}, bf16[1024,768]{1,0:T(8,128)(2,1)}, /*index=5*/bf16[1024,768]{1,0:T(8,128)(2,1)}) custom-call(bf16[12,768,256]{2,1,0:T(8,128)(2,1)} %get-tuple-element.28.du, bf16[12,256,768]{2,1,0:T(8,128)(2,1)} %get-tuple-element.29.dd, ...), custom_call_target="tpu_custom_call" | custom-call | tf_op jit(solution)/shard_map/pallas_call | solution.py:619
  289.0 0.0 copy-done
  289.0 0.6 copy.39
  (4 shorter events, 0.0 us)
Async XLA Ops:
  268.4 20.6 %copy-start = (f32[768]{0:T(1024)}, f32[768]{0:T(1024)S(1)}, u32[]{:S(2)}) copy-start(f32[768]{0:T(1024)S(1)} %get-tuple-element.76) | copy-start | bytes 9220

commit v5 on v4

--- a/solution.py
+++ b/solution.py
@@ -66,15 +66,18 @@
             self.dp_bits.append((mine, (self.seq, self.dp + (1 << b) * (1 - 2 * mine))))
         self.core, self.dp_bits = self.dp_bits[:1], self.dp_bits[1:]
 
-    def seq_first(self, turn):
-        mixed = []
-        for a, b in zip(self.seq_bits, self.seq_bits[::-1]):
-            mine = a[0] + turn * (b[0] - a[0])
-            mixed.append((mine, (a[1][0] + turn * (b[1][0] - a[1][0]), self.dp)))
-        return self.core + mixed + self.dp_bits
-
-    def seq_last(self):
-        return self.core + self.dp_bits + self.seq_bits
+    def order(self, name):
+        seq = self.seq_bits[::-1] if name.endswith("r") else self.seq_bits
+        name = name.rstrip("r")
+        first, then = (seq, self.dp_bits) if name[0] == "s" else (self.dp_bits, seq)
+        if len(name) == 1:
+            return self.core + first + then
+        n = min(len(first), len(then))
+        return self.core + [b for two in zip(first, then) for b in two] + first[n:] + then[n:]
+
+    def mix(self, a, b, turn):
+        return [(m + turn * (n - m), (p[0] + turn * (q[0] - p[0]), p[1] + turn * (q[1] - p[1])))
+                for (m, p), (n, q) in zip(self.order(a), self.order(b))]
 
     def peer(self, k):
         at = self.seq
@@ -82,9 +85,21 @@
             at = at + (1 << b) * lax.rem(k // (1 << b), 2) * (1 - 2 * mine)
         return at
 
+    def others(self, bits):
+        out = []
+        for c in range(1, 1 << len(bits)):
+            sq, dp = self.seq, self.dp
+            for j, (_, other) in enumerate(bits):
+                if c >> j & 1:
+                    sq, dp = sq + other[0] - self.seq, dp + other[1] - self.dp
+            out.append((sq, dp))
+        return out
+
     def enter(self):
         targets = [(self.peer(jnp.int32(k)), self.dp) for k in range(1, self.seq_n)]
-        targets += [bit[1] for bit in self.core + self.dp_bits]
+        targets += [bit[1] for bit in self.core]
+        for i in range(0, len(self.dp_bits), 2):
+            targets += self.others(self.dp_bits[i:i + 2])
         bar = pltpu.get_barrier_semaphore()
         for t in targets:
             pl.semaphore_signal(bar, inc=1, device_id=t, device_id_type=MESH)
@@ -145,17 +160,21 @@
         ops[k].start()
 
 
-ENDS_M = (1, 3, 5, 6, 7, 8, 9)
-ENDS_A = (1, 2, 3, 4, 5, 6, 7)
+ENDS_M = (1, 3, 5, 8, 10, 11, 12)
+ENDS_A = (1, 3, 5, 7, 9, 10, 11)
+UP, DOWN = ("s", "szr"), ("zr", "z")
+LEFT, RIGHT = ("s", "szr"), ("sr", "zs")
+GAPS_U, GAPS_D, GAPS_A = (2, 2, 3, 1, 1), (2, 3, 3, 3, 3), (2, 1, 2, 2)
+SPLIT_M = 3
 GAIN_A, SHIFT_A, GAIN_M, SHIFT_M, BIAS, BIAS_QKV, BIAS_UP = 0, 1, 2, 3, 4, 5, 8
 SMALL = 16
 
 
-def layer_kernel(sizes, x_in, g_in, cs_ref, vec_ref, bqkv_ref, wu_in, wd_in, wqkv_in, wo_in,
+def layer_kernel(sizes, x_in, g_in, cs_ref, vec_ref, wu_in, wd_in, wqkv_in, wo_in,
                  y_out, gm_out, du_out, dd_out, da_out, attn_out, ga_out, small_out,
-                 du, dd, land_u, land_d, da, land_x, land_y, xs, gs, css, small, land_s,
+                 du, dd, land_u, land_d, da, land_x, land_y, xs, gs, css, ob_own, small, land_s,
                  su, ru, sd, rd, sx, rx, sy, ry, s_u, r_u, s_d, r_d, s_x, r_x, s_y, r_y,
-                 s_in, r_in, s_c, r_c, s_out, r_out, s_s, r_s, s_l):
+                 s_in, r_in, s_c, r_c, s_o, r_o, s_out, r_out, s_s, r_s, s_l):
     place = Place(sizes)
     ns = place.seq_n
     _, L, W = x_in.shape
@@ -163,29 +182,29 @@
     n_chunk, _, C = du.shape
     pairs, R, _ = da.shape
     H2 = R // 2
-    hu = Halving(W, place.seq_last())
-    steps = len(hu.plan)
-    hx = Halving(H2, place.seq_first(0))
-    hy = Halving(H2, place.seq_first(1))
+    steps = len(place.order("s"))
     last_m = ENDS_M[steps - 1]
     last_a = ENDS_A[steps - 1]
     t_l = n_chunk
     t_p = t_l + 1
     t_h = t_p + ns
-    t_e = t_h + HEADS
-    t_g = t_e + 1
+    t_g = t_h + HEADS
     t_s = t_g + ns
+    t_e = t_s
     local = iter(range(100))
 
     place.enter()
 
     def mlp_pieces(p):
         at = lax.rem(p, 2) * (n_chunk // 2) + p // 2
-        hd = Halving(C, place.seq_first(lax.rem(p, 2)))
+        hu = Halving(W, place.mix(*UP, lax.rem(p, 2)))
+        hd = Halving(C, place.mix(*DOWN, lax.rem(p, 2)))
         return ((hu, (du.at[at], land_u.at[at], su.at[at], ru.at[at])),
                 (hd, (dd.at[at], land_d.at[at], sd.at[at], rd.at[at])))
 
     def attn_pieces(p):
+        hx = Halving(H2, place.mix(*LEFT, p // (pairs - 2)))
+        hy = Halving(H2, place.mix(*RIGHT, p // (pairs - 2)))
         return ((hx, (da.at[p, pl.ds(0, H2)], land_x.at[p], sx.at[p], rx.at[p])),
                 (hy, (da.at[p, pl.ds(H2, H2)], land_y.at[p], sy.at[p], ry.at[p])))
 
@@ -201,11 +220,11 @@
 
     plan = {}
 
-    def spread(at, gaps, srcs):
-        for h, src, dst, lo, send, recv in srcs:
+    def spread(at, srcs):
+        for h, src, dst, lo, send, recv, gaps in srcs:
             sem = s_l.at[next(local)]
             own = pltpu.make_async_copy(src.at[h.own(lo)], dst.at[h.own(lo)], sem)
-            view = dst.at[:, pl.ds(lo, H2)] if src.shape[1] == R and h in (hx, hy) else dst
+            view = dst.at[:, pl.ds(lo, H2)] if src.shape[1] == R else dst
             ops = h.chain(view, send, recv)
             t = at
             plan.setdefault(t, []).append(own.start)
@@ -216,30 +235,46 @@
                 t += gaps[min(k, len(gaps) - 1)]
 
     half = n_chunk // 2
-    third = half // 2
-    for gi in range(4):
-        turn, lo = gi // 2, (gi // 2) * half + (gi % 2) * third
-        made = 2 * ((gi % 2) * third + third - 1) + turn
-        grp = pl.ds(lo, third)
-        hd = Halving(C, place.seq_first(turn))
-        spread(made + last_m, (2, 2, 2, 1, 1), ((hu, du.at[grp], du_out.at[grp], 0, s_u.at[gi], r_u.at[gi]),
-                                                (hd, dd.at[grp], dd_out.at[grp], 0, s_d.at[gi], r_d.at[gi])))
-    for gi in range(2):
-        grp = pl.ds(gi * (pairs // 2), pairs // 2)
-        made = t_h + 2 * ((gi + 1) * (pairs // 2) - 1) + 1
-        spread(made + last_a, (1,), ((hx, da.at[grp], da_out.at[grp], 0, s_x.at[gi], r_x.at[gi]),
-                                     (hy, da.at[grp], da_out.at[grp], H2, s_y.at[gi], r_y.at[gi])))
-    for i in range(steps + 1):
-        def exchange(i=i):
-            def cp(i):
-                return pltpu.make_async_remote_copy(small, land_s.at[i], s_s.at[i], r_s.at[i],
-                                                    device_id=place.seq_last()[i][1], device_id_type=MESH)
-            if i > 0:
-                cp(i - 1).wait()
-                small[...] += land_s[i - 1]
-            if i < steps:
-                cp(i).start()
-        plan.setdefault(t_s + i, []).append(exchange)
+    third = half // SPLIT_M
+    for gi in range(2 * SPLIT_M):
+        turn, lo = gi // SPLIT_M, (gi % SPLIT_M) * third
+        made = 2 * (lo + third - 1) + turn
+        grp = pl.ds(turn * half + lo, third)
+        hu = Halving(W, place.order(UP[turn]))
+        hd = Halving(C, place.order(DOWN[turn]))
+        spread(made + last_m, ((hu, du.at[grp], du_out.at[grp], 0, s_u.at[gi], r_u.at[gi], GAPS_U),
+                               (hd, dd.at[grp], dd_out.at[grp], 0, s_d.at[gi], r_d.at[gi], GAPS_D)))
+    for gi in range(3):
+        grp = pl.ds(gi * (pairs // 3), pairs // 3)
+        made = t_h + 2 * ((gi + 1) * (pairs // 3) - 1) + 1
+        hx = Halving(H2, place.order(LEFT[gi // 2]))
+        hy = Halving(H2, place.order(RIGHT[gi // 2]))
+        spread(made + last_a, ((hx, da.at[grp], da_out.at[grp], 0, s_x.at[gi], r_x.at[gi], GAPS_A),
+                               (hy, da.at[grp], da_out.at[grp], H2, s_y.at[gi], r_y.at[gi], GAPS_A)))
+    rounds = [place.core] + [bits[i:i + 2] for bits in (place.seq_bits, place.dp_bits) for i in range(0, len(bits), 2)]
+
+    def small_copies(i):
+        return [pltpu.make_async_remote_copy(small, land_s.at[i, c + 1], s_s.at[i, c + 1], r_s.at[i, c + 1],
+                                             device_id=to, device_id_type=MESH)
+                for c, to in enumerate(place.others(rounds[i]))]
+
+    def small_round(i):
+        if i > 0:
+            bits = rounds[i - 1]
+            for m in small_copies(i - 1):
+                m.wait()
+            parts = {0: small[...]}
+            parts.update({c: land_s[i - 1, c] for c in range(1, 1 << len(bits))})
+            for j in range(len(bits)):
+                parts = {c: parts[c] + parts[c | 1 << j] for c in parts if not c >> j & 1}
+            small[...] = parts[0]
+        if i < len(rounds):
+            for m in small_copies(i):
+                m.start()
+
+    assert all(len(bits) <= 2 for bits in rounds)
+    for i in range(len(rounds) + 1):
+        plan.setdefault(t_s + i, []).append(functools.partial(small_round, i))
     end = max(plan) + 1
 
     def tick(t, lo, hi):
@@ -371,7 +406,7 @@
         for m in once:
             m.wait()
 
-    def attention(wqkv, wo, wT, xaT, qkvT, kn, vn, dOT, obT, attn, ga):
+    def attention(wqkv, wo, wT, xaT, qkvT, kn, vn, dOT, obT, obn, attn, ga):
         loads = [pltpu.make_async_copy(src, dst, s_l.at[next(local)]) for src, dst in ((wqkv_in, wqkv), (wo_in, wo))]
         for m in loads:
             m.start()
@@ -384,14 +419,21 @@
         keep = sub <= lane
         rowid = lax.broadcasted_iota(jnp.int32, (128, 1), 0)
 
-        def back_copy(a, k, src, dst):
+        def ga_copy(k):
             to = place.peer(k)
             return pltpu.make_async_remote_copy(
-                src.at[pl.ds(mul8(to * L), L)], dst.at[place.seq], s_out.at[a, k], r_out.at[a, k],
+                ga.at[pl.ds(mul8(to * L), L)], ga_out.at[place.seq], s_out.at[k], r_out.at[k],
                 device_id=(to, place.dp), device_id_type=MESH)
 
-        def own_copy(a, src, dst):
-            return pltpu.make_async_copy(src.at[me], dst.at[place.seq], s_out.at[a, 0])
+        ga_own = pltpu.make_async_copy(ga.at[me], ga_out.at[place.seq], s_out.at[0])
+        attn_copy = pltpu.make_async_copy(attn, attn_out, r_out.at[0])
+
+        def ob_copy(k, pair):
+            to = place.peer(jnp.int32(k))
+            cols = pl.ds(pl.multiple_of(pair * 128, 128), 128)
+            return pltpu.make_async_remote_copy(
+                obn.at[pl.ds(mul8(to * L), L), cols], ob_own.at[place.seq, :, cols], s_o.at[k, pair], r_o.at[k, pair],
+                device_id=(to, place.dp), device_id_type=MESH)
 
         def unrotate(d, b):
             cos = css[b, :8, :]
@@ -400,8 +442,6 @@
 
         @pl.loop(t_p, end)
         def _(t):
-            tick(t, t_p, end)
-
             @pl.when(t < t_h)
             def _():
                 b = t - t_p
@@ -413,7 +453,8 @@
                 sin = css[b, 8:, :]
                 for j in range(9):
                     at = slice(j * 256, (j + 1) * 256)
-                    m = nt(wT[at, :], xa) + bqkv_ref[at, :]
+                    bq = vec_ref[5 + j // 3:6 + j // 3, (j % 3) * 256:(j % 3 + 1) * 256]
+                    m = nt(wT[at, :], xa) + jnp.broadcast_to(bq, (8, 256)).T[:, :1]
                     if j < 6:
                         parts = []
                         for h in range(4):
@@ -433,7 +474,7 @@
                     at = slice(j * 256, (j + 1) * 256)
                     dOT[at, rows] = nt(wo[at, :], g).astype(BF)
 
-            @pl.when((t >= t_h) & (t < t_e))
+            @pl.when((t >= t_h) & (t < t_g))
             def _():
                 head = t - t_h
                 pair = head // 2
@@ -476,26 +517,23 @@
                     qkvT[kr, sl] = unrotate(dk[b], b).astype(BF)
                     qkvT[vr, sl] = dv[b].astype(BF)
 
-                @pl.when(lax.rem(head, 2) == 1)
-                def _():
-                    dm = jnp.concatenate([qkvT[cols, :], qkvT[pl.ds(W + r0, 128), :], qkvT[pl.ds(2 * W + r0, 128), :]], axis=0)
-                    da[pair, :384, :] = nt(dm, xaT[...]).astype(BF)
-                    da[pair, 384:, :] = nn(obT[cols, :], gs[...]).astype(BF)
-                    begin(attn_pieces(pair))
-                    db = nt(jnp.ones((8, T), BF), dm)
-                    for i in range(3):
-                        small[BIAS_QKV + i:BIAS_QKV + i + 1, cols] = db[0:1, i * 128:(i + 1) * 128]
-
-            @pl.when(t == t_e)
-            def _():
-                for k in range(ns - 1, -1, -1):
-                    b = place.peer(jnp.int32(k))
-                    rows = pl.ds(pl.multiple_of(b * L, L), L)
-                    attn[rows, :] = nn(obT[:, rows].T, wo[...]).astype(BF)
-                    if k > 0:
-                        back_copy(0, k, attn, attn_out).start()
-                    else:
-                        own_copy(0, attn, attn_out).start()
+            tick(t, t_p, end)
+
+            @pl.when((t >= t_h) & (t < t_g) & (lax.rem(t - t_h + HEADS, 2) == 1))
+            def _():
+                pair = (t - t_h) // 2
+                r0 = pl.multiple_of(pair * 128, 128)
+                cols = pl.ds(r0, 128)
+                obn[:, cols] = obT[cols, :].T
+                for k in range(ns - 1, 0, -1):
+                    ob_copy(k, pair).start()
+                dm = jnp.concatenate([qkvT[cols, :], qkvT[pl.ds(W + r0, 128), :], qkvT[pl.ds(2 * W + r0, 128), :]], axis=0)
+                da[pair, :384, :] = nt(dm, xaT[...]).astype(BF)
+                da[pair, 384:, :] = nn(obT[cols, :], gs[...]).astype(BF)
+                begin(attn_pieces(pair))
+                db = nt(jnp.ones((8, T), BF), dm)
+                for i in range(3):
+                    small[BIAS_QKV + i:BIAS_QKV + i + 1, cols] = db[0:1, i * 128:(i + 1) * 128]
 
             @pl.when((t >= t_g) & (t < t_s))
             def _():
@@ -510,16 +548,35 @@
 
                 @pl.when(k > 0)
                 def _():
-                    back_copy(1, k, ga, ga_out).start()
+                    ga_copy(k).start()
 
                 @pl.when(k == 0)
                 def _():
-                    own_copy(1, ga, ga_out).start()
-
-        for a, (src, dst) in enumerate(((attn, attn_out), (ga, ga_out))):
-            for k in range(ns - 1, 0, -1):
-                back_copy(a, jnp.int32(k), src, dst).wait()
-            own_copy(a, src, dst).wait()
+                    ga_own.start()
+
+            @pl.when(t == t_e)
+            def _():
+                for k in range(1, ns):
+                    for i in range(pairs):
+                        ob_copy(k, i).wait()
+
+            @pl.when((t >= t_e) & (t < t_e + ns))
+            def _():
+                b = t - t_e
+
+                @pl.when(b == place.seq)
+                def _():
+                    ob_own[b] = obn[me, :]
+                attn[b] = nn(ob_own[b], wo[...]).astype(BF)
+
+            @pl.when(t == t_e + ns - 1)
+            def _():
+                attn_copy.start()
+
+        for k in range(ns - 1, 0, -1):
+            ga_copy(jnp.int32(k)).wait()
+        ga_own.wait()
+        attn_copy.wait()
         small_out[...] = small[...]
 
     V = pltpu.VMEM
@@ -527,10 +584,10 @@
     pl.run_scoped(feed_forward, V((W, FF), BF), V((FF, W), BF), V((ns, L, W), BF), V((ns, L, W), BF), V((T, W), BF),
                   V((W, T), BF), V((T, W), F32), V((T, W), F32), V((T, C), BF), V((T, C), BF))
     pl.run_scoped(attention, V((W, 3 * W), BF), V((W, W), BF), V((3 * W, W), BF), V((W, T), BF), V((3 * W, T), BF), V((T, W), BF), V((T, W), BF),
-                  V((W, T), BF), V((W, T), BF), V((T, W), BF), V((T, W), BF))
-
-
-def layer_call(sizes, x, g, cs, vec, bqkv, wu, wd, wqkv, wo):
+                  V((W, T), BF), V((W, T), BF), V((T, W), BF), V((ns, L, W), BF), V((T, W), BF))
+
+
+def layer_call(sizes, x, g, cs, vec, wu, wd, wqkv, wo):
     ns, L, W = x.shape
     T = ns * L
     FF = wu.shape[1]
@@ -548,14 +605,14 @@
         functools.partial(layer_kernel, sizes),
         out_shape=(S((T, W), F32), S((T, W), F32), S((n, W, C), BF), S((n, C, W), BF), S((pairs, R, W), BF),
                    S((ns, L, W), BF), S((ns, L, W), BF), S((SMALL, W), F32)),
-        in_specs=[hbm, hbm, vm, vm, vm, hbm, hbm, hbm, hbm], out_specs=(hbm,) * 7 + (vm,),
+        in_specs=[hbm, hbm, vm, vm, hbm, hbm, hbm, hbm], out_specs=(hbm,) * 7 + (vm,),
         scratch_shapes=[V((n, W, C), BF), V((n, C, W), BF), V((n, Halving.land(W, steps), C), BF),
                         V((n, Halving.land(C, steps), W), BF), V((pairs, R, W), BF), V((pairs, la, W), BF),
-                        V((pairs, la, W), BF), V((T, W), BF), V((T, W), BF), V(cs.shape, F32), V((SMALL, W), F32), V((steps, SMALL, W), F32)]
-        + [dma((n, steps))] * 4 + [dma((pairs, steps))] * 4 + [dma((4, steps))] * 4 + [dma((2, steps))] * 4
-        + [dma((2, ns, MOVES))] * 2 + [dma((ns,))] * 2 + [dma((2, ns))] * 2 + [dma((steps,))] * 2 + [dma((32,))],
-        compiler_params=pltpu.CompilerParams(vmem_limit_bytes=62 << 20, collective_id=0, has_side_effects=True),
-    )(x, g, cs, vec, bqkv, wu, wd, wqkv, wo)
+                        V((pairs, la, W), BF), V((T, W), BF), V((T, W), BF), V(cs.shape, F32), V((ns, L, W), BF), V((SMALL, W), F32), V((steps, 4, SMALL, W), F32)]
+        + [dma((n, steps))] * 4 + [dma((pairs, steps))] * 4 + [dma((2 * SPLIT_M, steps))] * 4 + [dma((3, steps))] * 4
+        + [dma((2, ns, MOVES))] * 2 + [dma((ns,))] * 2 + [dma((ns, pairs))] * 2 + [dma((ns,))] * 2 + [dma((steps, 4))] * 2 + [dma((48,))],
+        compiler_params=pltpu.CompilerParams(vmem_limit_bytes=63 << 20, collective_id=0, has_side_effects=True),
+    )(x, g, cs, vec, wu, wd, wqkv, wo)
 
 
 def finish_kernel(du, dd, da, y, gm, attn, ga, dwu, dwd, dwqkv, ddw, out, grad,
@@ -623,7 +680,7 @@
         scratch_shapes=[V(du.shape, BF), V(dd.shape, BF), V(da.shape, BF), V((W, FF), F32), V((FF, W), F32),
                         V((W, 3 * W), F32), V((W, W), F32), V((tokens, W), F32), V((tokens, W), F32),
                         V((tokens, W), BF), V((tokens, W), BF), dma((2 * n + pairs + 4,)), dma((2 * n + 4 * pairs + 2,))],
-        compiler_params=pltpu.CompilerParams(vmem_limit_bytes=62 << 20),
+        compiler_params=pltpu.CompilerParams(vmem_limit_bytes=63 << 20),
     )(du, dd, da, y, gm, attn, ga)
 
 
@@ -636,10 +693,10 @@
     angles = freqs[:, None] * positions.astype(F32)[:, None, :]
     cs = jnp.concatenate([jnp.cos(angles), jnp.sin(angles)], axis=1)
     zero = jnp.zeros((W,), F32)
-    vec = jnp.concatenate([attn_gain, attn_shift, mlp_gain, mlp_shift, dense_bias + down_bias, zero, zero, zero,
+    vec = jnp.concatenate([attn_gain, attn_shift, mlp_gain, mlp_shift, dense_bias + down_bias, qkv_bias,
                            up_bias, zero, zero, zero, zero]).reshape(16, W)
     y, gm, du, dd, da, attn, ga, small = layer_call(
-        sizes, hidden_in, out_grad, cs, vec, qkv_bias.reshape(-1, 1), up_weight, down_weight, qkv_weight, dense_weight)
+        sizes, hidden_in, out_grad, cs, vec, up_weight, down_weight, qkv_weight, dense_weight)
     dwu, dwd, dwqkv, ddw, layer_out, input_grad = finish_call(du, dd, da, y, gm, attn.reshape(-1, W), ga.reshape(-1, W))
     db = small[BIAS]
     return (layer_out.reshape(hidden_in.shape), input_grad.reshape(hidden_in.shape), small[GAIN_A], small[SHIFT_A], dwqkv,

time: 290 us -> 252 us (0.87)
  Pallas kernels: 276 us -> 239 us
    pallas_call x1, Pallas kernels: 256 us -> 219 us  [layer_call(): pl.pallas_call(functools.partial(layer_kernel, sizes), out_shape=(S((T, W...]
where the time goes in v5:
time: 252 us
  Pallas kernels  239 us (95%)
  local copies, waits for them, and re-layouts  9.69 us (4%)
    pallas_call x1, Pallas kernels, layer_call(): pl.pallas_call(functools.partial(layer_kernel, sizes), out_shape=(S((T, W...  219 us
    pallas_call x1, Pallas kernels, finish_call(): pl.pallas_call(finish_kernel, out_shape=(S((W, FF), F32), S((FF, W), F32)...  20 us

profile of v5, /device:TPU:0, one launch (start us, length us, event | category | flops | bytes accessed | tf_op | source)
XLA Modules:
  0.0 251.7 jit_solution(17149149747333643223)
XLA Ops:
  0.7 0.7 convert_element_type.3
  1.4 0.7 constant_dynamic-update-slice_fusion.6
  2.0 0.7 constant_dynamic-update-slice_fusion.5
  2.7 0.7 constant_dynamic-update-slice_fusion.4
  3.4 0.7 constant_dynamic-update-slice_fusion.3
  4.1 0.7 constant_dynamic-update-slice_fusion.2
  4.8 0.7 constant_dynamic-update-slice_fusion.1
  5.5 0.7 constant_dynamic-update-slice_fusion
  6.3 0.6 reshape.55.vec_ref
  6.9 0.2 multiply_cosine_fusion
  7.1 0.6 pad_maximum_fusion.cs_ref
  7.7 219.1 %shard_map.254 = (f32[1024,768]{1,0:T(8,128)}, f32[1024,768]{1,0:T(8,128)}, bf16[12,768,256]{2,1,0:T(8,128)(2,1)}, bf16[12,256,768]{2,1,0:T(8,128)(2,1)}, bf16[6...) custom-call(bf16[4,256,768]{2,1,0:T(8,128)(2,1)} %x_in.1, ...), custom_call_target="tpu_custom_call" | custom-call | tf_op jit(solution)/shard_map/pallas_call | solution.py:604
  226.8 0.7 slice.23
  227.6 0.6 reshape.60
  228.2 0.7 slice.27
  228.9 1.6 slice_reduce_fusion
  230.5 0.0 copy-start
  230.5 0.6 reshape.61
  231.1 20.0 %shard_map.255 = (f32[768,3072]{1,0:T(8,128)}, f32[3072,768]{1,0:T(8,128)}, f32[768,2304]{1,0:T(8,128)}, f32[768,768]{1,0:T(8,128)}, bf16[1024,768]{1,0:T(8,128)(2,1)}, /*index=5*/bf16[1024,768]{1,0:T(8,128)(2,1)}) custom-call(bf16[12,768,256]{2,1,0:T(8,128)(2,1)} %get-tuple-element.28.du, bf16[12,256,768]{2,1,0:T(8,128)(2,1)} %get-tuple-element.29.dd, ...), custom_call_target="tpu_custom_call" | custom-call | tf_op jit(solution)/shard_map/pallas_call | solution.py:676
  251.1 0.0 copy-done
  251.1 0.6 copy.38
  (3 shorter events, 0.0 us)
Async XLA Ops:
  230.5 20.6 %copy-start = (f32[768]{0:T(1024)}, f32[768]{0:T(1024)S(1)}, u32[]{:S(2)}) copy-start(f32[768]{0:T(1024)S(1)} %get-tuple-element.76) | copy-start | bytes 9220

commit v6 on v5

--- a/solution.py
+++ b/solution.py
@@ -75,9 +75,12 @@
         n = min(len(first), len(then))
         return self.core + [b for two in zip(first, then) for b in two] + first[n:] + then[n:]
 
-    def mix(self, a, b, turn):
-        return [(m + turn * (n - m), (p[0] + turn * (q[0] - p[0]), p[1] + turn * (q[1] - p[1])))
-                for (m, p), (n, q) in zip(self.order(a), self.order(b))]
+    def mix(self, names, turn):
+        at = [jnp.where(turn == i, 1, 0) for i in range(len(names))]
+        orders = [self.order(name) for name in names]
+        return [(sum(w * o[i][0] for w, o in zip(at, orders)),
+                 (sum(w * o[i][1][0] for w, o in zip(at, orders)), sum(w * o[i][1][1] for w, o in zip(at, orders))))
+                for i in range(len(orders[0]))]
 
     def peer(self, k):
         at = self.seq
@@ -95,15 +98,20 @@
             out.append((sq, dp))
         return out
 
-    def enter(self):
+    def targets(self):
         targets = [(self.peer(jnp.int32(k)), self.dp) for k in range(1, self.seq_n)]
         targets += [bit[1] for bit in self.core]
         for i in range(0, len(self.dp_bits), 2):
             targets += self.others(self.dp_bits[i:i + 2])
+        return targets
+
+    def signal(self):
         bar = pltpu.get_barrier_semaphore()
-        for t in targets:
+        for t in self.targets():
             pl.semaphore_signal(bar, inc=1, device_id=t, device_id_type=MESH)
-        pl.semaphore_wait(bar, len(targets))
+
+    def enter(self):
+        pl.semaphore_wait(pltpu.get_barrier_semaphore(), len(self.targets()))
 
 
 class Halving:
@@ -137,7 +145,7 @@
         self.copy(i, buf, land, send, recv).wait()
         _, _, part, keep, _, off = self.plan[i]
         rows = pl.ds(mul8(keep), part)
-        buf[rows] = (buf[rows].astype(F32) + land[pl.ds(off, part)].astype(F32)).astype(buf.dtype)
+        buf[rows] = buf[rows] + land[pl.ds(off, part)]
 
     def own(self, lo=0):
         return (slice(None), pl.ds(mul8(lo + self.lo), self.n))
@@ -160,19 +168,22 @@
         ops[k].start()
 
 
-ENDS_M = (1, 3, 5, 8, 10, 11, 12)
-ENDS_A = (1, 3, 5, 7, 9, 10, 11)
-UP, DOWN = ("s", "szr"), ("zr", "z")
-LEFT, RIGHT = ("s", "szr"), ("sr", "zs")
-GAPS_U, GAPS_D, GAPS_A = (2, 2, 3, 1, 1), (2, 3, 3, 3, 3), (2, 1, 2, 2)
+ENDS_M = (2, 5, 7, 9, 11, 12, 13)
+ENDS_A = (2, 3, 4, 5, 7, 8, 9)
+ENDS_L = (1, 2, 3, 4, 5, 6, 7)
+UP, DOWN = ("sz", "zsr"), ("zsr", "sr")
+LEFT, RIGHT = ("szr", "s", "sz"), ("sz", "sr", "szr")
+GAPS_U, GAPS_D, GAPS_A, GAPS_L = (2, 3, 3, 3, 2), (2, 2, 2, 1, 1), (1, 2, 2, 1), (1,)
+WAIT_A = (1, 0, 0)
+GA_SENDS = (0, 6, 7)
 SPLIT_M = 3
 GAIN_A, SHIFT_A, GAIN_M, SHIFT_M, BIAS, BIAS_QKV, BIAS_UP = 0, 1, 2, 3, 4, 5, 8
 SMALL = 16
 
 
-def layer_kernel(sizes, x_in, g_in, cs_ref, vec_ref, wu_in, wd_in, wqkv_in, wo_in,
+def layer_kernel(sizes, x_in, g_in, cs_ref, ga_v, sa_v, gm_v, sm_v, bo_v, bd_v, bq_v, bu_v, wu_in, wd_in, wqkv_in, wo_in,
                  y_out, gm_out, du_out, dd_out, da_out, attn_out, ga_out, small_out,
-                 du, dd, land_u, land_d, da, land_x, land_y, xs, gs, css, ob_own, small, land_s,
+                 du, dd, land_u, land_d, da, land_x, land_y, xs, gs, css, ob_own, vec_ref, small, land_s,
                  su, ru, sd, rd, sx, rx, sy, ry, s_u, r_u, s_d, r_d, s_x, r_x, s_y, r_y,
                  s_in, r_in, s_c, r_c, s_o, r_o, s_out, r_out, s_s, r_s, s_l):
     place = Place(sizes)
@@ -184,7 +195,6 @@
     H2 = R // 2
     steps = len(place.order("s"))
     last_m = ENDS_M[steps - 1]
-    last_a = ENDS_A[steps - 1]
     t_l = n_chunk
     t_p = t_l + 1
     t_h = t_p + ns
@@ -192,19 +202,18 @@
     t_s = t_g + ns
     t_e = t_s
     local = iter(range(100))
-
-    place.enter()
+    place.signal()
 
     def mlp_pieces(p):
         at = lax.rem(p, 2) * (n_chunk // 2) + p // 2
-        hu = Halving(W, place.mix(*UP, lax.rem(p, 2)))
-        hd = Halving(C, place.mix(*DOWN, lax.rem(p, 2)))
+        hu = Halving(W, place.mix(UP, lax.rem(p, 2)))
+        hd = Halving(C, place.mix(DOWN, lax.rem(p, 2)))
         return ((hu, (du.at[at], land_u.at[at], su.at[at], ru.at[at])),
                 (hd, (dd.at[at], land_d.at[at], sd.at[at], rd.at[at])))
 
     def attn_pieces(p):
-        hx = Halving(H2, place.mix(*LEFT, p // (pairs - 2)))
-        hy = Halving(H2, place.mix(*RIGHT, p // (pairs - 2)))
+        hx = Halving(H2, place.mix(LEFT, p // 2))
+        hy = Halving(H2, place.mix(RIGHT, p // 2))
         return ((hx, (da.at[p, pl.ds(0, H2)], land_x.at[p], sx.at[p], rx.at[p])),
                 (hy, (da.at[p, pl.ds(H2, H2)], land_y.at[p], sy.at[p], ry.at[p])))
 
@@ -245,12 +254,15 @@
         spread(made + last_m, ((hu, du.at[grp], du_out.at[grp], 0, s_u.at[gi], r_u.at[gi], GAPS_U),
                                (hd, dd.at[grp], dd_out.at[grp], 0, s_d.at[gi], r_d.at[gi], GAPS_D)))
     for gi in range(3):
-        grp = pl.ds(gi * (pairs // 3), pairs // 3)
-        made = t_h + 2 * ((gi + 1) * (pairs // 3) - 1) + 1
-        hx = Halving(H2, place.order(LEFT[gi // 2]))
-        hy = Halving(H2, place.order(RIGHT[gi // 2]))
-        spread(made + last_a, ((hx, da.at[grp], da_out.at[grp], 0, s_x.at[gi], r_x.at[gi], GAPS_A),
-                               (hy, da.at[grp], da_out.at[grp], H2, s_y.at[gi], r_y.at[gi], GAPS_A)))
+        grp = pl.ds(2 * gi, 2)
+        made = t_h + 4 * gi + 3
+        late = gi == 2
+        hx = Halving(H2, place.order(LEFT[gi]))
+        hy = Halving(H2, place.order(RIGHT[gi]))
+        gaps = GAPS_L if late else GAPS_A
+        spread(made + (ENDS_L if late else ENDS_A)[steps - 1] + WAIT_A[gi],
+               ((hx, da.at[grp], da_out.at[grp], 0, s_x.at[gi], r_x.at[gi], gaps),
+                (hy, da.at[grp], da_out.at[grp], H2, s_y.at[gi], r_y.at[gi], gaps)))
     rounds = [place.core] + [bits[i:i + 2] for bits in (place.seq_bits, place.dp_bits) for i in range(0, len(bits), 2)]
 
     def small_copies(i):
@@ -275,7 +287,8 @@
     assert all(len(bits) <= 2 for bits in rounds)
     for i in range(len(rounds) + 1):
         plan.setdefault(t_s + i, []).append(functools.partial(small_round, i))
-    end = max(plan) + 1
+    end = max(max(plan), t_g + max(GA_SENDS)) + 1
+    assert ns == len(GA_SENDS) + 1 and pairs == 6
 
     def tick(t, lo, hi):
         for s in range(steps):
@@ -286,11 +299,12 @@
                 halve(mlp_pieces(p), s)
         if hi > t_h:
             for s in range(steps):
-                q = t - t_h - 1 - ENDS_A[s]
-
-                @pl.when((q >= 0) & (q < 2 * pairs) & (lax.rem(q + 2 * pairs, 2) == 0))
-                def _():
-                    halve(attn_pieces(q // 2), s)
+                for ends, first, end in ((ENDS_A, 0, 2 * pairs - 4), (ENDS_L, 2 * pairs - 4, 2 * pairs)):
+                    q = t - t_h - 1 - ends[s]
+
+                    @pl.when((q >= first) & (q < end) & (lax.rem(q + 2 * pairs, 2) == 0))
+                    def _():
+                        halve(attn_pieces(q // 2), s)
         for at in range(lo, hi):
             if at in plan:
                 @pl.when(t == at)
@@ -319,14 +333,25 @@
     for src, dst in ((x_in, xs.at[me]), (g_in, gs.at[me]), (cs_ref, css.at[place.seq])):
         once.append(pltpu.make_async_copy(src.at[place.seq], dst, s_l.at[next(local)]))
 
+
     def row(i):
         return vec_ref[i:i + 1, :]
 
     def feed_forward(wu_ref, wd_ref, x_ref, g_ref, xm, xmT, dxm, y, a_s, dh_s):
+        head, rest = pl.ds(0, C), pl.ds(C, FF - C)
         loads = [pltpu.make_async_copy(src, dst, s_l.at[next(local)])
-                 for src, dst in ((x_in, x_ref), (g_in, g_ref), (wu_in, wu_ref), (wd_in, wd_ref))]
-        for m in loads + once + moves(0):
+                 for src, dst in ((x_in, x_ref), (g_in, g_ref), (wu_in.at[:, head], wu_ref.at[:, head]),
+                                  (wd_in.at[head], wd_ref.at[head]), (wu_in.at[:, rest], wu_ref.at[:, rest]),
+                                  (wd_in.at[rest], wd_ref.at[rest]))]
+        for m in loads:
             m.start()
+        for i, v in enumerate((ga_v, sa_v, gm_v, sm_v)):
+            vec_ref[i:i + 1, :] = v[...].reshape(1, W)
+        vec_ref[4:5, :] = (bo_v[...] + bd_v[...]).reshape(1, W)
+        for i in range(3):
+            vec_ref[5 + i:6 + i, :] = bq_v[i * W:(i + 1) * W].reshape(1, W)
+        for i in range(FF // W):
+            vec_ref[8 + i:9 + i, :] = bu_v[i * W:(i + 1) * W].reshape(1, W)
         loads[0].wait()
         small[...] = jnp.zeros_like(small)
         for b in range(ns):
@@ -338,7 +363,10 @@
             xmT[:, rows] = v.T
             y[rows, :] = x + row(4)
         dxm[...] = jnp.zeros_like(dxm)
-        for m in loads[1:]:
+        place.enter()
+        for m in once + moves(0):
+            m.start()
+        for m in loads[1:4]:
             m.wait()
 
         @pl.loop(0, t_l + 1)
@@ -365,6 +393,11 @@
                     dh_s[rows, :] = dh
                     dbu += jnp.sum(dh.astype(F32), axis=0, keepdims=True)
                 small[pl.ds(BIAS_UP + t // 3, 1), pl.ds(pl.multiple_of(lax.rem(t, 3) * C, C), C)] = dbu
+
+            @pl.when(t == 0)
+            def _():
+                for m in loads[4:]:
+                    m.wait()
 
             tick(t, 0, t_l + 1)
 
@@ -406,14 +439,15 @@
         for m in once:
             m.wait()
 
-    def attention(wqkv, wo, wT, xaT, qkvT, kn, vn, dOT, obT, obn, attn, ga):
+    def attention(wqkv, wo, wT, xaT, qkvT, kn, vn, dOT, obT, obn):
+        attn, ga = kn, vn
         loads = [pltpu.make_async_copy(src, dst, s_l.at[next(local)]) for src, dst in ((wqkv_in, wqkv), (wo_in, wo))]
         for m in loads:
             m.start()
-        for m in loads:
-            m.wait()
+        loads[0].wait()
         for j in range(9):
             wT[j * 256:(j + 1) * 256, :] = wqkv[:, j * 256:(j + 1) * 256].T
+        loads[1].wait()
         sub = lax.broadcasted_iota(jnp.int32, (L, L), 0)
         lane = lax.broadcasted_iota(jnp.int32, (L, L), 1)
         keep = sub <= lane
@@ -517,7 +551,26 @@
                     qkvT[kr, sl] = unrotate(dk[b], b).astype(BF)
                     qkvT[vr, sl] = dv[b].astype(BF)
 
+            @pl.when((t >= t_g) & (t < t_s))
+            def _():
+                k = t_s - 1 - t
+                b = place.peer(k)
+                rows = pl.ds(pl.multiple_of(b * L, L), L)
+                dxa = nn(wqkv[...], qkvT[:, rows]).T
+                xhat, rstd = norm_parts(xs[rows, :].astype(F32))
+                small[GAIN_A:GAIN_A + 1, :] += jnp.sum(dxa * xhat, axis=0, keepdims=True)
+                small[SHIFT_A:SHIFT_A + 1, :] += jnp.sum(dxa, axis=0, keepdims=True)
+                ga[rows, :] = norm_back(dxa * row(0), xhat, rstd).astype(BF)
+
+                @pl.when(k == 0)
+                def _():
+                    ga_own.start()
+
             tick(t, t_p, end)
+            for i, later in enumerate(GA_SENDS):
+                @pl.when(t == t_g + later)
+                def _():
+                    ga_copy(jnp.int32(ns - 1 - i)).start()
 
             @pl.when((t >= t_h) & (t < t_g) & (lax.rem(t - t_h + HEADS, 2) == 1))
             def _():
@@ -535,25 +588,6 @@
                 for i in range(3):
                     small[BIAS_QKV + i:BIAS_QKV + i + 1, cols] = db[0:1, i * 128:(i + 1) * 128]
 
-            @pl.when((t >= t_g) & (t < t_s))
-            def _():
-                k = t_s - 1 - t
-                b = place.peer(k)
-                rows = pl.ds(pl.multiple_of(b * L, L), L)
-                dxa = nn(wqkv[...], qkvT[:, rows]).T
-                xhat, rstd = norm_parts(xs[rows, :].astype(F32))
-                small[GAIN_A:GAIN_A + 1, :] += jnp.sum(dxa * xhat, axis=0, keepdims=True)
-                small[SHIFT_A:SHIFT_A + 1, :] += jnp.sum(dxa, axis=0, keepdims=True)
-                ga[rows, :] = norm_back(dxa * row(0), xhat, rstd).astype(BF)
-
-                @pl.when(k > 0)
-                def _():
-                    ga_copy(k).start()
-
-                @pl.when(k == 0)
-                def _():
-                    ga_own.start()
-
             @pl.when(t == t_e)
             def _():
                 for k in range(1, ns):
@@ -567,7 +601,7 @@
                 @pl.when(b == place.seq)
                 def _():
                     ob_own[b] = obn[me, :]
-                attn[b] = nn(ob_own[b], wo[...]).astype(BF)
+                attn[pl.ds(pl.multiple_of(b * L, L), L), :] = nn(ob_own[b], wo[...]).astype(BF)
 
             @pl.when(t == t_e + ns - 1)
             def _():
@@ -584,10 +618,10 @@
     pl.run_scoped(feed_forward, V((W, FF), BF), V((FF, W), BF), V((ns, L, W), BF), V((ns, L, W), BF), V((T, W), BF),
                   V((W, T), BF), V((T, W), F32), V((T, W), F32), V((T, C), BF), V((T, C), BF))
     pl.run_scoped(attention, V((W, 3 * W), BF), V((W, W), BF), V((3 * W, W), BF), V((W, T), BF), V((3 * W, T), BF), V((T, W), BF), V((T, W), BF),
-                  V((W, T), BF), V((W, T), BF), V((T, W), BF), V((ns, L, W), BF), V((T, W), BF))
-
-
-def layer_call(sizes, x, g, cs, vec, wu, wd, wqkv, wo):
+                  V((W, T), BF), V((W, T), BF), V((T, W), BF))
+
+
+def layer_call(sizes, x, g, cs, vecs, wu, wd, wqkv, wo):
     ns, L, W = x.shape
     T = ns * L
     FF = wu.shape[1]
@@ -604,18 +638,18 @@
     return pl.pallas_call(
         functools.partial(layer_kernel, sizes),
         out_shape=(S((T, W), F32), S((T, W), F32), S((n, W, C), BF), S((n, C, W), BF), S((pairs, R, W), BF),
-                   S((ns, L, W), BF), S((ns, L, W), BF), S((SMALL, W), F32)),
-        in_specs=[hbm, hbm, vm, vm, hbm, hbm, hbm, hbm], out_specs=(hbm,) * 7 + (vm,),
+                   S((T, W), BF), S((ns, L, W), BF), S((SMALL, W), F32)),
+        in_specs=[hbm, hbm, vm] + [vm] * 8 + [hbm] * 4, out_specs=(hbm,) * 7 + (vm,),
         scratch_shapes=[V((n, W, C), BF), V((n, C, W), BF), V((n, Halving.land(W, steps), C), BF),
                         V((n, Halving.land(C, steps), W), BF), V((pairs, R, W), BF), V((pairs, la, W), BF),
-                        V((pairs, la, W), BF), V((T, W), BF), V((T, W), BF), V(cs.shape, F32), V((ns, L, W), BF), V((SMALL, W), F32), V((steps, 4, SMALL, W), F32)]
+                        V((pairs, la, W), BF), V((T, W), BF), V((T, W), BF), V(cs.shape, F32), V((ns, L, W), BF), V((SMALL, W), F32), V((SMALL, W), F32), V((steps, 4, SMALL, W), F32)]
         + [dma((n, steps))] * 4 + [dma((pairs, steps))] * 4 + [dma((2 * SPLIT_M, steps))] * 4 + [dma((3, steps))] * 4
         + [dma((2, ns, MOVES))] * 2 + [dma((ns,))] * 2 + [dma((ns, pairs))] * 2 + [dma((ns,))] * 2 + [dma((steps, 4))] * 2 + [dma((48,))],
         compiler_params=pltpu.CompilerParams(vmem_limit_bytes=63 << 20, collective_id=0, has_side_effects=True),
-    )(x, g, cs, vec, wu, wd, wqkv, wo)
-
-
-def finish_kernel(du, dd, da, y, gm, attn, ga, dwu, dwd, dwqkv, ddw, out, grad,
+    )(x, g, cs, *vecs, wu, wd, wqkv, wo)
+
+
+def finish_kernel(du, dd, da, y, gm, attn, ga, small, dwu, dwd, dwqkv, ddw, out, grad, s0, s1, s2, s3, s4, s4b, s5, s8,
                   vu, vd, va, ou, od, oq, ow, vy, vm, vo, vg, s_in, s_out):
     n, W, C = du.shape
     pairs = da.shape[0]
@@ -636,6 +670,12 @@
     fd = [fetch(dd.at[i], vd.at[i]) for i in range(n)]
     fa = [fetch(da.at[i], va.at[i]) for i in range(pairs)]
     fy = [fetch(a, b) for a, b in ((y, vy), (attn, vo), (gm, vm), (ga, vg))]
+    for i, v in ((GAIN_A, s0), (SHIFT_A, s1), (GAIN_M, s2), (SHIFT_M, s3), (BIAS, s4), (BIAS, s4b)):
+        v[...] = small[i, :]
+    for i in range(3):
+        s5[i * W:(i + 1) * W] = small[BIAS_QKV + i, :]
+    for i in range(n * C // W):
+        s8[i * W:(i + 1) * W] = small[BIAS_UP + i, :]
     for i in range(n):
         j = 2 * i if i < n // 2 else 2 * (i - n // 2) + 1
         c = slice(j * C, (j + 1) * C)
@@ -664,24 +704,26 @@
         c.wait()
 
 
-def finish_call(du, dd, da, y, gm, attn, ga):
+def finish_call(du, dd, da, y, gm, attn, ga, small):
     n, W, C = du.shape
     pairs = da.shape[0]
     FF = n * C
     tokens = y.shape[0]
+    vm = pl.BlockSpec(memory_space=pltpu.VMEM)
     hbm = pl.BlockSpec(memory_space=pl.ANY)
     S = jax.ShapeDtypeStruct
     V = pltpu.VMEM
     dma = pltpu.SemaphoreType.DMA
     return pl.pallas_call(
         finish_kernel,
-        out_shape=(S((W, FF), F32), S((FF, W), F32), S((W, 3 * W), F32), S((W, W), F32), S((tokens, W), BF), S((tokens, W), BF)),
-        in_specs=[hbm] * 7, out_specs=(hbm,) * 6,
+        out_shape=(S((W, FF), F32), S((FF, W), F32), S((W, 3 * W), F32), S((W, W), F32), S((tokens, W), BF), S((tokens, W), BF))
+        + (S((W,), F32),) * 6 + (S((3 * W,), F32), S((FF,), F32)),
+        in_specs=[hbm] * 7 + [vm], out_specs=(hbm,) * 6 + (vm,) * 8,
         scratch_shapes=[V(du.shape, BF), V(dd.shape, BF), V(da.shape, BF), V((W, FF), F32), V((FF, W), F32),
                         V((W, 3 * W), F32), V((W, W), F32), V((tokens, W), F32), V((tokens, W), F32),
                         V((tokens, W), BF), V((tokens, W), BF), dma((2 * n + pairs + 4,)), dma((2 * n + 4 * pairs + 2,))],
         compiler_params=pltpu.CompilerParams(vmem_limit_bytes=63 << 20),
-    )(du, dd, da, y, gm, attn, ga)
+    )(du, dd, da, y, gm, attn, ga, small)
 
 
 def on_device(hidden_in, positions, attn_gain, attn_shift, qkv_weight, qkv_bias, dense_weight, dense_bias,
@@ -692,16 +734,13 @@
     freqs = jnp.power(10000.0, -2.0 * jnp.arange(ROT // 2, dtype=F32) / ROT)
     angles = freqs[:, None] * positions.astype(F32)[:, None, :]
     cs = jnp.concatenate([jnp.cos(angles), jnp.sin(angles)], axis=1)
-    zero = jnp.zeros((W,), F32)
-    vec = jnp.concatenate([attn_gain, attn_shift, mlp_gain, mlp_shift, dense_bias + down_bias, qkv_bias,
-                           up_bias, zero, zero, zero, zero]).reshape(16, W)
+    vecs = (attn_gain, attn_shift, mlp_gain, mlp_shift, dense_bias, down_bias, qkv_bias, up_bias)
     y, gm, du, dd, da, attn, ga, small = layer_call(
-        sizes, hidden_in, out_grad, cs, vec, up_weight, down_weight, qkv_weight, dense_weight)
-    dwu, dwd, dwqkv, ddw, layer_out, input_grad = finish_call(du, dd, da, y, gm, attn.reshape(-1, W), ga.reshape(-1, W))
-    db = small[BIAS]
-    return (layer_out.reshape(hidden_in.shape), input_grad.reshape(hidden_in.shape), small[GAIN_A], small[SHIFT_A], dwqkv,
-            small[BIAS_QKV:BIAS_UP].reshape(-1), ddw, db, small[GAIN_M], small[SHIFT_M], dwu,
-            small[BIAS_UP:BIAS_UP + 4].reshape(-1), dwd, db)
+        sizes, hidden_in, out_grad, cs, vecs, up_weight, down_weight, qkv_weight, dense_weight)
+    dwu, dwd, dwqkv, ddw, layer_out, input_grad, s0, s1, s2, s3, s4, s4b, s5, s8 = finish_call(
+        du, dd, da, y, gm, attn, ga.reshape(-1, W), small)
+    return (layer_out.reshape(hidden_in.shape), input_grad.reshape(hidden_in.shape), s0, s1, dwqkv, s5, ddw, s4, s2, s3,
+            dwu, s8, dwd, s4b)
 
 
 def solution(mesh):

time: 252 us -> 228 us (0.905)
  Pallas kernels: 239 us -> 225 us
  local copies, waits for them, and re-layouts: 9.69 us -> 0 us
    pallas_call x1, Pallas kernels: 219 us -> 204 us  [layer_call(): pl.pallas_call(functools.partial(layer_kernel, sizes), out_shape=(S((T, W...]
    unnamed x9 -> x0, local copies, waits for them, and re-layouts: 4.79 us -> none
    slice x3 -> x0, local copies, waits for them, and re-layouts: 3.05 us -> none  [the longest x1 1.57 us: on_device(): small[SHIFT_M]]
where the time goes in v6:
time: 228 us
  Pallas kernels  225 us (99%)
    pallas_call x1, Pallas kernels, layer_call(): pl.pallas_call(functools.partial(layer_kernel, sizes), out_shape=(S((T, W...  204 us
    pallas_call x1, Pallas kernels, finish_call(): pl.pallas_call(finish_kernel, out_shape=(S((W, FF), F32), S((FF, W), F32)...  21.4 us

profile of v6, /device:TPU:0, one launch (start us, length us, event | category | flops | bytes accessed | tf_op | source)
XLA Modules:
  0.0 227.8 jit_solution(14359569280229634252)
XLA Ops:
  0.7 0.7 convert_element_type.3
  1.4 0.2 multiply_cosine_fusion
  1.6 0.6 pad_maximum_fusion.cs_ref
  2.2 203.9 %shard_map.254 = (f32[1024,768]{1,0:T(8,128)}, f32[1024,768]{1,0:T(8,128)}, bf16[12,768,256]{2,1,0:T(8,128)(2,1)}, bf16[12,256,768]{2,1,0:T(8,128)(2,1)}, bf16[6...) custom-call(bf16[4,256,768]{2,1,0:T(8,128)(2,1)} %x_in.1, ...), custom_call_target="tpu_custom_call" | custom-call | tf_op jit(solution)/shard_map/pallas_call | solution.py:638
  206.1 21.4 %shard_map.255 = (f32[768,3072]{1,0:T(8,128)}, f32[3072,768]{1,0:T(8,128)}, f32[768,2304]{1,0:T(8,128)}, f32[768,768]{1,0:T(8,128)}, bf16[1024,768]{1,0:T(8,128)...) custom-call(bf16[12,768,256]{2,1,0:T(8,128)(2,1)} %get-tuple-element, ...), custom_call_target="tpu_custom_call" | custom-call | tf_op jit(solution)/shard_map/pallas_call | solution.py:717
  (1 shorter events, 0.0 us)

commit v7 on v6

--- a/solution.py
+++ b/solution.py
@@ -168,14 +168,15 @@
         ops[k].start()
 
 
-ENDS_M = (2, 5, 7, 9, 11, 12, 13)
-ENDS_A = (2, 3, 4, 5, 7, 8, 9)
-ENDS_L = (1, 2, 3, 4, 5, 6, 7)
-UP, DOWN = ("sz", "zsr"), ("zsr", "sr")
-LEFT, RIGHT = ("szr", "s", "sz"), ("sz", "sr", "szr")
-GAPS_U, GAPS_D, GAPS_A, GAPS_L = (2, 3, 3, 3, 2), (2, 2, 2, 1, 1), (1, 2, 2, 1), (1,)
-WAIT_A = (1, 0, 0)
-GA_SENDS = (0, 6, 7)
+ENDS_M = (1, 3, 6, 9, 12, 13, 14)
+ENDS_A = (1, 3, 6, 9, 11, 12, 13)
+ENDS_L = (1, 2, 4, 5, 7, 8, 9)
+UP, DOWN = ('zs', 'szr'), ('z', 's')
+LEFT, RIGHT = ('sr', 'sz', 'sr'), ('s', 'szr', 's')
+GAPS_U, GAPS_D, GAPS_A, GAPS_L = (3, 2, 4, 2, 4), (3, 2, 4, 3, 2), (2, 2, 2, 1), (1, 1, 2, 2)
+WAIT_A = (2, 0, 0)
+GA_SENDS = (1, 4, 4)
+SMALL_TICKS = (0, 2, 4, 6)
 SPLIT_M = 3
 GAIN_A, SHIFT_A, GAIN_M, SHIFT_M, BIAS, BIAS_QKV, BIAS_UP = 0, 1, 2, 3, 4, 5, 8
 SMALL = 16
@@ -286,7 +287,7 @@
 
     assert all(len(bits) <= 2 for bits in rounds)
     for i in range(len(rounds) + 1):
-        plan.setdefault(t_s + i, []).append(functools.partial(small_round, i))
+        plan.setdefault(t_s + (SMALL_TICKS[i] if len(rounds) == 3 else i), []).append(functools.partial(small_round, i))
     end = max(max(plan), t_g + max(GA_SENDS)) + 1
     assert ns == len(GA_SENDS) + 1 and pairs == 6
 
@@ -416,7 +417,10 @@
 
             @pl.when(t == t_l)
             def _():
-                store = pltpu.make_async_copy(y, y_out, s_l.at[next(local)])
+                for b in range(ns):
+                    rows = slice(b * L, (b + 1) * L)
+                    xm[rows, :] = y[rows, :].astype(BF)
+                store = pltpu.make_async_copy(xm, y_out, s_l.at[next(local)])
                 store.start()
                 for b in range(ns):
                     rows = slice(b * L, (b + 1) * L)
@@ -426,8 +430,8 @@
                     small[GAIN_M:GAIN_M + 1, :] += jnp.sum(dxa * xhat, axis=0, keepdims=True)
                     small[SHIFT_M:SHIFT_M + 1, :] += jnp.sum(dxa, axis=0, keepdims=True)
                     small[BIAS:BIAS + 1, :] += jnp.sum(gf, axis=0, keepdims=True)
-                    dxm[rows, :] = gf + norm_back(dxa * row(2), xhat, rstd)
-                back = pltpu.make_async_copy(dxm, gm_out, s_l.at[next(local)])
+                    x_ref[b] = (gf + norm_back(dxa * row(2), xhat, rstd)).astype(BF)
+                back = pltpu.make_async_copy(x_ref, gm_out, s_l.at[next(local)])
                 back.start()
                 store.wait()
                 back.wait()
@@ -637,7 +641,7 @@
     la = Halving.land(R // 2, steps)
     return pl.pallas_call(
         functools.partial(layer_kernel, sizes),
-        out_shape=(S((T, W), F32), S((T, W), F32), S((n, W, C), BF), S((n, C, W), BF), S((pairs, R, W), BF),
+        out_shape=(S((T, W), BF), S((ns, L, W), BF), S((n, W, C), BF), S((n, C, W), BF), S((pairs, R, W), BF),
                    S((T, W), BF), S((ns, L, W), BF), S((SMALL, W), F32)),
         in_specs=[hbm, hbm, vm] + [vm] * 8 + [hbm] * 4, out_specs=(hbm,) * 7 + (vm,),
         scratch_shapes=[V((n, W, C), BF), V((n, C, W), BF), V((n, Halving.land(W, steps), C), BF),
@@ -645,7 +649,7 @@
                         V((pairs, la, W), BF), V((T, W), BF), V((T, W), BF), V(cs.shape, F32), V((ns, L, W), BF), V((SMALL, W), F32), V((SMALL, W), F32), V((steps, 4, SMALL, W), F32)]
         + [dma((n, steps))] * 4 + [dma((pairs, steps))] * 4 + [dma((2 * SPLIT_M, steps))] * 4 + [dma((3, steps))] * 4
         + [dma((2, ns, MOVES))] * 2 + [dma((ns,))] * 2 + [dma((ns, pairs))] * 2 + [dma((ns,))] * 2 + [dma((steps, 4))] * 2 + [dma((48,))],
-        compiler_params=pltpu.CompilerParams(vmem_limit_bytes=63 << 20, collective_id=0, has_side_effects=True),
+        compiler_params=pltpu.CompilerParams(vmem_limit_bytes=255 << 18, collective_id=0, has_side_effects=True),
     )(x, g, cs, *vecs, wu, wd, wqkv, wo)
 
 
@@ -666,8 +670,8 @@
         outs.append(c)
         c.start()
 
+    fd = [fetch(dd.at[i], vd.at[i]) for i in range(n)]
     fu = [fetch(du.at[i], vu.at[i]) for i in range(n)]
-    fd = [fetch(dd.at[i], vd.at[i]) for i in range(n)]
     fa = [fetch(da.at[i], va.at[i]) for i in range(pairs)]
     fy = [fetch(a, b) for a, b in ((y, vy), (attn, vo), (gm, vm), (ga, vg))]
     for i, v in ((GAIN_A, s0), (SHIFT_A, s1), (GAIN_M, s2), (SHIFT_M, s3), (BIAS, s4), (BIAS, s4b)):
@@ -676,29 +680,37 @@
         s5[i * W:(i + 1) * W] = small[BIAS_QKV + i, :]
     for i in range(n * C // W):
         s8[i * W:(i + 1) * W] = small[BIAS_UP + i, :]
+
+    def chunk(i):
+        j = 2 * i if i < n // 2 else 2 * (i - n // 2) + 1
+        return slice(j * C, (j + 1) * C)
+
     for i in range(n):
-        j = 2 * i if i < n // 2 else 2 * (i - n // 2) + 1
-        c = slice(j * C, (j + 1) * C)
-        fu[i].wait()
-        ou[:, c] = vu[i].astype(F32)
-        store(ou.at[:, c], dwu.at[:, c])
+        c = chunk(i)
         fd[i].wait()
         od[c, :] = vd[i].astype(F32)
         store(od.at[c, :], dwd.at[c, :])
+    for i in range(n):
+        fu[i].wait()
+        ou[:, chunk(i)] = vu[i].astype(F32)
+    for i in range(8):
+        rows = slice(i * W // 8, (i + 1) * W // 8)
+        store(ou.at[rows], dwu.at[rows])
     for i in range(pairs):
         fa[i].wait()
-        for k in range(3):
-            c = slice(k * W + i * 128, k * W + (i + 1) * 128)
-            oq[:, c] = va[i, k * 128:(k + 1) * 128, :].astype(F32).T
-            store(oq.at[:, c], dwqkv.at[:, c])
         c = slice(i * 128, (i + 1) * 128)
         ow[c, :] = va[i, 384:, :].astype(F32)
         store(ow.at[c, :], ddw.at[c, :])
+        for k in range(3):
+            oq[:, k * W + i * 128:k * W + (i + 1) * 128] = va[i, k * 128:(k + 1) * 128, :].astype(F32).T
+    for i in range(8):
+        rows = slice(i * W // 8, (i + 1) * W // 8)
+        store(oq.at[rows], dwqkv.at[rows])
     for f in fy:
         f.wait()
-    vo[...] = (vy[...] + vo[...].astype(F32)).astype(BF)
+    vo[...] = (vy[...].astype(F32) + vo[...].astype(F32)).astype(BF)
     store(vo, out)
-    vg[...] = (vm[...] + vg[...].astype(F32)).astype(BF)
+    vg[...] = (vm[...].astype(F32) + vg[...].astype(F32)).astype(BF)
     store(vg, grad)
     for c in outs:
         c.wait()
@@ -720,7 +732,7 @@
         + (S((W,), F32),) * 6 + (S((3 * W,), F32), S((FF,), F32)),
         in_specs=[hbm] * 7 + [vm], out_specs=(hbm,) * 6 + (vm,) * 8,
         scratch_shapes=[V(du.shape, BF), V(dd.shape, BF), V(da.shape, BF), V((W, FF), F32), V((FF, W), F32),
-                        V((W, 3 * W), F32), V((W, W), F32), V((tokens, W), F32), V((tokens, W), F32),
+                        V((W, 3 * W), F32), V((W, W), F32), V((tokens, W), BF), V((tokens, W), BF),
                         V((tokens, W), BF), V((tokens, W), BF), dma((2 * n + pairs + 4,)), dma((2 * n + 4 * pairs + 2,))],
         compiler_params=pltpu.CompilerParams(vmem_limit_bytes=63 << 20),
     )(du, dd, da, y, gm, attn, ga, small)
@@ -738,7 +750,7 @@
     y, gm, du, dd, da, attn, ga, small = layer_call(
         sizes, hidden_in, out_grad, cs, vecs, up_weight, down_weight, qkv_weight, dense_weight)
     dwu, dwd, dwqkv, ddw, layer_out, input_grad, s0, s1, s2, s3, s4, s4b, s5, s8 = finish_call(
-        du, dd, da, y, gm, attn, ga.reshape(-1, W), small)
+        du, dd, da, y, gm.reshape(-1, W), attn, ga.reshape(-1, W), small)
     return (layer_out.reshape(hidden_in.shape), input_grad.reshape(hidden_in.shape), s0, s1, dwqkv, s5, ddw, s4, s2, s3,
             dwu, s8, dwd, s4b)
 

time: 228 us -> 222 us (0.974)
  Pallas kernels: 225 us -> 220 us
    pallas_call x1, Pallas kernels: 204 us -> 200 us  [layer_call(): pl.pallas_call(functools.partial(layer_kernel, sizes), out_shape=(S((T, W...]
where the time goes in v7:
time: 222 us
  Pallas kernels  220 us (99%)
    pallas_call x1, Pallas kernels, layer_call(): pl.pallas_call(functools.partial(layer_kernel, sizes), out_shape=(S((T, W...  200 us
    pallas_call x1, Pallas kernels, finish_call(): pl.pallas_call(finish_kernel, out_shape=(S((W, FF), F32), S((FF, W), F32)...  19.5 us

profile of v7, /device:TPU:0, one launch (start us, length us, event | category | flops | bytes accessed | tf_op | source)
XLA Modules:
  0.0 222.2 jit_solution(14447347417484972309)
XLA Ops:
  0.7 0.7 convert_element_type.3
  1.4 0.2 multiply_cosine_fusion
  1.6 0.6 pad_maximum_fusion.cs_ref
  2.2 200.3 %shard_map.254 = (bf16[1024,768]{1,0:T(8,128)(2,1)}, bf16[4,256,768]{2,1,0:T(8,128)(2,1)}, bf16[12,768,256]{2,1,0:T(8,128)(2,1)}, bf16[12,256,768]{2,1,0:T(8,128...) custom-call(bf16[4,256,768]{2,1,0:T(8,128)(2,1)} %x_in.1, ...), custom_call_target="tpu_custom_call" | custom-call | tf_op jit(solution)/shard_map/pallas_call | solution.py:642
  202.5 19.5 %shard_map.255 = (f32[768,3072]{1,0:T(8,128)}, f32[3072,768]{1,0:T(8,128)}, f32[768,2304]{1,0:T(8,128)}, f32[768,768]{1,0:T(8,128)}, bf16[1024,768]{1,0:T(8,128)...) custom-call(bf16[12,768,256]{2,1,0:T(8,128)(2,1)} %get-tuple-element, ...), custom_call_target="tpu_custom_call" | custom-call | tf_op jit(solution)/shard_map/pallas_call | solution.py:729
  (1 shorter events, 0.0 us)

commit v8 on v7

--- a/solution.py
+++ b/solution.py
@@ -370,6 +370,8 @@
         for m in loads[1:4]:
             m.wait()
 
+        stores = [pltpu.make_async_copy(src, dst, s_l.at[next(local)]) for src, dst in ((xm, y_out), (x_ref, gm_out))]
+
         @pl.loop(0, t_l + 1)
         def _(t):
             c = pl.ds(pl.multiple_of(jnp.minimum(t, n_chunk - 1) * C, C), C)
@@ -420,8 +422,7 @@
                 for b in range(ns):
                     rows = slice(b * L, (b + 1) * L)
                     xm[rows, :] = y[rows, :].astype(BF)
-                store = pltpu.make_async_copy(xm, y_out, s_l.at[next(local)])
-                store.start()
+                stores[0].start()
                 for b in range(ns):
                     rows = slice(b * L, (b + 1) * L)
                     xhat, rstd = norm_parts(x_ref[b].astype(F32))
@@ -431,16 +432,13 @@
                     small[SHIFT_M:SHIFT_M + 1, :] += jnp.sum(dxa, axis=0, keepdims=True)
                     small[BIAS:BIAS + 1, :] += jnp.sum(gf, axis=0, keepdims=True)
                     x_ref[b] = (gf + norm_back(dxa * row(2), xhat, rstd)).astype(BF)
-                back = pltpu.make_async_copy(x_ref, gm_out, s_l.at[next(local)])
-                back.start()
-                store.wait()
-                back.wait()
+                stores[1].start()
 
         @pl.loop(0, MOVES)
         def _(i):
             for m in moves(i):
                 m.wait()
-        for m in once:
+        for m in once + stores:
             m.wait()
 
     def attention(wqkv, wo, wT, xaT, qkvT, kn, vn, dOT, obT, obn):
@@ -541,9 +539,9 @@
                     delta = jnp.sum(dO * oT, axis=0, keepdims=True)
                     obT[hr, qs] = oT.astype(BF)
                     dp = nn(vn[0:n, cols], dO2)
-                    ds = (e * ((dp - delta) * inv)).astype(BF)
-                    dq[i] = nn(qkvT[kr, 0:n], ds) * (HEAD ** -0.5)
-                    dkT = nt(qkvT[hr, qs], ds)
+                    ds = (e * (dp - delta)).astype(BF)
+                    dq[i] = nn(qkvT[kr, 0:n], ds) * (inv * HEAD ** -0.5)
+                    dkT = nt((qkvT[hr, qs].astype(F32) * inv).astype(BF), ds)
                     dvT = nt((dO * inv).astype(BF), p)
                     for b in range(i + 1):
                         sl = slice(b * L, (b + 1) * L)

time: 222 us -> 222 us (level)
  no operation moved by 1% of the time
where the time goes in v8:
time: 222 us
  Pallas kernels  219 us (99%)
    pallas_call x1, Pallas kernels, layer_call(): pl.pallas_call(functools.partial(layer_kernel, sizes), out_shape=(S((T, W...  200 us
    pallas_call x1, Pallas kernels, finish_call(): pl.pallas_call(finish_kernel, out_shape=(S((W, FF), F32), S((FF, W), F32)...  19.5 us

profile of v8, /device:TPU:0, one launch (start us, length us, event | category | flops | bytes accessed | tf_op | source)
XLA Modules:
  0.0 221.9 jit_solution(16004216451848713054)
XLA Ops:
  0.7 0.7 convert_element_type.3
  1.4 0.2 multiply_cosine_fusion
  1.6 0.6 pad_maximum_fusion.cs_ref
  2.2 199.9 %shard_map.254 = (bf16[1024,768]{1,0:T(8,128)(2,1)}, bf16[4,256,768]{2,1,0:T(8,128)(2,1)}, bf16[12,768,256]{2,1,0:T(8,128)(2,1)}, bf16[12,256,768]{2,1,0:T(8,128...) custom-call(bf16[4,256,768]{2,1,0:T(8,128)(2,1)} %x_in.1, ...), custom_call_target="tpu_custom_call" | custom-call | tf_op jit(solution)/shard_map/pallas_call | solution.py:640
  202.1 19.5 %shard_map.255 = (f32[768,3072]{1,0:T(8,128)}, f32[3072,768]{1,0:T(8,128)}, f32[768,2304]{1,0:T(8,128)}, f32[768,768]{1,0:T(8,128)}, bf16[1024,768]{1,0:T(8,128)...) custom-call(bf16[12,768,256]{2,1,0:T(8,128)(2,1)} %get-tuple-element, ...), custom_call_target="tpu_custom_call" | custom-call | tf_op jit(solution)/shard_map/pallas_call | solution.py:727
  (1 shorter events, 0.0 us)
